TPU v7x, 32 devices: a whole 2x2x4 slice. The times are simulated.
32 devices in a mesh: groups: 2 (over y), seq: 4 (over z), head: 2 (over x), sub: 2 (over core).
Axes of the slice: x: 2, y: 2, z: 4, core: 2. Of those that a mesh axis runs over, the one named last changes fastest.
Arguments:
- wave_pieces: float32 [8, 2, 2, 64, 3072], P(('groups', 'seq'), 'head', 'sub'), parts along dimension 0, may hold values from -6 to 6
- piece_target: int32 [8, 2, 2, 64], P(('groups', 'seq'), 'head', 'sub'), parts along dimension 0, may hold values from -1 to 127, as said below
- utt_lengths: int32 [8], P('groups'), parts along dimension 0, may hold values from 1 to 1088, 2176 in all
- sub_weight: bfloat16 [512, 1536], P(None, 'head'), may hold values from -2 to 2
- sub_bias: bfloat16 [1536], P('head'), may hold values from -4 to 4
- norm_gain: float32 [1536], replicated, may hold values from 0.1 to 1.9
- qkv_weight: bfloat16 [1536, 3, 1536], P(None, None, 'head'), may hold values from -0.21875 to 0.21875
- rel_bias: float32 [24, 543], P('head'), may hold values from -4 to 250
Outputs:
- context: bfloat16 [4352, 1536], P(('groups', 'seq', 'sub'), 'head'), parts along dimension 0
There are 2 independent parts, one for each index of `groups`. A program takes and returns all parts, laid end to end along the dimension named above; an argument that names none is the same for every part. Nothing has to cross between parts.
Inputs may be any that keep to these rules, and one draw needn't show every extreme that they name: `piece_target`: each value is -1 (an empty slot) or s * 32 + p, naming piece p of seq index s for the loader's own head and sub indices. Every piece of every eighth is named by exactly one slot of a loader with the same head and sub indices. A loader names at most 16 pieces of one seq index; in every draw some loaders name exactly 16 pieces of every seq index, so that all their slots are full.
All inputs are finite; a program needn't handle non-finite values.
Results may differ from a plain program's by a relative error of at most 0.006.
Values may be sent and summed in bfloat16 or wider, within the bound.
No kernel may reach another device: no remote copies, remote signals or barrier semaphores. Data moves between devices by JAX's collectives and lax.ppermute only.
A program may use at most 64 MiB of HBM per device.

v0:
```python
import functools
import math

import jax
import jax.numpy as jnp
import ml_dtypes
import numpy as np
from jax import lax
from jax.experimental import pallas as pl
from jax.experimental.pallas import tpu as pltpu
from jax.sharding import PartitionSpec as P

HDIM = 64
MEL = 128
NFFT = 512
HOP = 160
FP = 17
CH = 136
PE = 32

SAMPLE_RATE = 16000.0
EPSILON = 1e-05
MASKED = -1e30

LANES = 128
PIECE_BITS = 5
ROWS = 144
GROUP = 4
STACK = 4
MEL_WIDTH = FP * MEL
BF16 = jnp.bfloat16
F32 = jnp.float32


def split_bf16(values):
    high = values.astype(ml_dtypes.bfloat16)
    low = (values - high.astype(np.float64)).astype(ml_dtypes.bfloat16)
    return np.stack([high, low])


def fourier_tables():
    n = np.arange(NFFT)
    bins = NFFT // 2
    window = 0.5 - 0.5 * np.cos(2.0 * np.pi * n / NFFT)
    phase = 2.0 * np.pi * ((n[:, None] * np.arange(bins + 1)[None, :]) % NFFT) / NFFT
    sine = np.sin(phase[:, :bins])
    sine[:, 0] = np.cos(phase[:, bins])
    return split_bf16(np.concatenate([np.cos(phase[:, :bins]), sine], axis=1) * window[:, None])


def mel_tables():
    bins = NFFT // 2
    highest = 2595.0 * math.log10(1.0 + SAMPLE_RATE / 2.0 / 700.0)
    points = np.arange(MEL + 2) * (highest / (MEL + 1))
    hertz = 700.0 * (10.0 ** (points / 2595.0) - 1.0)
    centres = np.arange(bins + 1) * (SAMPLE_RATE / NFFT)
    rising = (centres[:, None] - hertz[None, :-2]) / (hertz[1:-1] - hertz[:-2])[None, :]
    falling = (hertz[None, 2:] - centres[:, None]) / (hertz[2:] - hertz[1:-1])[None, :]
    filters = np.maximum(0.0, np.minimum(rising, falling))
    second = filters[:bins].copy()
    second[0] = filters[bins]
    return split_bf16(np.concatenate([filters[:bins], second], axis=0))


def dot(a, b):
    return jnp.dot(a, b, preferred_element_type=F32)


def iota(shape, dim):
    return lax.broadcasted_iota(jnp.int32, shape, dim)


def mel_kernel(shards, capacity, relative, x_ref, target_ref, fourier_ref, mel_ref, *outs):
    slots = x_ref.shape[0]
    x = x_ref[...]
    frames = [None] * FP
    for phase in range(4):
        shift = phase * (HOP % LANES)
        moved = x if phase == 0 else pltpu.roll(x, x.shape[1] - shift, 1)
        high = moved.astype(BF16)
        low = (moved - high.astype(F32)).astype(BF16)
        members = list(range(phase, FP, 4))
        starts = [HOP * f - shift for f in members]
        high = jnp.concatenate([high[:, s : s + NFFT] for s in starts], axis=0)
        low = jnp.concatenate([low[:, s : s + NFFT] for s in starts], axis=0)
        spectra = dot(high, fourier_ref[0]) + dot(low, fourier_ref[0]) + dot(high, fourier_ref[1])
        power = spectra * spectra
        power_high = power.astype(BF16)
        power_low = (power - power_high.astype(F32)).astype(BF16)
        energy = (
            dot(power_high, mel_ref[0]) + dot(power_low, mel_ref[0]) + dot(power_high, mel_ref[1])
        )
        log_mel = jnp.log(1.0 + energy).astype(BF16)
        for k, f in enumerate(members):
            frames[f] = log_mel[k * slots : (k + 1) * slots]
    target = target_ref[...]
    owner = lax.shift_right_arithmetic(target, PIECE_BITS)
    place = jnp.where(target < 0, 0, (target & (PE - 1)) + 1).astype(F32)
    row, col = iota((slots, slots), 0), iota((slots, slots), 1)
    diagonal = row == col
    owner_col = jnp.sum(jnp.where(diagonal, owner, 0), axis=1, keepdims=True)
    place_col = jnp.sum(jnp.where(diagonal, place, 0.0), axis=1, keepdims=True)
    rank = jnp.sum(((owner_col == owner) & (row < col)).astype(jnp.int32), axis=0, keepdims=True)
    chosen = row // capacity
    if relative:
        chosen = chosen ^ lax.axis_index("seq")
    pick = ((chosen == owner) & (row % capacity == rank)).astype(F32).astype(BF16)
    marks = jnp.broadcast_to(place_col, (slots, LANES)).astype(BF16)
    packed = dot(pick, jnp.concatenate(frames + [marks], axis=1)).astype(BF16)
    count = slots // len(outs)
    for d, out in enumerate(outs):
        out[...] = packed[d * count : (d + 1) * count]


def place_kernel(*refs):
    parts, out = refs[:-1], refs[-1]
    rows = jnp.concatenate([part[...] for part in parts], axis=0)
    slots = rows.shape[0]
    mark = rows[:, MEL_WIDTH : MEL_WIDTH + LANES].astype(F32)[:, :1]
    row, col = iota((slots, slots), 0), iota((slots, slots), 1)
    mark = jnp.sum(jnp.where(row == col, mark, 0.0), axis=0, keepdims=True)
    at = iota((PE, slots), 0)
    groups = PE // GROUP
    wanted = (at % groups) * GROUP + at // groups + 1
    pick = (wanted.astype(F32) == mark).astype(F32).astype(BF16)
    out[...] = dot(pick, rows[:, :MEL_WIDTH]).astype(BF16)


def token_rows(pieces):
    groups = PE // GROUP
    pieces = pieces.astype(F32)
    rows = []
    for i in range(FP):
        cells = []
        for j in range(STACK):
            q, f = divmod(STACK * i + j, FP)
            cells.append(pieces[q * groups : (q + 1) * groups, f * MEL : (f + 1) * MEL])
        rows.append(jnp.concatenate(cells, axis=1))
    rows.append(jnp.zeros((ROWS - CH, STACK * MEL), F32))
    mixed = jnp.concatenate(rows, axis=0).astype(BF16)
    row, col = iota((ROWS, ROWS), 0), iota((ROWS, ROWS), 1)
    token = (col % groups) * FP + col // groups
    order = ((row == token) & (col < CH)).astype(F32).astype(BF16)
    return dot(order, mixed).astype(BF16)


def bias_kernel(lengths_ref, table_ref, out_ref):
    pairs, blocks = out_ref.shape[:2]
    half = blocks * CH
    first = (lax.axis_index("seq") * lax.axis_size("sub") + lax.axis_index("sub")) * half
    total = lax.axis_size("seq") * lax.axis_size("sub") * half
    lane, row = iota((1, 3 * ROWS), 1), iota((ROWS, 1), 0)
    key_block = lane // ROWS
    key_place = lane - key_block * ROWS
    masks = []
    for c in range(blocks):
        query = first + c * CH + row
        key = first + (c - 1) * CH + key_block * CH + key_place
        query_utt, key_utt = jnp.zeros_like(query), jnp.zeros_like(key)
        end = jnp.int32(0)
        for r in range(lengths_ref.shape[0]):
            end = end + lengths_ref[r]
            query_utt = query_utt + (query >= end).astype(jnp.int32)
            key_utt = key_utt + (key >= end).astype(jnp.int32)
        inside = (key >= 0) & (key < total) & (key_place < CH)
        key_utt = jnp.where(inside, key_utt, -1)
        masks.append(jnp.where(query_utt == key_utt, 0.0, MASKED))
    width = table_ref.shape[1]

    def one_head(head, side):
        line = jnp.broadcast_to(table_ref[pl.ds(head, 1), :], (ROWS, width))
        turned = [
            pltpu.roll(line, (8 * b - (CH - 1)) % width, 1, stride=1, stride_axis=0)[:, : 3 * ROWS]
            for b in range(3)
        ]
        bias = jnp.where(
            key_block == 0, turned[0], jnp.where(key_block == 1, turned[1], turned[2])
        )
        for c in range(blocks):
            out_ref[head // 2, c, side * ROWS : (side + 1) * ROWS, :] = bias + masks[c]

    @pl.loop(0, pairs)
    def _(pair):
        one_head(2 * pair, 0)
        one_head(2 * pair + 1, 1)


def attend_kernel(heads_split, *refs):
    n = heads_split
    pieces, refs = refs[: n + 2], refs[n + 2 :]
    conv, refs = refs[: 1 + 2 * (n - 1)], refs[1 + 2 * (n - 1) :]
    conv_bias, gain, qkv_hbm, bias_hbm, out = refs[:5]
    tokens, normed, queries, keys, values, qkv, bias, sems = refs[5:]
    me = lax.axis_index("head")
    depth = qkv.shape[1] // n
    copies = []
    for p in range(3):
        for d in range(n):
            source = pl.multiple_of(lax.rem(me + d, n) * depth, depth)
            copy = pltpu.make_async_copy(
                qkv_hbm.at[p, pl.ds(source, depth), :],
                qkv.at[p, pl.ds(d * depth, depth), :],
                sems.at[p * n + d],
            )
            copy.start()
            copies.append(copy)
    bias_copy = pltpu.make_async_copy(bias_hbm, bias, sems.at[3 * n])
    bias_copy.start()

    blocks = n + 2
    tokens[0] = token_rows(pieces[n][...])
    tokens[n + 1] = token_rows(pieces[n + 1][...])
    for d in range(n):
        tokens[1 + lax.rem(me + d, n)] = token_rows(pieces[d][...])
    every = tokens[...].reshape(blocks * ROWS, STACK * MEL)
    features = []
    for d in range(n):
        if d == 0:
            summed = dot(every, conv[0][...])
        else:
            rows = conv[2 * d - 1].shape[0]
            summed = dot(every[:, :rows], conv[2 * d - 1][...])
            summed = summed + dot(every[:, rows:], conv[2 * d][...])
        summed = summed + conv_bias[d].astype(F32)
        features.append((summed / (1.0 + jnp.exp(-summed))).astype(BF16).astype(F32))
    width = depth * n
    mean = sum(jnp.sum(f, axis=1, keepdims=True) for f in features) * (1.0 / width)
    centred = [f - mean for f in features]
    variance = sum(jnp.sum(c * c, axis=1, keepdims=True) for c in centred) * (1.0 / width)
    scale = lax.rsqrt(variance + EPSILON)
    for d in range(n):
        normed[:, d * depth : (d + 1) * depth] = (
            centred[d] * scale * gain[lax.rem(me + d, n)]
        ).astype(BF16)

    for copy in copies:
        copy.wait()
    local = qkv.shape[2]
    queries[...] = dot(normed[ROWS : (n + 1) * ROWS, :], qkv[0]).astype(BF16).reshape(
        n, ROWS, local
    )
    keys[...] = dot(normed[...], qkv[1]).astype(BF16).reshape(blocks, ROWS, local)
    values[...] = dot(normed[...], qkv[2]).astype(BF16).reshape(blocks, ROWS, local)
    bias_copy.wait()
    lane = iota((ROWS, LANES), 1)
    low_lanes = lane < HDIM

    @pl.loop(0, local // LANES)
    def _(pair):
        at = pl.ds(pl.multiple_of(pair * LANES, LANES), LANES)
        results = []
        for c in range(n):
            q = queries[c, :, at] * jnp.asarray(1.0 / math.sqrt(HDIM), BF16)
            zero = jnp.zeros_like(q)
            q = jnp.concatenate(
                [jnp.where(low_lanes, q, zero), jnp.where(low_lanes, zero, q)], axis=0
            )
            k = keys[c : c + 3, :, at].reshape(3 * ROWS, LANES)
            v = values[c : c + 3, :, at].reshape(3 * ROWS, LANES)
            scores = lax.dot_general(q, k, (((1,), (1,)), ((), ())), preferred_element_type=F32)
            scores = scores + bias[pair, c]
            weights = jnp.exp(scores - jnp.max(scores, axis=1, keepdims=True))
            weights = weights / jnp.sum(weights, axis=1, keepdims=True)
            context = dot(weights.astype(BF16), v)
            results.append(jnp.where(low_lanes, context[:ROWS], context[ROWS:])[:CH])
        out[:, at] = jnp.concatenate(results, axis=0).astype(BF16)


def vmem(count):
    return [pl.BlockSpec(memory_space=pltpu.VMEM)] * count


def exchange_weights(weight):
    n, cores = lax.axis_size("head"), lax.axis_size("sub")
    assert cores == 2
    rows = weight.shape[0] // cores
    core = lax.axis_index("sub")
    mine = lax.dynamic_slice_in_dim(weight, core * rows, rows, 0)
    pieces = []
    for d in range(1, n):
        got = lax.ppermute(mine, "head", [((i + d) % n, i) for i in range(n)])
        swapped = lax.ppermute(got, "sub", [(0, 1), (1, 0)])
        pieces.append(jnp.where(core == 0, got, swapped))
        pieces.append(jnp.where(core == 0, swapped, got))
    return pieces


def local(
    wave_pieces, piece_target, utt_lengths, sub_weight, sub_bias, norm_gain, qkv_weight, rel_bias
):
    shards, n, cores = lax.axis_size("seq"), lax.axis_size("head"), lax.axis_size("sub")
    slots, length = wave_pieces.shape[3:]
    capacity = slots // shards
    relative = shards in (2, 4) and capacity % 16 == 0
    outs = shards if relative else 1
    payload = MEL_WIDTH + LANES
    packed = pl.pallas_call(
        functools.partial(mel_kernel, shards, capacity, relative),
        out_shape=[jax.ShapeDtypeStruct((slots // outs, payload), BF16)] * outs,
        in_specs=vmem(4),
        out_specs=vmem(outs),
        compiler_params=pltpu.CompilerParams(vmem_limit_bytes=40 << 20),
        name="log_mel",
    )(
        wave_pieces.reshape(slots, length),
        piece_target.reshape(1, slots),
        jnp.asarray(fourier_tables()),
        jnp.asarray(mel_tables()),
    )
    if relative:
        received = [packed[0]] + [
            lax.ppermute(packed[d], "seq", [(i, i ^ d) for i in range(shards)])
            for d in range(1, shards)
        ]
    else:
        blocks = packed[0].reshape(shards, capacity, payload)
        blocks = lax.all_to_all(blocks, "seq", split_axis=0, concat_axis=0, tiled=True)
        received = [blocks.reshape(slots, payload)]
    own = pl.pallas_call(
        place_kernel,
        out_shape=jax.ShapeDtypeStruct((PE, MEL_WIDTH), BF16),
        in_specs=vmem(len(received)),
        out_specs=vmem(1)[0],
        name="place",
    )(*received)

    halves = shards * cores
    axes = ("seq", "head", "sub")

    def device(half, head):
        return ((half // cores) * n + head) * cores + half % cores

    others = [
        lax.ppermute(own, "head", [((i + d) % n, i) for i in range(n)]) for d in range(1, n)
    ]
    around = []
    for d in range(n):
        pairs = []
        for half in range(halves - 1):
            pairs.append((device(half, n - 1), device(half + 1, d)))
            pairs.append((device(half + 1, 0), device(half, (d + 1) % n)))
        around.append(lax.ppermute(own, axes, pairs))
    me = lax.axis_index("head")
    previous, following = around[0], around[n - 1]
    for d in range(1, n):
        previous = jnp.where(me == d, around[d], previous)
        following = jnp.where(me == d, around[d - 1], following)

    local_width = qkv_weight.shape[2]
    pairs = local_width // LANES
    table = jnp.pad(rel_bias[:, ::-1], ((0, 0), (0, -rel_bias.shape[1] % LANES)))
    bias = pl.pallas_call(
        bias_kernel,
        out_shape=jax.ShapeDtypeStruct((pairs, n, 2 * ROWS, 3 * ROWS), F32),
        in_specs=[pl.BlockSpec(memory_space=pltpu.SMEM), pl.BlockSpec(memory_space=pltpu.VMEM)],
        out_specs=vmem(1)[0],
        compiler_params=pltpu.CompilerParams(vmem_limit_bytes=40 << 20),
        name="bias",
    )(utt_lengths, table)
    conv = [sub_weight] + exchange_weights(sub_weight)
    conv_bias = jnp.stack(
        [sub_bias]
        + [
            lax.ppermute(sub_bias, "head", [((i + d) % n, i) for i in range(n)])
            for d in range(1, n)
        ]
    )
    conv_bias = conv_bias.reshape(n, 1, sub_bias.shape[0])
    width = qkv_weight.shape[0]
    blocks = n + 2
    return pl.pallas_call(
        functools.partial(attend_kernel, n),
        out_shape=jax.ShapeDtypeStruct((n * CH, local_width), BF16),
        in_specs=vmem(blocks + len(conv) + 2) + [pl.BlockSpec(memory_space=pl.ANY)] * 2,
        out_specs=vmem(1)[0],
        scratch_shapes=[
            pltpu.VMEM((blocks, ROWS, STACK * MEL), BF16),
            pltpu.VMEM((blocks * ROWS, width), BF16),
            pltpu.VMEM((n, ROWS, local_width), BF16),
            pltpu.VMEM((blocks, ROWS, local_width), BF16),
            pltpu.VMEM((blocks, ROWS, local_width), BF16),
            pltpu.VMEM((3, width, local_width), BF16),
            pltpu.VMEM(bias.shape, F32),
            pltpu.SemaphoreType.DMA((3 * n + 1,)),
        ],
        compiler_params=pltpu.CompilerParams(vmem_limit_bytes=48 << 20),
        name="attend",
    )(
        own,
        *others,
        previous,
        following,
        *conv,
        conv_bias,
        norm_gain.reshape(n, 1, width // n),
        jnp.transpose(qkv_weight, (1, 0, 2)),
        bias,
    )


def solution(mesh):
    placed = (
        P(("groups", "seq"), "head", "sub", None, None),
        P(("groups", "seq"), "head", "sub", None),
        P("groups"),
        P(None, "head"),
        P("head"),
        P(),
        P(None, None, "head"),
        P("head", None),
    )
    return jax.shard_map(
        local,
        mesh=mesh,
        in_specs=placed,
        out_specs=P(("groups", "seq", "sub"), "head"),
        check_vma=False,
    )
```

profile of v0, /device:TPU:0, one launch (start us, length us, event | category | flops | bytes accessed | tf_op | source)
XLA Modules:
  0.0 61.0 jit_solution(4874937626547254340)
XLA Ops:
  0.0 1.1 %constant_dynamic-slice_fusion = bf16[256,768]{1,0:T(8,128)(2,1)S(1)} fusion(bf16[512,768]{1,0:T(8,128)(2,1)} %refs_4_.1, s32[]{:T(128)S(6)} %select_n.31), kind=kLoop, calls=%fused_computation.5 | loop fusion | bytes 786436 | tf_op jit(solution)/shard_map/dynamic_slice | solution.py:278
  1.1 3.0 %collective-permute-start.6 = (bf16[256,768]{1,0:T(8,128)(2,1)S(1)}, bf16[256,768]{1,0:T(8,128)(2,1)S(1)}, u32[]{:S(2)}, u32[]{:S(2)}) collective-permute-start(bf16[256,768]{1,0:T(8,128)(2,1)S(1)} %constant_dynamic-slice_fusion), channel_id=1, source_target_pairs={{2,0},{0,2},{3,1},{1,3},{6,4},{4,6},{7,5},{5,7},{10,8},{8,10},{11,... | collective-permute-start | bytes 1179656 | tf_op jit(solution)/shard_map/ppermute | solution.py:281
  4.1 1.2 %copy-done.2 = bf16[2,512,512]{2,1,0:T(8,128)(2,1)S(1)} copy-done((bf16[2,512,512]{2,1,0:T(8,128)(2,1)S(1)}, bf16[2,512,512]{2,1,0:T(8,128)(2,1)}, u32[]{:S(2)}) %copy-start.2) | copy-done | bytes 1048600
  5.3 1.1 %copy-done.3 = f32[1,1,1,64,3072]{4,3,2,1,0:T(8,128)S(1)} copy-done((f32[1,1,1,64,3072]{4,3,2,1,0:T(8,128)S(1)}, f32[1,1,1,64,3072]{4,3,2,1,0:T(8,128)}, u32[]{:S(2)}) %copy-start.3) | copy-done | bytes 786456
  6.5 0.9 %copy-done.5 = bf16[2,512,128]{2,1,0:T(8,128)(2,1)S(1)} copy-done((bf16[2,512,128]{2,1,0:T(8,128)(2,1)S(1)}, bf16[2,512,128]{2,1,0:T(8,128)(2,1)}, u32[]{:S(2)}) %copy-start.5) | copy-done | bytes 262168
  7.4 0.7 %copy-done.7 = s32[1,1,1,64]{3,2,1,0:T(1,128)S(1)} copy-done((s32[1,1,1,64]{3,2,1,0:T(1,128)S(1)}, s32[1,1,1,64]{3,2,1,0:T(1,128)}, u32[]{:S(2)}) %copy-start.7) | copy-done | bytes 280
  8.1 3.2 %log_mel.1 = (bf16[16,2304]{1,0:T(8,128)(2,1)S(1)}, bf16[16,2304]{1,0:T(8,128)(2,1)S(1)}, bf16[16,2304]{1,0:T(8,128)(2,1)S(1)}, bf16[16,2304]{1,0:T(8,128)(2,1)S(1)}) custom-call(f32[64,3072]{1,0:T(8,128)S(1)} %bitcast.6, s32[1,64]{1,0:T(1,128)S(1)} %bitcast.7, bf16[2,512,512]{2,1,0:T(8,128)(2,1)S(1)} %copy-done.2, bf16[2,512,128]{2,1,0:T(8,128)(2,1)S(1)} %copy-done.5), custom_call_target="tpu_custom_call" | custom-call | tf_op jit(solution)/shard_map/log_mel/pallas_call | solution.py:297
  11.3 0.6 %copy-done.6 = bf16[16,2304]{1,0:T(8,128)(2,1)} copy-done((bf16[16,2304]{1,0:T(8,128)(2,1)}, bf16[16,2304]{1,0:T(8,128)(2,1)S(1)}, u32[]{:S(2)}) %copy-start.6) | copy-done | bytes 73752
  11.9 1.6 %collective-permute-start = (bf16[16,2304]{1,0:T(8,128)(2,1)S(1)}, bf16[16,2304]{1,0:T(8,128)(2,1)S(1)}, u32[]{:S(2)}, u32[]{:S(2)}) collective-permute-start(bf16[16,2304]{1,0:T(8,128)(2,1)S(1)} %get-tuple-element.10), channel_id=1, source_target_pairs={{0,4},{4,0},{8,12},{12,8},{1,5},{5,1},{9,13},{13,9},{2,6},{6,2},{1... | collective-permute-start | bytes 221192 | tf_op jit(solution)/shard_map/ppermute | solution.py:312
  13.5 2.6 %collective-permute-start.1 = (bf16[16,2304]{1,0:T(8,128)(2,1)S(1)}, bf16[16,2304]{1,0:T(8,128)(2,1)S(1)}, u32[]{:S(2)}, u32[]{:S(2)}) collective-permute-start(bf16[16,2304]{1,0:T(8,128)(2,1)S(1)} %get-tuple-element.11), channel_id=1, source_target_pairs={{0,8},{4,12},{8,0},{12,4},{1,9},{5,13},{9,1},{13,5},{2,10},{6,14},... | collective-permute-start | bytes 221192 | tf_op jit(solution)/shard_map/ppermute | solution.py:312
  16.1 0.2 collective-permute-start.2
  16.3 4.7 %collective-permute-done.1.refs_2_ = bf16[16,2304]{1,0:T(8,128)(2,1)S(1)} collective-permute-done((bf16[16,2304]{1,0:T(8,128)(2,1)S(1)}, bf16[16,2304]{1,0:T(8,128)(2,1)S(1)}, u32[]{:S(2)}, u32[]{:S(2)}) %collective-permute-start.1) | collective-permute-done | bytes 73760 | tf_op jit(solution)/shard_map/ppermute | solution.py:312
  21.0 1.3 %collective-permute-done.2.refs_3_ = bf16[16,2304]{1,0:T(8,128)(2,1)S(1)} collective-permute-done((bf16[16,2304]{1,0:T(8,128)(2,1)S(1)}, bf16[16,2304]{1,0:T(8,128)(2,1)S(1)}, u32[]{:S(2)}, u32[]{:S(2)}) %collective-permute-start.2) | collective-permute-done | bytes 73760 | tf_op jit(solution)/shard_map/ppermute | solution.py:312
  22.4 0.6 %copy-done.11 = bf16[16,2304]{1,0:T(8,128)(2,1)} copy-done((bf16[16,2304]{1,0:T(8,128)(2,1)}, bf16[16,2304]{1,0:T(8,128)(2,1)S(1)}, u32[]{:S(2)}) %copy-start.11) | copy-done | bytes 73752
  23.0 1.9 %place.1.refs_0_ = bf16[32,2176]{1,0:T(8,128)(2,1)} custom-call(bf16[16,2304]{1,0:T(8,128)(2,1)} %copy-done.6, bf16[16,2304]{1,0:T(8,128)(2,1)} %copy-done.9, bf16[16,2304]{1,0:T(8,128)(2,1)} %copy-done.10, bf16[16,2304]{1,0:T(8,128)(2,1)} %copy-done.11), custom_call_target="tpu_custom_call" | custom-call | tf_op jit(solution)/shard_map/place/pallas_call | solution.py:319
  24.9 0.8 %collective-permute-start.5 = (bf16[32,2176]{1,0:T(8,128)(2,1)}, bf16[32,2176]{1,0:T(8,128)(2,1)S(1)}, u32[]{:S(2)}, u32[]{:S(2)}) collective-permute-start(bf16[32,2176]{1,0:T(8,128)(2,1)} %place.1.refs_0_), channel_id=1, source_target_pairs={{2,1},{1,2},{3,4},{4,3},{6,5},{5,6},{7,8},{8,7},{10,9},{9,10},{11,... | collective-permute-start | bytes 417800 | tf_op jit(solution)/shard_map/ppermute | solution.py:342
  25.7 1.3 %collective-permute-start.4 = (bf16[32,2176]{1,0:T(8,128)(2,1)}, bf16[32,2176]{1,0:T(8,128)(2,1)S(1)}, u32[]{:S(2)}, u32[]{:S(2)}) collective-permute-start(bf16[32,2176]{1,0:T(8,128)(2,1)} %place.1.refs_0_), channel_id=1, source_target_pairs={{2,3},{1,0},{3,6},{4,1},{6,7},{5,4},{7,10},{8,5},{10,11},{9,8},{11... | collective-permute-start | bytes 417800 | tf_op jit(solution)/shard_map/ppermute | solution.py:342
  27.0 4.3 %collective-permute-start.8 = (bf16[768]{0:T(1024)(128)(2,1)}, bf16[768]{0:T(1024)(128)(2,1)S(1)}, u32[]{:S(2)}, u32[]{:S(2)}) collective-permute-start(bf16[768]{0:T(1024)(128)(2,1)} %param.14), channel_id=1, source_target_pairs={{2,0},{0,2},{3,1},{1,3},{6,4},{4,6},{7,5},{5,7},{10,8},{8,10},{11,... | collective-permute-start | bytes 4616 | tf_op jit(solution)/shard_map/ppermute | solution.py:364
  31.3 0.7 %stack.9 = bf16[1,768]{1,0:T(2,128)(2,1)S(1)} reshape(bf16[768]{0:T(1024)(128)(2,1)} %param.14) | data formatting | bytes 3072 | tf_op jit(solution)/shard_map/stack | solution.py:361
  32.0 0.7 %reshape.15.refs_8_ = f32[2,1,768]{2,1,0:T(1,128)S(1)} reshape(f32[1536]{0:T(1024)} %param.15) | data formatting | bytes 12288 | tf_op jit(solution)/shard_map/reshape | solution.py:395
  32.7 2.3 %reverse = f32[12,640]{1,0:T(8,128)S(1)} reverse(f32[12,640]{1,0:T(8,128)} %bitcast.9), dimensions={1} | reverse | bytes 61440
  35.0 0.1 slice
  35.1 0.0 copy-start.8
  35.1 0.6 %copy-done.8 = s32[4]{0:T(128)S(1)} copy-done((s32[4]{0:T(128)S(1)}, s32[4]{0:T(128)}, u32[]{:S(2)}) %copy-start.8) | copy-done | bytes 40
  35.8 2.3 %bias.1.refs_10_ = f32[6,2,288,432]{3,2,1,0:T(8,128)S(1)} custom-call(s32[4]{0:T(128)S(1)} %copy-done.8, f32[12,640]{1,0:T(8,128)S(1)} %pad.4.table_ref), custom_call_target="tpu_custom_call" | custom-call | tf_op jit(solution)/shard_map/bias/pallas_call | solution.py:352
  38.1 2.9 %copy-done = f32[6,2,288,432]{3,2,1,0:T(8,128)} copy-done((f32[6,2,288,432]{3,2,1,0:T(8,128)}, f32[6,2,288,432]{3,2,1,0:T(8,128)S(1)}, u32[]{:S(2)}) %copy-start) | copy-done | bytes 5971992
  41.0 0.1 collective-permute-start.3
  41.1 0.1 collective-permute-start.7
  41.3 1.6 %collective-permute-done.7 = bf16[256,768]{1,0:T(8,128)(2,1)S(1)} collective-permute-done((bf16[256,768]{1,0:T(8,128)(2,1)S(1)}, bf16[256,768]{1,0:T(8,128)(2,1)S(1)}, u32[]{:S(2)}, u32[]{:S(2)}) %collective-permute-start.7) | collective-permute-done | bytes 393248 | tf_op jit(solution)/shard_map/ppermute | solution.py:282
  42.9 0.1 broadcast_select_fusion
  43.0 3.4 %collective-permute-done.3.refs_1_ = bf16[32,2176]{1,0:T(8,128)(2,1)S(1)} collective-permute-done((bf16[32,2176]{1,0:T(8,128)(2,1)S(1)}, bf16[32,2176]{1,0:T(8,128)(2,1)S(1)}, u32[]{:S(2)}, u32[]{:S(2)}) %collective-permute-start.3) | collective-permute-done | bytes 139296 | tf_op jit(solution)/shard_map/ppermute | solution.py:334
  46.4 14.6 %attend.1 = bf16[272,768]{1,0:T(8,128)(2,1)} custom-call(bf16[32,2176]{1,0:T(8,128)(2,1)S(1)} %copy-done.4, bf16[32,2176]{1,0:T(8,128)(2,1)S(1)} %collective-permute-done.3.refs_1_, bf16[32,2176]{1,0:T(8,128)(2,1)S(1)} %get-tuple-element.16.refs_2_, bf16[32,2176]{1,0:T(8,128)(2,1)S(1)} %get-tuple-element.15.refs_3_, bf16[512,768]{1,0:T(8,128)(2,1)S(1)} %copy-done.1, ...), custom_call_target="tpu_custom_call" | custom-call | tf_op jit(solution)/shard_map/attend/pallas_call | solution.py:371
  (25 shorter events, 0.1 us)
Async XLA Ops:
  0.0 46.4 %copy-start.1 = (bf16[512,768]{1,0:T(8,128)(2,1)S(1)}, bf16[512,768]{1,0:T(8,128)(2,1)}, u32[]{:S(2)}) copy-start(bf16[512,768]{1,0:T(8,128)(2,1)} %refs_4_.1) | copy-start | bytes 2359300
  1.1 40.0 %collective-permute-start.6 = (bf16[256,768]{1,0:T(8,128)(2,1)S(1)}, bf16[256,768]{1,0:T(8,128)(2,1)S(1)}, u32[]{:S(2)}, u32[]{:S(2)}) collective-permute-start(bf16[256,768]{1,0:T(8,128)(2,1)S(1)} %constant_dynamic-slice_fusion), channel_id=1, source_target_pairs={{2,0},{0,2},{3,1},{1,3},{6,4},{4,6},{7,5},{5,7},{10,8},{8,10},{11,... | collective-permute-start | bytes 1179656 | tf_op jit(solution)/shard_map/ppermute | solution.py:281
  4.1 1.2 %copy-start.2 = (bf16[2,512,512]{2,1,0:T(8,128)(2,1)S(1)}, bf16[2,512,512]{2,1,0:T(8,128)(2,1)}, u32[]{:S(2)}) copy-start(bf16[2,512,512]{2,1,0:T(8,128)(2,1)} %constant.20.clone.fourier_ref) | copy-start | bytes 3145732
  5.3 1.1 %copy-start.3 = (f32[1,1,1,64,3072]{4,3,2,1,0:T(8,128)S(1)}, f32[1,1,1,64,3072]{4,3,2,1,0:T(8,128)}, u32[]{:S(2)}) copy-start(f32[1,1,1,64,3072]{4,3,2,1,0:T(8,128)} %param.10) | copy-start | bytes 2359300
  6.5 0.9 %copy-start.5 = (bf16[2,512,128]{2,1,0:T(8,128)(2,1)S(1)}, bf16[2,512,128]{2,1,0:T(8,128)(2,1)}, u32[]{:S(2)}) copy-start(bf16[2,512,128]{2,1,0:T(8,128)(2,1)} %constant.21.clone.mel_ref) | copy-start | bytes 786436
  7.4 0.7 %copy-start.7 = (s32[1,1,1,64]{3,2,1,0:T(1,128)S(1)}, s32[1,1,1,64]{3,2,1,0:T(1,128)}, u32[]{:S(2)}) copy-start(s32[1,1,1,64]{3,2,1,0:T(1,128)} %param.11) | copy-start | bytes 772
  11.3 0.6 %copy-start.6 = (bf16[16,2304]{1,0:T(8,128)(2,1)}, bf16[16,2304]{1,0:T(8,128)(2,1)S(1)}, u32[]{:S(2)}) copy-start(bf16[16,2304]{1,0:T(8,128)(2,1)S(1)} %get-tuple-element.9.refs_0_) | copy-start | bytes 221188
  11.9 4.4 %collective-permute-start = (bf16[16,2304]{1,0:T(8,128)(2,1)S(1)}, bf16[16,2304]{1,0:T(8,128)(2,1)S(1)}, u32[]{:S(2)}, u32[]{:S(2)}) collective-permute-start(bf16[16,2304]{1,0:T(8,128)(2,1)S(1)} %get-tuple-element.10), channel_id=1, source_target_pairs={{0,4},{4,0},{8,12},{12,8},{1,5},{5,1},{9,13},{13,9},{2,6},{6,2},{1... | collective-permute-start | bytes 221192 | tf_op jit(solution)/shard_map/ppermute | solution.py:312
  13.5 7.5 %collective-permute-start.1 = (bf16[16,2304]{1,0:T(8,128)(2,1)S(1)}, bf16[16,2304]{1,0:T(8,128)(2,1)S(1)}, u32[]{:S(2)}, u32[]{:S(2)}) collective-permute-start(bf16[16,2304]{1,0:T(8,128)(2,1)S(1)} %get-tuple-element.11), channel_id=1, source_target_pairs={{0,8},{4,12},{8,0},{12,4},{1,9},{5,13},{9,1},{13,5},{2,10},{6,14},... | collective-permute-start | bytes 221192 | tf_op jit(solution)/shard_map/ppermute | solution.py:312
  16.1 6.3 %collective-permute-start.2 = (bf16[16,2304]{1,0:T(8,128)(2,1)S(1)}, bf16[16,2304]{1,0:T(8,128)(2,1)S(1)}, u32[]{:S(2)}, u32[]{:S(2)}) collective-permute-start(bf16[16,2304]{1,0:T(8,128)(2,1)S(1)} %get-tuple-element.12), channel_id=1, source_target_pairs={{0,12},{4,8},{8,4},{12,0},{1,13},{5,9},{9,5},{13,1},{2,14},{6,10},... | collective-permute-start | bytes 221192 | tf_op jit(solution)/shard_map/ppermute | solution.py:312
  16.3 6.0 %copy-start.9 = (bf16[16,2304]{1,0:T(8,128)(2,1)}, bf16[16,2304]{1,0:T(8,128)(2,1)S(1)}, u32[]{:S(2)}) copy-start(bf16[16,2304]{1,0:T(8,128)(2,1)S(1)} %collective-permute-done.refs_1_) | copy-start | bytes 221188
  21.0 1.4 %copy-start.10 = (bf16[16,2304]{1,0:T(8,128)(2,1)}, bf16[16,2304]{1,0:T(8,128)(2,1)S(1)}, u32[]{:S(2)}) copy-start(bf16[16,2304]{1,0:T(8,128)(2,1)S(1)} %collective-permute-done.1.refs_2_) | copy-start | bytes 221188
  22.4 0.6 %copy-start.11 = (bf16[16,2304]{1,0:T(8,128)(2,1)}, bf16[16,2304]{1,0:T(8,128)(2,1)S(1)}, u32[]{:S(2)}) copy-start(bf16[16,2304]{1,0:T(8,128)(2,1)S(1)} %collective-permute-done.2.refs_3_) | copy-start | bytes 221188
  24.9 16.1 %copy-start.4 = (bf16[32,2176]{1,0:T(8,128)(2,1)S(1)}, bf16[32,2176]{1,0:T(8,128)(2,1)}, u32[]{:S(2)}) copy-start(bf16[32,2176]{1,0:T(8,128)(2,1)} %place.1.refs_0_) | copy-start | bytes 417796
  24.9 16.3 %collective-permute-start.5 = (bf16[32,2176]{1,0:T(8,128)(2,1)}, bf16[32,2176]{1,0:T(8,128)(2,1)S(1)}, u32[]{:S(2)}, u32[]{:S(2)}) collective-permute-start(bf16[32,2176]{1,0:T(8,128)(2,1)} %place.1.refs_0_), channel_id=1, source_target_pairs={{2,1},{1,2},{3,4},{4,3},{6,5},{5,6},{7,8},{8,7},{10,9},{9,10},{11,... | collective-permute-start | bytes 417800 | tf_op jit(solution)/shard_map/ppermute | solution.py:342
  25.7 15.5 %collective-permute-start.4 = (bf16[32,2176]{1,0:T(8,128)(2,1)}, bf16[32,2176]{1,0:T(8,128)(2,1)S(1)}, u32[]{:S(2)}, u32[]{:S(2)}) collective-permute-start(bf16[32,2176]{1,0:T(8,128)(2,1)} %place.1.refs_0_), channel_id=1, source_target_pairs={{2,3},{1,0},{3,6},{4,1},{6,7},{5,4},{7,10},{8,5},{10,11},{9,8},{11... | collective-permute-start | bytes 417800 | tf_op jit(solution)/shard_map/ppermute | solution.py:342
  27.0 14.0 %collective-permute-start.8 = (bf16[768]{0:T(1024)(128)(2,1)}, bf16[768]{0:T(1024)(128)(2,1)S(1)}, u32[]{:S(2)}, u32[]{:S(2)}) collective-permute-start(bf16[768]{0:T(1024)(128)(2,1)} %param.14), channel_id=1, source_target_pairs={{2,0},{0,2},{3,1},{1,3},{6,4},{4,6},{7,5},{5,7},{10,8},{8,10},{11,... | collective-permute-start | bytes 4616 | tf_op jit(solution)/shard_map/ppermute | solution.py:364
  35.1 0.7 %copy-start.8 = (s32[4]{0:T(128)S(1)}, s32[4]{0:T(128)}, u32[]{:S(2)}) copy-start(s32[4]{0:T(128)} %lengths_ref.1) | copy-start | bytes 52
  38.1 2.9 %copy-start = (f32[6,2,288,432]{3,2,1,0:T(8,128)}, f32[6,2,288,432]{3,2,1,0:T(8,128)S(1)}, u32[]{:S(2)}) copy-start(f32[6,2,288,432]{3,2,1,0:T(8,128)S(1)} %bias.1.refs_10_) | copy-start | bytes 17915908
  41.0 5.4 %collective-permute-start.3 = (bf16[32,2176]{1,0:T(8,128)(2,1)S(1)}, bf16[32,2176]{1,0:T(8,128)(2,1)S(1)}, u32[]{:S(2)}, u32[]{:S(2)}) collective-permute-start(bf16[32,2176]{1,0:T(8,128)(2,1)S(1)} %copy-done.4), channel_id=1, source_target_pairs={{2,0},{0,2},{3,1},{1,3},{6,4},{4,6},{7,5},{5,7},{10,8},{8,10},{11,... | collective-permute-start | bytes 417800 | tf_op jit(solution)/shard_map/ppermute | solution.py:334
  41.1 1.8 %collective-permute-start.7 = (bf16[256,768]{1,0:T(8,128)(2,1)S(1)}, bf16[256,768]{1,0:T(8,128)(2,1)S(1)}, u32[]{:S(2)}, u32[]{:S(2)}) collective-permute-start(bf16[256,768]{1,0:T(8,128)(2,1)S(1)} %collective-permute-done.6), channel_id=1, source_target_pairs={{0,1},{1,0},{2,3},{3,2},{4,5},{5,4},{6,7},{7,6},{8,9},{9,8},{10,11... | collective-permute-start | bytes 1179656 | tf_op jit(solution)/shard_map/ppermute | solution.py:282
where the time goes:
time: 61.6 us; the launch traced here: 61 us
  Pallas kernels  22.1 us (36%)
  starting transfers between devices  13.9 us (23%)
  local copies, waits for them, and re-layouts  13.6 us (22%)
  waiting for transfers between devices  11.1 us (18%)
    pallas_call x1, Pallas kernels, local(): pl.pallas_call(functools.partial(attend_kernel, n), out_shape=jax.ShapeDt...  14.6 us
    unnamed x26, local copies, waits for them, and re-layouts  11.1 us
    ppermute x3, waiting for transfers between devices, local(): lax.ppermute(packed[d], 'seq', [(i, i ^ d) for i in range(shards)])  6.03 us
    ppermute x3, starting transfers between devices, local(): lax.ppermute(packed[d], 'seq', [(i, i ^ d) for i in range(shards)])  4.39 us
    ppermute x1, starting transfers between devices, local(): lax.ppermute(sub_bias, 'head', [((i + d) % n, i) for i in range(n)])  4.29 us
    ppermute x1, waiting for transfers between devices, local(): lax.ppermute(own, 'head', [((i + d) % n, i) for i in range(n)])  3.43 us
    pallas_call x1, Pallas kernels, local(): pl.pallas_call(functools.partial(mel_kernel, shards, capacity, relative),...  3.24 us
    ppermute x1, starting transfers between devices, exchange_weights(): got = lax.ppermute(mine, 'head', [((i + d) % n, i) for i in range(n)])  3 us
  transfers between devices with their start and end apart: 9, of which 4 were waited for; matrix products, arithmetic and copies ran while one was open for 6% of the time, Pallas kernels for 12%

commit v1 on v0

v1 whole, which is shorter than its diff:
```python
import functools
import math

import jax
import jax.numpy as jnp
import ml_dtypes
import numpy as np
from jax import lax
from jax.experimental import pallas as pl
from jax.experimental.pallas import tpu as pltpu
from jax.sharding import PartitionSpec as P

HDIM = 64
MEL = 128
NFFT = 512
HOP = 160
FP = 17
CH = 136
PE = 32

SAMPLE_RATE = 16000.0
EPSILON = 1e-05
MASKED = -1e30

LANES = 128
PIECE_BITS = 5
ROWS = 144
GROUP = 4
STACK = 4
MEL_WIDTH = FP * MEL
BF16 = jnp.bfloat16
F32 = jnp.float32


def split_bf16(values):
    high = values.astype(ml_dtypes.bfloat16)
    low = (values - high.astype(np.float64)).astype(ml_dtypes.bfloat16)
    return np.stack([high, low])


def fourier_tables():
    n = np.arange(NFFT)
    bins = NFFT // 2
    window = 0.5 - 0.5 * np.cos(2.0 * np.pi * n / NFFT)
    phase = 2.0 * np.pi * ((n[:, None] * np.arange(bins + 1)[None, :]) % NFFT) / NFFT
    sine = np.sin(phase[:, :bins])
    sine[:, 0] = np.cos(phase[:, bins])
    return split_bf16(np.concatenate([np.cos(phase[:, :bins]), sine], axis=1) * window[:, None])


def mel_tables():
    bins = NFFT // 2
    highest = 2595.0 * math.log10(1.0 + SAMPLE_RATE / 2.0 / 700.0)
    points = np.arange(MEL + 2) * (highest / (MEL + 1))
    hertz = 700.0 * (10.0 ** (points / 2595.0) - 1.0)
    centres = np.arange(bins + 1) * (SAMPLE_RATE / NFFT)
    rising = (centres[:, None] - hertz[None, :-2]) / (hertz[1:-1] - hertz[:-2])[None, :]
    falling = (hertz[None, 2:] - centres[:, None]) / (hertz[2:] - hertz[1:-1])[None, :]
    filters = np.maximum(0.0, np.minimum(rising, falling))
    high, low = split_bf16(np.concatenate([filters, np.zeros((15, MEL))], axis=0))
    return np.concatenate([high, low], axis=1)


def dot(a, b):
    return jnp.dot(a, b, preferred_element_type=F32)


def iota(shape, dim):
    return lax.broadcasted_iota(jnp.int32, shape, dim)


def mel_kernel(
    shards, capacity, relative, x_hbm, target_hbm, weight_hbm, fourier_hbm, mel_hbm, *refs
):
    sent, *outs = refs[:-5]
    x_ref, target_ref, fourier_ref, mel_ref, sems = refs[-5:]
    slots, rows = x_ref.shape[0], sent.shape[0]
    first = pl.multiple_of(lax.axis_index("sub") * rows, rows)
    copies = [
        pltpu.make_async_copy(source, target, sems.at[k])
        for k, (source, target) in enumerate(
            (
                (x_hbm, x_ref),
                (fourier_hbm, fourier_ref),
                (mel_hbm, mel_ref),
                (target_hbm, target_ref),
                (weight_hbm.at[pl.ds(first, rows), :], sent),
            )
        )
    ]
    for copy in copies:
        copy.start()
    copies[3].wait()
    target = target_ref[...]
    owner = lax.shift_right_arithmetic(target, PIECE_BITS)
    place = jnp.where(target < 0, 0, (target & (PE - 1)) + 1).astype(F32)
    row, col = iota((slots, slots), 0), iota((slots, slots), 1)
    diagonal = row == col
    owner_col = jnp.sum(jnp.where(diagonal, owner, 0), axis=1, keepdims=True)
    place_col = jnp.sum(jnp.where(diagonal, place, 0.0), axis=1, keepdims=True)
    rank = jnp.sum(((owner_col == owner) & (row < col)).astype(jnp.int32), axis=0, keepdims=True)
    chosen = row // capacity
    if relative:
        chosen = chosen ^ lax.axis_index("seq")
    pick = ((chosen == owner) & (row % capacity == rank)).astype(F32).astype(BF16)
    marks = jnp.broadcast_to(place_col, (slots, LANES)).astype(BF16)

    copies[0].wait()
    x = x_ref[...]
    frames = [None] * FP
    bins = NFFT // 2
    later = iota((1, bins), 1) > 0
    for phase in range(4):
        shift = phase * (HOP % LANES)
        moved = x if phase == 0 else pltpu.roll(x, x.shape[1] - shift, 1)
        high = moved.astype(BF16)
        low = (moved - high.astype(F32)).astype(BF16)
        members = list(range(phase, FP, 4))
        starts = [HOP * f - shift for f in members]
        high = jnp.concatenate([high[:, s : s + NFFT] for s in starts], axis=0)
        low = jnp.concatenate([low[:, s : s + NFFT] for s in starts], axis=0)
        if phase == 0:
            copies[1].wait()
        table_high, table_low = fourier_ref[0], fourier_ref[1]
        spectra = dot(
            jnp.concatenate([high, low, high], axis=1),
            jnp.concatenate([table_high, table_high, table_low], axis=0),
        )
        squares = spectra * spectra
        if phase == 0:
            copies[2].wait()
        if phase == 0:
            filters = mel_ref[:bins, :]
            last_row = mel_ref[bins:, :].astype(F32)
            last_row = last_row[:1, :MEL] + last_row[:1, MEL:]
        last = squares[:, bins : bins + 1] * last_row
        power = squares[:, :bins] + jnp.where(later, squares[:, bins:], 0.0)
        power_high = power.astype(BF16)
        power_low = (power - power_high.astype(F32)).astype(BF16)
        both = dot(
            jnp.concatenate([power_high, power_low], axis=1),
            jnp.concatenate([filters, filters], axis=0),
        )
        energy = both[:, :MEL] + both[:, MEL:] + last
        log_mel = jnp.log(1.0 + energy).astype(BF16)
        for k, f in enumerate(members):
            frames[f] = log_mel[k * slots : (k + 1) * slots]
    packed = dot(pick, jnp.concatenate(frames + [marks], axis=1)).astype(BF16)
    count = slots // len(outs)
    for d, out in enumerate(outs):
        out[...] = packed[d * count : (d + 1) * count]
    copies[4].wait()


def place_kernel(*refs):
    parts, out = refs[:-1], refs[-1]
    rows = jnp.concatenate([part[...] for part in parts], axis=0)
    slots = rows.shape[0]
    mark = rows[:, MEL_WIDTH : MEL_WIDTH + LANES].astype(F32)[:, :1]
    row, col = iota((slots, slots), 0), iota((slots, slots), 1)
    mark = jnp.sum(jnp.where(row == col, mark, 0.0), axis=0, keepdims=True)
    at = iota((PE, slots), 0)
    groups = PE // GROUP
    wanted = (at % groups) * GROUP + at // groups + 1
    pick = (wanted.astype(F32) == mark).astype(F32).astype(BF16)
    out[...] = dot(pick, rows[:, :MEL_WIDTH]).astype(BF16)


def token_rows(pieces):
    groups = PE // GROUP
    pieces = pieces.astype(F32)
    rows = []
    for i in range(FP):
        cells = []
        for j in range(STACK):
            q, f = divmod(STACK * i + j, FP)
            cells.append(pieces[q * groups : (q + 1) * groups, f * MEL : (f + 1) * MEL])
        rows.append(jnp.concatenate(cells, axis=1))
    rows.append(jnp.zeros((ROWS - CH, STACK * MEL), F32))
    mixed = jnp.concatenate(rows, axis=0).astype(BF16)
    row, col = iota((ROWS, ROWS), 0), iota((ROWS, ROWS), 1)
    token = (col % groups) * FP + col // groups
    order = ((row == token) & (col < CH)).astype(F32).astype(BF16)
    return dot(order, mixed).astype(BF16)


def prepare_kernel(
    lengths_hbm, table_hbm, qkv_hbm, out_ref, qkv_ref, lengths_ref, table_ref, flipped, sems
):
    copies = [
        pltpu.make_async_copy(lengths_hbm, lengths_ref, sems.at[0]),
        pltpu.make_async_copy(table_hbm, table_ref, sems.at[1]),
        pltpu.make_async_copy(qkv_hbm, qkv_ref, sems.at[2]),
    ]
    for copy in copies:
        copy.start()
    copies[0].wait()
    copies[1].wait()
    pairs, blocks = out_ref.shape[:2]
    half = blocks * CH
    first = (lax.axis_index("seq") * lax.axis_size("sub") + lax.axis_index("sub")) * half
    total = lax.axis_size("seq") * lax.axis_size("sub") * half
    lane, row = iota((1, 3 * ROWS), 1), iota((ROWS, 1), 0)
    key_block = lane // ROWS
    key_place = lane - key_block * ROWS
    masks = []
    for c in range(blocks):
        query = first + c * CH + row
        key = first + (c - 1) * CH + key_block * CH + key_place
        query_utt, key_utt = jnp.zeros_like(query), jnp.zeros_like(key)
        end = jnp.int32(0)
        for r in range(lengths_ref.shape[0]):
            end = end + lengths_ref[r]
            query_utt = query_utt + (query >= end).astype(jnp.int32)
            key_utt = key_utt + (key >= end).astype(jnp.int32)
        inside = (key >= 0) & (key < total) & (key_place < CH)
        key_utt = jnp.where(inside, key_utt, -1)
        masks.append(jnp.where(query_utt == key_utt, 0.0, MASKED))
    heads, entries = table_ref.shape
    width = flipped.shape[1]
    mirror = iota((entries, width), 0) + iota((entries, width), 1) == entries - 1
    mirror = mirror.astype(F32).astype(BF16)
    rest, lines = table_ref[...], 0.0
    for _ in range(3):
        part = rest.astype(BF16)
        rest = rest - part.astype(F32)
        lines = lines + dot(part, mirror)
    flipped[...] = lines

    def one_head(head, side):
        line = jnp.broadcast_to(flipped[pl.ds(head, 1), :], (ROWS, width))
        turned = [
            pltpu.roll(line, (8 * b - (CH - 1)) % width, 1, stride=1, stride_axis=0)[:, : 3 * ROWS]
            for b in range(3)
        ]
        bias = jnp.where(
            key_block == 0, turned[0], jnp.where(key_block == 1, turned[1], turned[2])
        )
        for c in range(blocks):
            out_ref[head // 2, c, side * ROWS : (side + 1) * ROWS, :] = bias + masks[c]

    @pl.loop(0, pairs)
    def _(pair):
        one_head(2 * pair, 0)
        one_head(2 * pair + 1, 1)

    copies[2].wait()


def normalize(tokens, conv, conv_bias, gain, out):
    summed = dot(tokens, conv[...]) + conv_bias[...]
    features = (summed / (1.0 + jnp.exp(-summed))).astype(BF16).astype(F32)
    scale = 1.0 / features.shape[1]
    centred = features - jnp.sum(features, axis=1, keepdims=True) * scale
    variance = jnp.sum(centred * centred, axis=1, keepdims=True) * scale
    out[...] = (centred * lax.rsqrt(variance + EPSILON) * gain[...]).astype(BF16)


def own_kernel(n, *refs):
    pieces, parts, refs = refs[0], refs[1 : 2 * n], refs[2 * n :]
    bias_parts, gain_rows, refs = refs[:n], refs[n], refs[n + 1 :]
    qkv, q_out, k_out, v_out, conv, conv_bias, gain, normed = refs
    me, core = lax.axis_index("head"), lax.axis_index("sub")
    depth = parts[0].shape[1]
    for d in range(n):
        start = pl.multiple_of(lax.rem(me + d, n) * depth, depth)
        at = pl.ds(start, depth)
        lines = bias_parts[d][...].astype(F32)
        for k in range(depth // LANES):
            conv_bias[:, pl.ds(start + k * LANES, LANES)] = lines[k : k + 1]
        if d == 0:
            conv[:, at] = parts[0][...]
        else:
            got, swapped = parts[2 * d - 1 : 2 * d + 1]
            rows = got.shape[0]
            conv[pl.ds(pl.multiple_of(core * rows, rows), rows), at] = got[...]
            conv[pl.ds(pl.multiple_of((1 - core) * rows, rows), rows), at] = swapped[...]
    for k in range(gain_rows.shape[0]):
        gain[:, k * LANES : (k + 1) * LANES] = gain_rows[k : k + 1, :]
    normalize(token_rows(pieces[...]), conv, conv_bias, gain, normed)
    for p, out in enumerate((q_out, k_out, v_out)):
        out[0] = dot(normed[...], qkv[p]).astype(BF16)


def others_kernel(*refs):
    pieces = refs[:-8]
    conv, conv_bias, gain, qkv, *outs, normed = refs[-8:]
    tokens = jnp.concatenate([token_rows(piece[...]) for piece in pieces], axis=0)
    normalize(tokens, conv, conv_bias, gain, normed)
    for p, out in enumerate(outs):
        got = dot(normed[...], qkv[p]).astype(BF16)
        for k in range(len(pieces)):
            out[k] = got[k * ROWS : (k + 1) * ROWS]


def attend(q, k, v, bias):
    low_lanes = iota((ROWS, LANES), 1) < HDIM
    q = q * jnp.asarray(1.0 / math.sqrt(HDIM), BF16)
    zero = jnp.zeros_like(q)
    q = jnp.concatenate([jnp.where(low_lanes, q, zero), jnp.where(low_lanes, zero, q)], axis=0)
    scores = lax.dot_general(q, k, (((1,), (1,)), ((), ())), preferred_element_type=F32) + bias
    weights = jnp.exp(scores - jnp.max(scores, axis=1, keepdims=True))
    total = jnp.sum(weights, axis=1, keepdims=True)
    context = dot(weights.astype(BF16), v) * (1.0 / total)
    return jnp.where(low_lanes, context[:ROWS], context[ROWS:])


def inner_kernel(n, *refs):
    own, others, near = refs[:3], refs[3:6], refs[6]
    conv, conv_bias, gain, qkv, bias, out, keys, values, queries, normed = refs[7:]
    me, core = lax.axis_index("head"), lax.axis_index("sub")
    for source, target, first in zip(own, (queries, keys, values), (0, 1, 1)):
        target[first + me] = source[0]
    for d in range(1, n):
        for source, target, first in zip(others, (queries, keys, values), (0, 1, 1)):
            target[first + lax.rem(me + d, n)] = source[d - 1]
    normalize(token_rows(near[...]), conv, conv_bias, gain, normed)
    place = jnp.where(core == 0, n + 1, 0)
    keys[place] = dot(normed[...], qkv[1]).astype(BF16)
    values[place] = dot(normed[...], qkv[2]).astype(BF16)
    for k in range(n - 1):
        c = k + 1 - core
        for pair in range(qkv.shape[2] // LANES):
            at = slice(pair * LANES, (pair + 1) * LANES)
            out[k, :, at] = attend(
                queries[c, :, at],
                keys[pl.ds(c, 3), :, at].reshape(3 * ROWS, LANES),
                values[pl.ds(c, 3), :, at].reshape(3 * ROWS, LANES),
                bias[pair, c],
            ).astype(BF16)
    edge = jnp.where(core == 0, 0, n - 1)
    queries[0] = queries[edge]
    first = jnp.where(core == 0, 1, n - 1)
    for target in (keys, values):
        kept = target[pl.ds(first, 2)]
        target[0] = kept[0]
        target[1] = kept[1]


def outer_kernel(n, *refs):
    inner, keys, values, queries, far, conv, conv_bias, gain, qkv, bias = refs[:10]
    out, all_keys, all_values, normed = refs[10:]
    core = lax.axis_index("sub")
    normalize(token_rows(far[...]), conv, conv_bias, gain, normed)
    for p, source, target in ((1, keys, all_keys), (2, values, all_values)):
        target[1 - core] = source[0]
        target[2 - core] = source[1]
        target[2 * core] = dot(normed[...], qkv[p]).astype(BF16)
    c = jnp.where(core == 0, 0, n - 1)
    for pair in range(qkv.shape[2] // LANES):
        at = slice(pair * LANES, (pair + 1) * LANES)
        context = attend(
            queries[0, :, at],
            all_keys[:, :, at].reshape(3 * ROWS, LANES),
            all_values[:, :, at].reshape(3 * ROWS, LANES),
            bias[pair, c],
        ).astype(BF16)
        context = context.astype(F32)[:CH]
        done = [inner[k, :, at].astype(F32)[:CH] for k in range(n - 1)]
        out[:, at] = jnp.where(
            core == 0,
            jnp.concatenate([context] + done, axis=0),
            jnp.concatenate(done + [context], axis=0),
        ).astype(BF16)


def vmem(count):
    return [pl.BlockSpec(memory_space=pltpu.VMEM)] * count


def from_hbm(array):
    return pltpu.with_memory_space_constraint(array, pltpu.HBM)


def in_vmem(array):
    return pltpu.with_memory_space_constraint(array, pltpu.VMEM)


def from_heads(block, n):
    return [lax.ppermute(block, "head", [((i + d) % n, i) for i in range(n)]) for d in range(1, n)]


def local(
    wave_pieces, piece_target, utt_lengths, sub_weight, sub_bias, norm_gain, qkv_weight, rel_bias
):
    shards, n, cores = lax.axis_size("seq"), lax.axis_size("head"), lax.axis_size("sub")
    assert cores == 2
    slots, length = wave_pieces.shape[3:]
    capacity = slots // shards
    relative = shards in (2, 4) and capacity % 16 == 0
    outs = shards if relative else 1
    payload = MEL_WIDTH + LANES
    fourier, filters = fourier_tables(), mel_tables()
    in_hbm = pl.BlockSpec(memory_space=pltpu.HBM)
    conv_rows = sub_weight.shape[0]
    bias_got = from_heads(sub_bias, n)
    weight_sent, *packed = pl.pallas_call(
        functools.partial(mel_kernel, shards, capacity, relative),
        out_shape=[jax.ShapeDtypeStruct((conv_rows // cores, sub_weight.shape[1]), BF16)]
        + [jax.ShapeDtypeStruct((slots // outs, payload), BF16)] * outs,
        in_specs=[in_hbm] * 5,
        out_specs=vmem(outs + 1),
        scratch_shapes=[
            pltpu.VMEM((slots, length), F32),
            pltpu.VMEM((1, slots), jnp.int32),
            pltpu.VMEM(fourier.shape, BF16),
            pltpu.VMEM(filters.shape, BF16),
            pltpu.SemaphoreType.DMA((5,)),
        ],
        compiler_params=pltpu.CompilerParams(vmem_limit_bytes=24 << 20),
        name="log_mel",
    )(
        from_hbm(wave_pieces.reshape(slots, length)),
        from_hbm(piece_target.reshape(1, slots)),
        from_hbm(sub_weight),
        from_hbm(jnp.asarray(fourier)),
        from_hbm(jnp.asarray(filters)),
    )
    if relative:
        received = [packed[0]] + [
            lax.ppermute(packed[d], "seq", [(i, i ^ d) for i in range(shards)])
            for d in range(1, shards)
        ]
    else:
        blocks = packed[0].reshape(shards, capacity, payload)
        blocks = lax.all_to_all(blocks, "seq", split_axis=0, concat_axis=0, tiled=True)
        received = [blocks.reshape(slots, payload)]

    weight_got = from_heads(weight_sent, n)

    local_width = qkv_weight.shape[2]
    pairs = local_width // LANES
    gain = norm_gain.reshape(-1, LANES)
    me, core = lax.axis_index("head"), lax.axis_index("sub")
    last, first = lax.rem(n - 1 - me + n, n), lax.rem(n - me, n)
    near_at, far_at = jnp.where(core == 0, last, first), jnp.where(core == 0, first, last)
    near_is, far_is = [near_at == d for d in range(n)], [far_at == d for d in range(n)]
    conv_bias = [part.reshape(-1, LANES) for part in [sub_bias] + bias_got]
    rel_bias, gain, near_is, far_is, _ = lax.optimization_barrier(
        (rel_bias, gain, near_is, far_is, packed[0])
    )
    entries = rel_bias.shape[1]
    qkv = jnp.transpose(qkv_weight, (1, 0, 2))
    bias, qkv = pl.pallas_call(
        prepare_kernel,
        out_shape=[
            pltpu.VMEM((pairs, n, 2 * ROWS, 3 * ROWS), F32),
            pltpu.VMEM(qkv.shape, BF16),
        ],
        in_specs=[in_hbm] * 3,
        out_specs=vmem(2),
        scratch_shapes=[
            pltpu.SMEM(utt_lengths.shape, jnp.int32),
            pltpu.VMEM(rel_bias.shape, F32),
            pltpu.VMEM((2 * pairs, entries + -entries % LANES), F32),
            pltpu.SemaphoreType.DMA((3,)),
        ],
        compiler_params=pltpu.CompilerParams(vmem_limit_bytes=8 << 20),
        cost_estimate=pl.CostEstimate(flops=1 << 31, bytes_accessed=8 << 20, transcendentals=0),
        name="prepare",
    )(from_hbm(utt_lengths), from_hbm(rel_bias), from_hbm(qkv))
    received, weight_got, conv_bias, bias, qkv, gain, near_is, far_is = lax.optimization_barrier(
        (received, weight_got, conv_bias, bias, qkv, gain, near_is, far_is)
    )
    conv = [sub_weight]
    for got in weight_got:
        conv += [got, lax.ppermute(got, "sub", [(0, 1), (1, 0)])]

    own = pl.pallas_call(
        place_kernel,
        out_shape=jax.ShapeDtypeStruct((PE, MEL_WIDTH), BF16),
        in_specs=vmem(len(received)),
        out_specs=vmem(1)[0],
        compiler_params=pltpu.CompilerParams(vmem_limit_bytes=8 << 20),
        name="place",
    )(*received)

    others = from_heads(own, n)
    near_sent = far_sent = own
    for d in range(1, n):
        near_sent = jnp.where(near_is[d], others[d - 1], near_sent)
        far_sent = jnp.where(far_is[d], others[d - 1], far_sent)
    near = lax.ppermute(near_sent, "sub", [(0, 1), (1, 0)])
    swaps = [(cores * k + 1, cores * k + 2) for k in range(shards - 1)]
    far = lax.ppermute(far_sent, ("seq", "sub"), swaps + [(b, a) for a, b in swaps])

    width = qkv_weight.shape[0]
    qkv = in_vmem(qkv)
    limit = pltpu.CompilerParams(vmem_limit_bytes=16 << 20)
    *own_qkv, whole, whole_bias, whole_gain = pl.pallas_call(
        functools.partial(own_kernel, n),
        out_shape=[jax.ShapeDtypeStruct((1, ROWS, local_width), BF16)] * 3
        + [
            jax.ShapeDtypeStruct((sub_weight.shape[0], width), BF16),
            jax.ShapeDtypeStruct((1, width), F32),
            jax.ShapeDtypeStruct((1, width), F32),
        ],
        in_specs=vmem(1 + len(conv) + n + 2),
        out_specs=vmem(6),
        scratch_shapes=[pltpu.VMEM((ROWS, width), BF16)],
        compiler_params=limit,
        cost_estimate=pl.CostEstimate(flops=2 << 30, bytes_accessed=9 << 20, transcendentals=0),
        name="own",
    )(own, *conv, *conv_bias, gain, qkv)
    weights = (whole, whole_bias, whole_gain, qkv)
    other_qkv = pl.pallas_call(
        others_kernel,
        out_shape=[jax.ShapeDtypeStruct((n - 1, ROWS, local_width), BF16)] * 3,
        in_specs=vmem(n - 1 + len(weights)),
        out_specs=vmem(3),
        scratch_shapes=[pltpu.VMEM(((n - 1) * ROWS, width), BF16)],
        compiler_params=limit,
        cost_estimate=pl.CostEstimate(flops=2 << 30, bytes_accessed=9 << 20, transcendentals=0),
        name="others",
    )(*others, *weights)
    inner, keys, values, queries = pl.pallas_call(
        functools.partial(inner_kernel, n),
        out_shape=[
            jax.ShapeDtypeStruct((n - 1, ROWS, local_width), BF16),
            jax.ShapeDtypeStruct((n + 2, ROWS, local_width), BF16),
            jax.ShapeDtypeStruct((n + 2, ROWS, local_width), BF16),
            jax.ShapeDtypeStruct((n, ROWS, local_width), BF16),
        ],
        in_specs=vmem(7 + len(weights) + 1),
        out_specs=vmem(4),
        scratch_shapes=[pltpu.VMEM((ROWS, width), BF16)],
        compiler_params=limit,
        cost_estimate=pl.CostEstimate(flops=4 << 30, bytes_accessed=9 << 20, transcendentals=0),
        name="inner",
    )(*own_qkv, *other_qkv, near, *weights, in_vmem(bias))
    return pl.pallas_call(
        functools.partial(outer_kernel, n),
        out_shape=jax.ShapeDtypeStruct((n * CH, local_width), BF16),
        in_specs=vmem(5 + len(weights) + 1),
        out_specs=vmem(1)[0],
        scratch_shapes=[
            pltpu.VMEM((3, ROWS, local_width), BF16),
            pltpu.VMEM((3, ROWS, local_width), BF16),
            pltpu.VMEM((ROWS, width), BF16),
        ],
        compiler_params=limit,
        name="outer",
    )(inner, keys, values, queries, far, *weights, in_vmem(bias))


def solution(mesh):
    placed = (
        P(("groups", "seq"), "head", "sub", None, None),
        P(("groups", "seq"), "head", "sub", None),
        P("groups"),
        P(None, "head"),
        P("head"),
        P(),
        P(None, None, "head"),
        P("head", None),
    )
    return jax.shard_map(
        local,
        mesh=mesh,
        in_specs=placed,
        out_specs=P(("groups", "seq", "sub"), "head"),
        check_vma=False,
    )
```

time: 61.6 us -> 37.9 us (0.62)
  local copies, waits for them, and re-layouts: 13.6 us -> 0.01 us
  waiting for transfers between devices: 11.1 us -> 6.72 us
  Pallas kernels: 22.1 us -> 19.2 us
  starting transfers between devices: 13.9 us -> 11.6 us
    unnamed x26 -> x6, local copies, waits for them, and re-layouts: 11.1 us -> 0.01 us
    ppermute x3, waiting for transfers between devices: 6.03 us -> 1.76 us  [local(): lax.ppermute(packed[d], 'seq', [(i, i ^ d) for i in range(shards)])]
    ppermute x6, starting transfers between devices: 9.52 us -> 7 us  [the longest x3 4.64 us: from_heads(): lax.ppermute(block, 'head', [((i + d) % n, i) for i in range(n)])]
    pallas_call x2 -> x5, Pallas kernels: 16.9 us -> 14.4 us  [the longest x1 3.78 us: local(): pl.pallas_call(functools.partial(outer_kernel, n), out_shape=jax.ShapeDty...]
    pallas_call x1, Pallas kernels: 1.91 us -> 0.25 us  [local(): pl.pallas_call(place_kernel, out_shape=jax.ShapeDtypeStruct((PE, MEL_WIDT...]
    pallas_call x1, Pallas kernels: 3.24 us -> 4.55 us  [local(): pl.pallas_call(functools.partial(mel_kernel, shards, capacity, relative),...]
    dynamic_slice x1 -> x0, local copies, waits for them, and re-layouts: 1.09 us -> none  [exchange_weights(): mine = lax.dynamic_slice_in_dim(weight, core * rows, rows, 0)]
    another operation x2 -> x0, local copies, waits for them, and re-layouts: 0.72 us -> none  [local(): jnp.stack([sub_bias] + [lax.ppermute(sub_bias, 'head', [((i + d) % n, i)...]
  transfers between devices with their start and end apart: 9 -> 9, of which waited for: 4 -> 4; matrix products, arithmetic and copies ran while one was open for 6% -> 0% of each run, Pallas kernels for 12% -> 28%
where the time goes in v1:
time: 37.9 us; the launch traced here: 37.7 us
  Pallas kernels  19.2 us (51%)
  starting transfers between devices  11.6 us (31%)
  waiting for transfers between devices  6.72 us (18%)
    ppermute x3, waiting for transfers between devices, from_heads(): lax.ppermute(block, 'head', [((i + d) % n, i) for i in range(n)])  4.95 us
    ppermute x3, starting transfers between devices, from_heads(): lax.ppermute(block, 'head', [((i + d) % n, i) for i in range(n)])  4.64 us
    ppermute x3, starting transfers between devices, local(): lax.ppermute(packed[d], 'seq', [(i, i ^ d) for i in range(shards)])  4.62 us
    pallas_call x1, Pallas kernels, local(): pl.pallas_call(functools.partial(mel_kernel, shards, capacity, relative),...  4.55 us
    pallas_call x1, Pallas kernels, local(): pl.pallas_call(functools.partial(outer_kernel, n), out_shape=jax.ShapeDty...  3.78 us
    pallas_call x1, Pallas kernels, local(): pl.pallas_call(functools.partial(inner_kernel, n), out_shape=[jax.ShapeDt...  3.21 us
    pallas_call x1, Pallas kernels, local(): pl.pallas_call(prepare_kernel, out_shape=[pltpu.VMEM((pairs, n, 2 * ROWS,...  3.06 us
    pallas_call x1, Pallas kernels, local(): pl.pallas_call(functools.partial(own_kernel, n), out_shape=[jax.ShapeDtyp...  2.2 us
  transfers between devices with their start and end apart: 9, of which 4 were waited for; matrix products, arithmetic and copies ran while one was open for 0% of the time, Pallas kernels for 28%

profile of v1, /device:TPU:0, one launch (start us, length us, event | category | flops | bytes accessed | tf_op | source)
XLA Modules:
  0.0 37.7 jit_solution(2438080922106863085)
XLA Ops:
  0.0 0.0 copy-start
  0.0 0.0 copy-start.2
  0.0 0.0 copy-start.1
  0.0 4.5 %log_mel.1 = (bf16[256,768]{1,0:T(8,128)(2,1)S(1)}, bf16[16,2304]{1,0:T(8,128)(2,1)S(1)}, bf16[16,2304]{1,0:T(8,128)(2,1)S(1)}, bf16[16,2304]{1,0:T(8,128)(2,1)S(1)}, bf16[16,2304]{1,0:T(8,128)(2,1)S(1)}) custom-call(f32[64,3072]{1,0:T(8,128)} %bitcast.9, s32[1,64]{1,0:T(1,128)} %bitcast.10, bf16[512,768]{1,0:T(8,128)(2,1)} %refs_1_.1, ...), custom_call_target="tpu_custom_call" | custom-call | tf_op jit(solution)/shard_map/log_mel/pallas_call | solution.py:397
  4.6 3.0 %collective-permute-start.3 = (bf16[256,768]{1,0:T(8,128)(2,1)S(1)}, bf16[256,768]{1,0:T(8,128)(2,1)S(1)}, u32[]{:S(2)}, u32[]{:S(2)}) collective-permute-start(bf16[256,768]{1,0:T(8,128)(2,1)S(1)} %get-tuple-element.45), channel_id=1, source_target_pairs={{2,0},{0,2},{3,1},{1,3},{6,4},{4,6},{7,5},{5,7},{10,8},{8,10},{11,... | collective-permute-start | bytes 1179656 | tf_op jit(solution)/shard_map/ppermute | solution.py:380
  7.6 0.1 collective-permute-start.4
  7.7 2.0 %collective-permute-start = (bf16[16,2304]{1,0:T(8,128)(2,1)S(1)}, bf16[16,2304]{1,0:T(8,128)(2,1)S(1)}, u32[]{:S(2)}, u32[]{:S(2)}) collective-permute-start(bf16[16,2304]{1,0:T(8,128)(2,1)S(1)} %get-tuple-element.42), channel_id=1, source_target_pairs={{0,4},{4,0},{8,12},{12,8},{1,5},{5,1},{9,13},{13,9},{2,6},{6,2},{1... | collective-permute-start | bytes 221192 | tf_op jit(solution)/shard_map/ppermute | solution.py:421
  9.7 2.6 %collective-permute-start.1 = (bf16[16,2304]{1,0:T(8,128)(2,1)S(1)}, bf16[16,2304]{1,0:T(8,128)(2,1)S(1)}, u32[]{:S(2)}, u32[]{:S(2)}) collective-permute-start(bf16[16,2304]{1,0:T(8,128)(2,1)S(1)} %get-tuple-element.43), channel_id=1, source_target_pairs={{0,8},{4,12},{8,0},{12,4},{1,9},{5,13},{9,1},{13,5},{2,10},{6,14},... | collective-permute-start | bytes 221192 | tf_op jit(solution)/shard_map/ppermute | solution.py:421
  12.3 0.0 collective-permute-start.2
  12.3 3.1 %prepare.1 = (f32[6,2,288,432]{3,2,1,0:T(8,128)S(1)}, bf16[3,1536,768]{2,1,0:T(8,128)(2,1)S(1)}) custom-call(s32[4]{0:T(128)} %lengths_hbm.1, f32[12,543]{1,0:T(8,128)} %table_hbm, bf16[3,1536,768]{2,1,0:T(8,128)(2,1)} %bitcast.11), custom_call_target="tpu_custom_call" | custom-call | flops 2147483648 | bytes 8388608 | tf_op jit(solution)/shard_map/prepare/pallas_call | solution.py:444
  15.3 1.4 %collective-permute-done.4 = bf16[768]{0:T(1024)(128)(2,1)S(1)} collective-permute-done((bf16[768]{0:T(1024)(128)(2,1)}, bf16[768]{0:T(1024)(128)(2,1)S(1)}, u32[]{:S(2)}, u32[]{:S(2)}) %collective-permute-start.4) | collective-permute-done | bytes 1568 | tf_op jit(solution)/shard_map/ppermute | solution.py:380
  16.7 0.0 collective-permute-done.refs_1_
  16.7 0.2 collective-permute-done.1.refs_2_
  16.9 1.6 %collective-permute-done.2.refs_3_ = bf16[16,2304]{1,0:T(8,128)(2,1)S(1)} collective-permute-done((bf16[16,2304]{1,0:T(8,128)(2,1)S(1)}, bf16[16,2304]{1,0:T(8,128)(2,1)S(1)}, u32[]{:S(2)}, u32[]{:S(2)}) %collective-permute-start.2) | collective-permute-done | bytes 73760 | tf_op jit(solution)/shard_map/ppermute | solution.py:421
  18.5 0.0 collective-permute-done.3.refs_2_
  18.5 0.3 place.1.refs_0_
  18.7 1.6 %collective-permute-start.6 = (bf16[32,2176]{1,0:T(8,128)(2,1)S(1)}, bf16[32,2176]{1,0:T(8,128)(2,1)S(1)}, u32[]{:S(2)}, u32[]{:S(2)}) collective-permute-start(bf16[32,2176]{1,0:T(8,128)(2,1)S(1)} %place.1.refs_0_), channel_id=1, source_target_pairs={{2,0},{0,2},{3,1},{1,3},{6,4},{4,6},{7,5},{5,7},{10,8},{8,10},{11,... | collective-permute-start | bytes 417800 | tf_op jit(solution)/shard_map/ppermute | solution.py:380
  20.3 0.0 collective-permute-start.5
  20.3 3.6 %collective-permute-done.6.refs_0_ = bf16[32,2176]{1,0:T(8,128)(2,1)S(1)} collective-permute-done((bf16[32,2176]{1,0:T(8,128)(2,1)S(1)}, bf16[32,2176]{1,0:T(8,128)(2,1)S(1)}, u32[]{:S(2)}, u32[]{:S(2)}) %collective-permute-start.6) | collective-permute-done | bytes 139296 | tf_op jit(solution)/shard_map/ppermute | solution.py:380
  23.9 0.8 %collective-permute-start.8 = (bf16[32,2176]{1,0:T(8,128)(2,1)S(1)}, bf16[32,2176]{1,0:T(8,128)(2,1)S(1)}, u32[]{:S(2)}, u32[]{:S(2)}) collective-permute-start(bf16[32,2176]{1,0:T(8,128)(2,1)S(1)} %get-tuple-element.77), channel_id=1, source_target_pairs={{1,4},{5,8},{9,12},{4,1},{8,5},{12,9},{3,6},{7,10},{11,14},{6,3},{... | collective-permute-start | bytes 417800 | tf_op jit(solution)/shard_map/ppermute | solution.py:485
  24.8 1.5 %collective-permute-start.7 = (bf16[32,2176]{1,0:T(8,128)(2,1)S(1)}, bf16[32,2176]{1,0:T(8,128)(2,1)S(1)}, u32[]{:S(2)}, u32[]{:S(2)}) collective-permute-start(bf16[32,2176]{1,0:T(8,128)(2,1)S(1)} %get-tuple-element.78), channel_id=1, source_target_pairs={{0,1},{1,0},{2,3},{3,2},{4,5},{5,4},{6,7},{7,6},{8,9},{9,8},{10,11... | collective-permute-start | bytes 417800 | tf_op jit(solution)/shard_map/ppermute | solution.py:483
  26.3 0.0 collective-permute-done.5.refs_3_
  26.3 0.0 copy-done
  26.3 0.0 copy-done.2
  26.3 0.0 copy-done.1
  26.3 2.2 %own.1 = (bf16[1,144,768]{2,1,0:T(8,128)(2,1)S(1)}, bf16[1,144,768]{2,1,0:T(8,128)(2,1)S(1)}, bf16[1,144,768]{2,1,0:T(8,128)(2,1)S(1)}, bf16[512,1536]{1,0:T(8,1...) custom-call(bf16[32,2176]{1,0:T(8,128)(2,1)S(1)} %place.1.refs_0_, bf16[512,768]{1,0:T(8,128)(2,1)S(1)} %copy-done, ...), custom_call_target="tpu_custom_call" | custom-call | flops 2147483648 | bytes 9437184 | tf_op jit(solution)/shard_map/own/pallas_call | solution.py:490
  28.5 2.2 %others.1 = (bf16[1,144,768]{2,1,0:T(8,128)(2,1)S(1)}, bf16[1,144,768]{2,1,0:T(8,128)(2,1)S(1)}, bf16[1,144,768]{2,1,0:T(8,128)(2,1)S(1)}) custom-call(bf16[32,2176]{1,0:T(8,128)(2,1)S(1)} %collective-permute-done.6.refs_0_, bf16[512,1536]{1,0:T(8,128)(2,1)S(1)} %get-tuple-element.64.refs_1_.refs_7_.refs_5_, ...), custom_call_target="tpu_custom_call" | custom-call | flops 2147483648 | bytes 9437184 | tf_op jit(solution)/shard_map/others/pallas_call | solution.py:506
  30.7 0.0 collective-permute-done.7.refs_6_
  30.7 3.2 %inner.1 = (bf16[1,144,768]{2,1,0:T(8,128)(2,1)S(1)}, bf16[4,144,768]{2,1,0:T(8,128)(2,1)S(1)}, bf16[4,144,768]{2,1,0:T(8,128)(2,1)S(1)}, bf16[2,144,768]{2,1,0:T(8,128)(2,1)S(1)}) custom-call(bf16[1,144,768]{2,1,0:T(8,128)(2,1)S(1)} %get-tuple-element.61.refs_0_, bf16[1,144,768]{2,1,0:T(8,128)(2,1)S(1)} %get-tuple-element.62.refs_1_, ...), custom_call_target="tpu_custom_call" | custom-call | flops 4294967296 | bytes 9437184 | tf_op jit(solution)/shard_map/inner/pallas_call | solution.py:516
  33.9 0.0 collective-permute-done.8.refs_4_
  33.9 3.8 %outer.1 = bf16[272,768]{1,0:T(8,128)(2,1)} custom-call(bf16[1,144,768]{2,1,0:T(8,128)(2,1)S(1)} %get-tuple-element.72.refs_0_, bf16[4,144,768]{2,1,0:T(8,128)(2,1)S(1)} %get-tuple-element.73.refs_1_, bf16[4,144,768]{2,1,0:T(8,128)(2,1)S(1)} %get-tuple-element.74.refs_2_, bf16[2,144,768]{2,1,0:T(8,128)(2,1)S(1)} %get-tuple-element.75.refs_3_, ...), custom_call_target="tpu_custom_call" | custom-call | tf_op jit(solution)/shard_map/outer/pallas_call | solution.py:531
  (1 shorter events, 0.0 us)
Async XLA Ops:
  0.0 26.3 %copy-start = (bf16[512,768]{1,0:T(8,128)(2,1)S(1)}, bf16[512,768]{1,0:T(8,128)(2,1)}, u32[]{:S(2)}) copy-start(bf16[512,768]{1,0:T(8,128)(2,1)} %refs_1_.1) | copy-start | bytes 2359300
  0.0 26.3 %copy-start.2 = (bf16[768]{0:T(1024)(128)(2,1)S(1)}, bf16[768]{0:T(1024)(128)(2,1)}, u32[]{:S(2)}) copy-start(bf16[768]{0:T(1024)(128)(2,1)} %param.14) | copy-start | bytes 4612
  0.0 26.3 %copy-start.1 = (f32[1536]{0:T(1024)S(1)}, f32[1536]{0:T(1024)}, u32[]{:S(2)}) copy-start(f32[1536]{0:T(1024)} %param.15) | copy-start | bytes 18436
  4.6 13.9 %collective-permute-start.3 = (bf16[256,768]{1,0:T(8,128)(2,1)S(1)}, bf16[256,768]{1,0:T(8,128)(2,1)S(1)}, u32[]{:S(2)}, u32[]{:S(2)}) collective-permute-start(bf16[256,768]{1,0:T(8,128)(2,1)S(1)} %get-tuple-element.45), channel_id=1, source_target_pairs={{2,0},{0,2},{3,1},{1,3},{6,4},{4,6},{7,5},{5,7},{10,8},{8,10},{11,... | collective-permute-start | bytes 1179656 | tf_op jit(solution)/shard_map/ppermute | solution.py:380
  7.6 9.2 %collective-permute-start.4 = (bf16[768]{0:T(1024)(128)(2,1)}, bf16[768]{0:T(1024)(128)(2,1)S(1)}, u32[]{:S(2)}, u32[]{:S(2)}) collective-permute-start(bf16[768]{0:T(1024)(128)(2,1)} %param.14), channel_id=1, source_target_pairs={{2,0},{0,2},{3,1},{1,3},{6,4},{4,6},{7,5},{5,7},{10,8},{8,10},{11,... | collective-permute-start | bytes 4616 | tf_op jit(solution)/shard_map/ppermute | solution.py:380
  7.7 9.1 %collective-permute-start = (bf16[16,2304]{1,0:T(8,128)(2,1)S(1)}, bf16[16,2304]{1,0:T(8,128)(2,1)S(1)}, u32[]{:S(2)}, u32[]{:S(2)}) collective-permute-start(bf16[16,2304]{1,0:T(8,128)(2,1)S(1)} %get-tuple-element.42), channel_id=1, source_target_pairs={{0,4},{4,0},{8,12},{12,8},{1,5},{5,1},{9,13},{13,9},{2,6},{6,2},{1... | collective-permute-start | bytes 221192 | tf_op jit(solution)/shard_map/ppermute | solution.py:421
  9.7 7.2 %collective-permute-start.1 = (bf16[16,2304]{1,0:T(8,128)(2,1)S(1)}, bf16[16,2304]{1,0:T(8,128)(2,1)S(1)}, u32[]{:S(2)}, u32[]{:S(2)}) collective-permute-start(bf16[16,2304]{1,0:T(8,128)(2,1)S(1)} %get-tuple-element.43), channel_id=1, source_target_pairs={{0,8},{4,12},{8,0},{12,4},{1,9},{5,13},{9,1},{13,5},{2,10},{6,14},... | collective-permute-start | bytes 221192 | tf_op jit(solution)/shard_map/ppermute | solution.py:421
  12.3 6.2 %collective-permute-start.2 = (bf16[16,2304]{1,0:T(8,128)(2,1)S(1)}, bf16[16,2304]{1,0:T(8,128)(2,1)S(1)}, u32[]{:S(2)}, u32[]{:S(2)}) collective-permute-start(bf16[16,2304]{1,0:T(8,128)(2,1)S(1)} %get-tuple-element.44), channel_id=1, source_target_pairs={{0,12},{4,8},{8,4},{12,0},{1,13},{5,9},{9,5},{13,1},{2,14},{6,10},... | collective-permute-start | bytes 221192 | tf_op jit(solution)/shard_map/ppermute | solution.py:421
  18.7 5.1 %collective-permute-start.6 = (bf16[32,2176]{1,0:T(8,128)(2,1)S(1)}, bf16[32,2176]{1,0:T(8,128)(2,1)S(1)}, u32[]{:S(2)}, u32[]{:S(2)}) collective-permute-start(bf16[32,2176]{1,0:T(8,128)(2,1)S(1)} %place.1.refs_0_), channel_id=1, source_target_pairs={{2,0},{0,2},{3,1},{1,3},{6,4},{4,6},{7,5},{5,7},{10,8},{8,10},{11,... | collective-permute-start | bytes 417800 | tf_op jit(solution)/shard_map/ppermute | solution.py:380
  20.3 6.0 %collective-permute-start.5 = (bf16[256,768]{1,0:T(8,128)(2,1)S(1)}, bf16[256,768]{1,0:T(8,128)(2,1)S(1)}, u32[]{:S(2)}, u32[]{:S(2)}) collective-permute-start(bf16[256,768]{1,0:T(8,128)(2,1)S(1)} %collective-permute-done.3.refs_2_), channel_id=1, source_target_pairs={{0,1},{1,0},{2,3},{3,2},{4,5},{5,4},{6,7},{7,6},{8,9},{9,8},{10,11... | collective-permute-start | bytes 1179656 | tf_op jit(solution)/shard_map/ppermute | solution.py:467
  23.9 10.0 %collective-permute-start.8 = (bf16[32,2176]{1,0:T(8,128)(2,1)S(1)}, bf16[32,2176]{1,0:T(8,128)(2,1)S(1)}, u32[]{:S(2)}, u32[]{:S(2)}) collective-permute-start(bf16[32,2176]{1,0:T(8,128)(2,1)S(1)} %get-tuple-element.77), channel_id=1, source_target_pairs={{1,4},{5,8},{9,12},{4,1},{8,5},{12,9},{3,6},{7,10},{11,14},{6,3},{... | collective-permute-start | bytes 417800 | tf_op jit(solution)/shard_map/ppermute | solution.py:485
  24.8 5.9 %collective-permute-start.7 = (bf16[32,2176]{1,0:T(8,128)(2,1)S(1)}, bf16[32,2176]{1,0:T(8,128)(2,1)S(1)}, u32[]{:S(2)}, u32[]{:S(2)}) collective-permute-start(bf16[32,2176]{1,0:T(8,128)(2,1)S(1)} %get-tuple-element.78), channel_id=1, source_target_pairs={{0,1},{1,0},{2,3},{3,2},{4,5},{5,4},{6,7},{7,6},{8,9},{9,8},{10,11... | collective-permute-start | bytes 417800 | tf_op jit(solution)/shard_map/ppermute | solution.py:483

commit v2 on v1

v2 whole, which is shorter than its diff:
```python
import functools
import math

import jax
import jax.numpy as jnp
import ml_dtypes
import numpy as np
from jax import lax
from jax.experimental import pallas as pl
from jax.experimental.pallas import tpu as pltpu
from jax.sharding import PartitionSpec as P

HDIM = 64
MEL = 128
NFFT = 512
HOP = 160
FP = 17
CH = 136
PE = 32

SAMPLE_RATE = 16000.0
EPSILON = 1e-05
MASKED = -1e30

LANES = 128
PIECE_BITS = 5
ROWS = 144
GROUP = 4
STACK = 4
MEL_WIDTH = FP * MEL
BF16 = jnp.bfloat16
F32 = jnp.float32


def split_bf16(values):
    high = values.astype(ml_dtypes.bfloat16)
    low = (values - high.astype(np.float64)).astype(ml_dtypes.bfloat16)
    return np.stack([high, low])


def fourier_tables():
    n, bins = np.arange(NFFT // 2)[:, None], NFFT // 2

    def phase(k):
        return 2.0 * np.pi * ((n * k[None, :]) % NFFT) / NFFT

    even, odd = np.arange(0, bins, 2), np.arange(1, bins, 2)
    sine = np.sin(phase(even))
    sine[:, 0] = np.cos(phase(np.array([bins])))[:, 0]
    return np.stack(
        [
            split_bf16(np.concatenate([np.cos(phase(even)), sine], axis=1)),
            split_bf16(np.concatenate([np.cos(phase(odd)), np.sin(phase(odd))], axis=1)),
        ]
    )


def window_halves():
    window = 0.5 - 0.5 * np.cos(2.0 * np.pi * np.arange(NFFT) / NFFT)
    return window.reshape(2, NFFT // 2).astype(np.float32)


def mel_tables():
    bins = NFFT // 2
    highest = 2595.0 * math.log10(1.0 + SAMPLE_RATE / 2.0 / 700.0)
    points = np.arange(MEL + 2) * (highest / (MEL + 1))
    hertz = 700.0 * (10.0 ** (points / 2595.0) - 1.0)
    centres = np.arange(bins + 1) * (SAMPLE_RATE / NFFT)
    rising = (centres[:, None] - hertz[None, :-2]) / (hertz[1:-1] - hertz[:-2])[None, :]
    falling = (hertz[None, 2:] - centres[:, None]) / (hertz[2:] - hertz[1:-1])[None, :]
    filters = np.maximum(0.0, np.minimum(rising, falling))
    filters = [filters[0:bins:2], filters[1:bins:2], filters[bins:], np.zeros((15, MEL))]
    high, low = split_bf16(np.concatenate(filters, axis=0))
    return np.concatenate([high, low], axis=1)


def dot(a, b):
    return jnp.dot(a, b, preferred_element_type=F32)


def iota(shape, dim):
    return lax.broadcasted_iota(jnp.int32, shape, dim)


def mel_kernel(shards, capacity, relative, *refs):
    sources, outs = refs[:5], refs[5:-6]
    targets, sems = refs[-6:-1], refs[-1]
    x_ref, target_ref, window_ref, fourier_ref, mel_ref = targets
    slots = x_ref.shape[0]
    pairs = zip(sources, targets)
    copies = [pltpu.make_async_copy(*pair, sems.at[k]) for k, pair in enumerate(pairs)]
    for copy in copies:
        copy.start()
    copies[1].wait()
    target = target_ref[...]
    owner = lax.shift_right_arithmetic(target, PIECE_BITS)
    place = jnp.where(target < 0, 0, (target & (PE - 1)) + 1).astype(F32)
    row, col = iota((slots, slots), 0), iota((slots, slots), 1)
    diagonal = row == col
    owner_col = jnp.sum(jnp.where(diagonal, owner, 0), axis=1, keepdims=True)
    place_col = jnp.sum(jnp.where(diagonal, place, 0.0), axis=1, keepdims=True)
    rank = jnp.sum(((owner_col == owner) & (row < col)).astype(jnp.int32), axis=0, keepdims=True)
    chosen = row // capacity
    if relative:
        chosen = chosen ^ lax.axis_index("seq")
    pick = ((chosen == owner) & (row % capacity == rank)).astype(F32).astype(BF16)
    marks = jnp.broadcast_to(place_col, (slots, LANES)).astype(BF16)

    copies[0].wait()
    copies[2].wait()
    x = x_ref[...]
    frames = [None] * FP
    half, bins = NFFT // 2, NFFT // 4
    rising, falling = window_ref[0:1, :], window_ref[1:2, :]
    later = iota((1, bins), 1) > 0
    for phase in range(4):
        shift = phase * (HOP % LANES)
        moved = x if phase == 0 else pltpu.roll(x, x.shape[1] - shift, 1)
        members = list(range(phase, FP, 4))
        sums, differences = [], []
        for f in members:
            start = HOP * f - shift
            left = moved[:, start : start + half] * rising
            right = moved[:, start + half : start + NFFT] * falling
            sums.append(left + right)
            differences.append(left - right)
        squares = []
        for k, parts in enumerate((sums, differences)):
            values = jnp.concatenate(parts, axis=0)
            high = values.astype(BF16)
            low = (values - high.astype(F32)).astype(BF16)
            if phase == 0 and k == 0:
                copies[3].wait()
            table_high, table_low = fourier_ref[k, 0], fourier_ref[k, 1]
            spectra = dot(
                jnp.concatenate([high, low, high], axis=1),
                jnp.concatenate([table_high, table_high, table_low], axis=0),
            )
            squares.append(spectra * spectra)
        if phase == 0:
            copies[4].wait()
            filters = mel_ref[:half, :]
            last_row = mel_ref[half:, :].astype(F32)
            last_row = last_row[:1, :MEL] + last_row[:1, MEL:]
        even, odd = squares
        last = even[:, bins : bins + 1] * last_row
        even = even[:, :bins] + jnp.where(later, even[:, bins:], 0.0)
        power = jnp.concatenate([even, odd[:, :bins] + odd[:, bins:]], axis=1)
        power_high = power.astype(BF16)
        power_low = (power - power_high.astype(F32)).astype(BF16)
        both = dot(
            jnp.concatenate([power_high, power_low], axis=1),
            jnp.concatenate([filters, filters], axis=0),
        )
        energy = both[:, :MEL] + both[:, MEL:] + last
        log_mel = jnp.log(1.0 + energy).astype(BF16)
        for k, f in enumerate(members):
            frames[f] = log_mel[k * slots : (k + 1) * slots]
    packed = dot(pick, jnp.concatenate(frames + [marks], axis=1)).astype(BF16)
    count = slots // len(outs)
    for d, out in enumerate(outs):
        out[...] = packed[d * count : (d + 1) * count]


def place_kernel(*refs):
    parts, out = refs[:-1], refs[-1]
    rows = jnp.concatenate([part[...] for part in parts], axis=0)
    slots = rows.shape[0]
    mark = rows[:, MEL_WIDTH : MEL_WIDTH + LANES].astype(F32)[:, :1]
    row, col = iota((slots, slots), 0), iota((slots, slots), 1)
    mark = jnp.sum(jnp.where(row == col, mark, 0.0), axis=0, keepdims=True)
    at = iota((PE, slots), 0)
    groups = PE // GROUP
    wanted = (at % groups) * GROUP + at // groups + 1
    pick = (wanted.astype(F32) == mark).astype(F32).astype(BF16)
    out[...] = dot(pick, rows[:, :MEL_WIDTH]).astype(BF16)


def token_rows(pieces):
    groups = PE // GROUP
    pieces = pieces.astype(F32)
    rows = []
    for i in range(FP):
        cells = []
        for j in range(STACK):
            q, f = divmod(STACK * i + j, FP)
            cells.append(pieces[q * groups : (q + 1) * groups, f * MEL : (f + 1) * MEL])
        rows.append(jnp.concatenate(cells, axis=1))
    rows.append(jnp.zeros((ROWS - CH, STACK * MEL), F32))
    mixed = jnp.concatenate(rows, axis=0).astype(BF16)
    row, col = iota((ROWS, ROWS), 0), iota((ROWS, ROWS), 1)
    token = (col % groups) * FP + col // groups
    order = ((row == token) & (col < CH)).astype(F32).astype(BF16)
    return dot(order, mixed).astype(BF16)


def prepare_kernel(
    lengths_hbm, table_hbm, qkv_hbm, out_ref, qkv_ref, lengths_ref, table_ref, flipped, sems
):
    copies = [
        pltpu.make_async_copy(lengths_hbm, lengths_ref, sems.at[0]),
        pltpu.make_async_copy(table_hbm, table_ref, sems.at[1]),
        pltpu.make_async_copy(qkv_hbm, qkv_ref, sems.at[2]),
    ]
    for copy in copies:
        copy.start()
    copies[0].wait()
    copies[1].wait()
    pairs, blocks = out_ref.shape[:2]
    half = blocks * CH
    first = (lax.axis_index("seq") * lax.axis_size("sub") + lax.axis_index("sub")) * half
    total = lax.axis_size("seq") * lax.axis_size("sub") * half
    lane, row = iota((1, 3 * ROWS), 1), iota((ROWS, 1), 0)
    orders = ((0, 1, 2), (2, 0, 1))
    slot = lane // ROWS
    key_place = lane - slot * ROWS
    masks = []
    for c in range(blocks):
        order = orders[1 if c == blocks - 1 else 0]
        key_block = jnp.where(slot == 0, order[0], jnp.where(slot == 1, order[1], order[2]))
        query = first + c * CH + row
        key = first + (c - 1) * CH + key_block * CH + key_place
        query_utt, key_utt = jnp.zeros_like(query), jnp.zeros_like(key)
        end = jnp.int32(0)
        for r in range(lengths_ref.shape[0]):
            end = end + lengths_ref[r]
            query_utt = query_utt + (query >= end).astype(jnp.int32)
            key_utt = key_utt + (key >= end).astype(jnp.int32)
        inside = (key >= 0) & (key < total) & (key_place < CH)
        key_utt = jnp.where(inside, key_utt, -1)
        masks.append(jnp.where(query_utt == key_utt, 0.0, MASKED))
    heads, entries = table_ref.shape
    width = flipped.shape[1]
    mirror = iota((entries, width), 0) + iota((entries, width), 1) == entries - 1
    mirror = mirror.astype(F32).astype(BF16)
    rest, lines = table_ref[...], 0.0
    for _ in range(3):
        part = rest.astype(BF16)
        rest = rest - part.astype(F32)
        lines = lines + dot(part, mirror)
    flipped[...] = lines

    def one_head(head, side):
        line = jnp.broadcast_to(flipped[pl.ds(head, 1), :], (ROWS, width))
        biases = []
        for order in orders:
            turned = [
                pltpu.roll(
                    line, (ROWS * at - CH * b - (CH - 1)) % width, 1, stride=1, stride_axis=0
                )[:, : 3 * ROWS]
                for at, b in enumerate(order)
            ]
            biases.append(
                jnp.where(slot == 0, turned[0], jnp.where(slot == 1, turned[1], turned[2]))
            )
        for c in range(blocks):
            bias = biases[1 if c == blocks - 1 else 0]
            out_ref[head // 2, c, side * ROWS : (side + 1) * ROWS, :] = bias + masks[c]

    @pl.loop(0, pairs)
    def _(pair):
        one_head(2 * pair, 0)
        one_head(2 * pair + 1, 1)

    copies[2].wait()


def normalize(tokens, conv, conv_bias, gain, out):
    summed = dot(tokens, conv[...]) + conv_bias[...]
    features = (summed / (1.0 + jnp.exp(-summed))).astype(BF16).astype(F32)
    scale = 1.0 / features.shape[1]
    centred = features - jnp.sum(features, axis=1, keepdims=True) * scale
    variance = jnp.sum(centred * centred, axis=1, keepdims=True) * scale
    out[...] = (centred * lax.rsqrt(variance + EPSILON) * gain[...]).astype(BF16)


def half_kernel(n, *refs):
    pieces, parts, bias_parts = refs[:n], refs[n : 3 * n - 1], refs[3 * n - 1 : 4 * n - 1]
    gain_rows, qkv, *outs, sent, conv, conv_bias, gain, normed = refs[4 * n - 1 :]
    me, core = lax.axis_index("head"), lax.axis_index("sub")
    depth = parts[0].shape[1]
    for d in range(n):
        start = pl.multiple_of(lax.rem(me + d, n) * depth, depth)
        at = pl.ds(start, depth)
        lines = bias_parts[d][...].astype(F32)
        for k in range(depth // LANES):
            conv_bias[:, pl.ds(start + k * LANES, LANES)] = lines[k : k + 1]
        if d == 0:
            conv[:, at] = parts[0][...]
        else:
            got, passed = parts[2 * d - 1 : 2 * d + 1]

            @pl.when(core == 0)
            def _(got=got, at=at):
                conv[:, at] = got[...]

            @pl.when(core == 1)
            def _(passed=passed, at=at):
                conv[:, at] = passed[...]

    for k in range(gain_rows.shape[0]):
        gain[:, k * LANES : (k + 1) * LANES] = gain_rows[k : k + 1, :]
    tokens = jnp.concatenate([token_rows(piece[...]) for piece in pieces], axis=0)
    normalize(tokens, conv, conv_bias, gain, normed)
    wanted = jnp.where(core == 0, n - 1, 0)
    for p, out in enumerate(outs):
        got = dot(normed[...], qkv[p]).astype(BF16)
        for d in range(n):
            out[lax.rem(me + d, n)] = got[d * ROWS : (d + 1) * ROWS]
        if p > 0:
            sent[p - 1] = out[wanted]


def attend(q, k, v, bias):
    low_lanes = iota((ROWS, LANES), 1) < HDIM
    q = q * jnp.asarray(1.0 / math.sqrt(HDIM), BF16)
    zero = jnp.zeros_like(q)
    q = jnp.concatenate([jnp.where(low_lanes, q, zero), jnp.where(low_lanes, zero, q)], axis=0)
    scores = lax.dot_general(q, k, (((1,), (1,)), ((), ())), preferred_element_type=F32) + bias
    weights = jnp.exp(scores - jnp.max(scores, axis=1, keepdims=True)).astype(BF16)
    summed = dot(weights, jnp.concatenate([v, jnp.ones_like(v)], axis=1))
    context = summed[:, :LANES] * (1.0 / summed[:, LANES:])
    return jnp.where(low_lanes, context[:ROWS], context[ROWS:])


def edge_context(pair, block, halo_keys, halo_values, first, queries, keys, values, bias):
    at = slice(pair * LANES, (pair + 1) * LANES)
    return attend(
        queries[block, :, at],
        jnp.concatenate([halo_keys[:, at], keys[first, :, at], keys[first + 1, :, at]], axis=0),
        jnp.concatenate(
            [halo_values[:, at], values[first, :, at], values[first + 1, :, at]], axis=0
        ),
        bias[pair, block],
    )


def far_kernel(n, *refs):
    queries, keys, values, far, conv, conv_bias, gain, qkv, bias, out = refs[:10]
    normed, far_keys, far_values = refs[10:]
    core = lax.axis_index("sub")
    normalize(token_rows(far[...]), conv, conv_bias, gain, normed)
    far_keys[...] = dot(normed[...], qkv[1]).astype(BF16)
    far_values[...] = dot(normed[...], qkv[2]).astype(BF16)
    block, first = jnp.where(core == 0, 0, n - 1), jnp.where(core == 0, 0, n - 2)
    for pair in range(qkv.shape[2] // LANES):
        context = edge_context(
            pair, block, far_keys, far_values, first, queries, keys, values, bias
        )
        out[:, pair * LANES : (pair + 1) * LANES] = context.astype(BF16)


def near_kernel(n, *refs):
    queries, keys, values, near, far_context, bias, out = refs
    core = lax.axis_index("sub")
    block, first = jnp.where(core == 0, n - 1, 0), jnp.where(core == 0, n - 2, 0)
    for pair in range(queries.shape[2] // LANES):
        at = slice(pair * LANES, (pair + 1) * LANES)
        context = edge_context(
            pair, block, near.at[0], near.at[1], first, queries, keys, values, bias
        )[:CH]
        middle = [
            attend(
                queries[c, :, at],
                keys[c - 1 : c + 2, :, at].reshape(3 * ROWS, LANES),
                values[c - 1 : c + 2, :, at].reshape(3 * ROWS, LANES),
                bias[pair, c],
            )[:CH]
            for c in range(1, n - 1)
        ]
        other = far_context[:, at].astype(F32)[:CH]
        out[:, at] = jnp.where(
            core == 0,
            jnp.concatenate([other] + middle + [context], axis=0),
            jnp.concatenate([context] + middle + [other], axis=0),
        ).astype(BF16)


def vmem(count):
    return [pl.BlockSpec(memory_space=pltpu.VMEM)] * count


def from_hbm(array):
    return pltpu.with_memory_space_constraint(array, pltpu.HBM)


def in_vmem(array):
    return pltpu.with_memory_space_constraint(array, pltpu.VMEM)


def from_heads(block, n):
    return [lax.ppermute(block, "head", [((i + d) % n, i) for i in range(n)]) for d in range(1, n)]


def local(
    wave_pieces, piece_target, utt_lengths, sub_weight, sub_bias, norm_gain, qkv_weight, rel_bias
):
    shards, n, cores = lax.axis_size("seq"), lax.axis_size("head"), lax.axis_size("sub")
    assert cores == 2
    slots, length = wave_pieces.shape[3:]
    capacity = slots // shards
    relative = shards in (2, 4) and capacity % 16 == 0
    outs = shards if relative else 1
    payload = MEL_WIDTH + LANES
    fourier, filters, window = fourier_tables(), mel_tables(), window_halves()
    in_hbm = pl.BlockSpec(memory_space=pltpu.HBM)
    groups = lax.axis_size("groups")
    weight_got = []
    for d in range(1, n):
        links = []
        for g in range(groups):
            for h in range(n):
                at = (g * n + h) * cores
                links.append(((g * n + (h + d) % n) * cores, at))
                links.append((((g + 1) % groups * n + h) * cores + 1, at + 1))
        weight_got.append(lax.ppermute(sub_weight, ("groups", "head", "sub"), links))
    packed = pl.pallas_call(
        functools.partial(mel_kernel, shards, capacity, relative),
        out_shape=[jax.ShapeDtypeStruct((slots // outs, payload), BF16)] * outs,
        in_specs=[in_hbm] * 5,
        out_specs=vmem(outs),
        scratch_shapes=[
            pltpu.VMEM((slots, length), F32),
            pltpu.VMEM((1, slots), jnp.int32),
            pltpu.VMEM(window.shape, F32),
            pltpu.VMEM(fourier.shape, BF16),
            pltpu.VMEM(filters.shape, BF16),
            pltpu.SemaphoreType.DMA((5,)),
        ],
        compiler_params=pltpu.CompilerParams(vmem_limit_bytes=24 << 20),
        name="log_mel",
    )(
        from_hbm(wave_pieces.reshape(slots, length)),
        from_hbm(piece_target.reshape(1, slots)),
        from_hbm(jnp.asarray(window)),
        from_hbm(jnp.asarray(fourier)),
        from_hbm(jnp.asarray(filters)),
    )
    if relative:
        received = [
            lax.ppermute(packed[d], "seq", [(i, i ^ d) for i in range(shards)])
            for d in range(shards - 1, 0, -1)
        ] + [packed[0]]
    else:
        blocks = packed[0].reshape(shards, capacity, payload)
        blocks = lax.all_to_all(blocks, "seq", split_axis=0, concat_axis=0, tiled=True)
        received = [blocks.reshape(slots, payload)]

    local_width = qkv_weight.shape[2]
    pairs = local_width // LANES
    gain = norm_gain.reshape(-1, LANES)
    me, core = lax.axis_index("head"), lax.axis_index("sub")
    last, first = lax.rem(n - 1 - me + n, n), lax.rem(n - me, n)
    far_at = jnp.where(core == 0, first, last)
    far_is = [far_at == d for d in range(n)]
    rel_bias, gain, far_is, _ = lax.optimization_barrier(
        (rel_bias, gain, far_is, packed[0])
    )
    entries = rel_bias.shape[1]
    qkv = jnp.transpose(qkv_weight, (1, 0, 2))
    bias, qkv = pl.pallas_call(
        prepare_kernel,
        out_shape=[
            pltpu.VMEM((pairs, n, 2 * ROWS, 3 * ROWS), F32),
            pltpu.VMEM(qkv.shape, BF16),
        ],
        in_specs=[in_hbm] * 3,
        out_specs=vmem(2),
        scratch_shapes=[
            pltpu.SMEM(utt_lengths.shape, jnp.int32),
            pltpu.VMEM(rel_bias.shape, F32),
            pltpu.VMEM((2 * pairs, entries + -entries % LANES), F32),
            pltpu.SemaphoreType.DMA((3,)),
        ],
        compiler_params=pltpu.CompilerParams(vmem_limit_bytes=8 << 20),
        cost_estimate=pl.CostEstimate(flops=1 << 31, bytes_accessed=8 << 20, transcendentals=0),
        name="prepare",
    )(from_hbm(utt_lengths), from_hbm(rel_bias), from_hbm(qkv))
    received, weight_got, bias, qkv, gain, far_is = lax.optimization_barrier(
        (received, weight_got, bias, qkv, gain, far_is)
    )
    own = pl.pallas_call(
        place_kernel,
        out_shape=jax.ShapeDtypeStruct((PE, MEL_WIDTH), BF16),
        in_specs=vmem(len(received)),
        out_specs=vmem(1)[0],
        compiler_params=pltpu.CompilerParams(vmem_limit_bytes=8 << 20),
        name="place",
    )(*received)
    bias_sent, _ = lax.optimization_barrier((sub_bias, own))
    bias_lines = [part.reshape(-1, LANES) for part in [sub_bias] + from_heads(bias_sent, n)]
    conv = [sub_weight]
    for got in weight_got:
        got, _ = lax.optimization_barrier((got, own))
        conv += [got, lax.ppermute(got, "sub", [(0, 1), (1, 0)])]

    others = from_heads(own, n)
    width = qkv_weight.shape[0]
    qkv = in_vmem(qkv)
    limit = pltpu.CompilerParams(vmem_limit_bytes=16 << 20)
    far_sent = own
    for d in range(1, n):
        far_sent = jnp.where(far_is[d], others[d - 1], far_sent)
    links = []
    for h in range(n):
        for k in range(shards - 1):
            above, below = ((k + 1) * n + h) * cores, (k * n + h) * cores + 1
            links += [(above, below), (below, above)]
        links.append((h * cores, (h + 1) % n * cores))
        ends = (shards - 1) * n
        links.append(((ends + h) * cores + 1, (ends + (h + 1) % n) * cores + 1))
    far = lax.ppermute(far_sent, ("seq", "head", "sub"), links)
    *half_qkv, near_sent, whole, whole_bias, whole_gain = pl.pallas_call(
        functools.partial(half_kernel, n),
        out_shape=[jax.ShapeDtypeStruct((n, ROWS, local_width), BF16)] * 3
        + [
            jax.ShapeDtypeStruct((2, ROWS, local_width), BF16),
            jax.ShapeDtypeStruct((sub_weight.shape[0], width), BF16),
            jax.ShapeDtypeStruct((1, width), F32),
            jax.ShapeDtypeStruct((1, width), F32),
        ],
        in_specs=vmem(n + len(conv) + n + 2),
        out_specs=vmem(7),
        scratch_shapes=[pltpu.VMEM((n * ROWS, width), BF16)],
        compiler_params=limit,
        cost_estimate=pl.CostEstimate(flops=4 << 30, bytes_accessed=9 << 20, transcendentals=0),
        name="half",
    )(own, *others, *conv, *bias_lines, gain, qkv)
    weights = (whole, whole_bias, whole_gain, qkv)
    near = lax.ppermute(near_sent, "sub", [(0, 1), (1, 0)])
    far_context = pl.pallas_call(
        functools.partial(far_kernel, n),
        out_shape=jax.ShapeDtypeStruct((ROWS, local_width), BF16),
        in_specs=vmem(4 + len(weights) + 1),
        out_specs=vmem(1)[0],
        scratch_shapes=[
            pltpu.VMEM((ROWS, width), BF16),
            pltpu.VMEM((ROWS, local_width), BF16),
            pltpu.VMEM((ROWS, local_width), BF16),
        ],
        compiler_params=limit,
        cost_estimate=pl.CostEstimate(flops=16 << 30, bytes_accessed=9 << 20, transcendentals=0),
        name="far",
    )(*half_qkv, far, *weights, in_vmem(bias))
    return pl.pallas_call(
        functools.partial(near_kernel, n),
        out_shape=jax.ShapeDtypeStruct((n * CH, local_width), BF16),
        in_specs=vmem(6),
        out_specs=vmem(1)[0],
        compiler_params=limit,
        name="near",
    )(*half_qkv, near, far_context, in_vmem(bias))


def solution(mesh):
    placed = (
        P(("groups", "seq"), "head", "sub", None, None),
        P(("groups", "seq"), "head", "sub", None),
        P("groups"),
        P(None, "head"),
        P("head"),
        P(),
        P(None, None, "head"),
        P("head", None),
    )
    return jax.shard_map(
        local,
        mesh=mesh,
        in_specs=placed,
        out_specs=P(("groups", "seq", "sub"), "head"),
        check_vma=False,
    )
```

time: 37.9 us -> 32.9 us (0.87)
  Pallas kernels: 19.2 us -> 16.1 us
  waiting for transfers between devices: 6.72 us -> 5.62 us
  starting transfers between devices: 11.6 us -> 10.9 us
    ppermute x1 -> x2, starting transfers between devices: 0.85 us -> 4.3 us  [the longest x1 3.01 us: local(): lax.ppermute(sub_weight, ('groups', 'head', 'sub'), links)]
    ppermute x3 -> x2, starting transfers between devices: 4.64 us -> 2.09 us  [from_heads(): lax.ppermute(block, 'head', [((i + d) % n, i) for i in range(n)])]
    pallas_call x4 -> x3, Pallas kernels: 11.4 us -> 9.26 us  [the longest x1 4.08 us: local(): pl.pallas_call(functools.partial(half_kernel, n), out_shape=[jax.ShapeDty...]
    ppermute x1, starting transfers between devices: 1.5 us -> 0.06 us  [local(): near = lax.ppermute(near_sent, 'sub', [(0, 1), (1, 0)])]
    ppermute x3 -> x2, waiting for transfers between devices: 4.95 us -> 3.55 us  [from_heads(): lax.ppermute(block, 'head', [((i + d) % n, i) for i in range(n)])]
    pallas_call x1, Pallas kernels: 4.55 us -> 3.46 us  [local(): pl.pallas_call(functools.partial(mel_kernel, shards, capacity, relative),...]
  transfers between devices with their start and end apart: 9 -> 9, of which waited for: 4 -> 2; matrix products, arithmetic and copies ran while one was open for 0% -> 0% of each run, Pallas kernels for 28% -> 42%
where the time goes in v2:
time: 32.9 us; the launch traced here: 32.7 us
  Pallas kernels  16.1 us (49%)
  starting transfers between devices  10.9 us (33%)
  waiting for transfers between devices  5.62 us (17%)
    ppermute x3, starting transfers between devices, local(): lax.ppermute(packed[d], 'seq', [(i, i ^ d) for i in range(shards)])  4.45 us
    pallas_call x1, Pallas kernels, local(): pl.pallas_call(functools.partial(half_kernel, n), out_shape=[jax.ShapeDty...  4.08 us
    ppermute x2, waiting for transfers between devices, from_heads(): lax.ppermute(block, 'head', [((i + d) % n, i) for i in range(n)])  3.55 us
    pallas_call x1, Pallas kernels, local(): pl.pallas_call(functools.partial(mel_kernel, shards, capacity, relative),...  3.46 us
    pallas_call x1, Pallas kernels, local(): pl.pallas_call(prepare_kernel, out_shape=[pltpu.VMEM((pairs, n, 2 * ROWS,...  3.1 us
    ppermute x1, starting transfers between devices, local(): lax.ppermute(sub_weight, ('groups', 'head', 'sub'), links)  3.01 us
    pallas_call x1, Pallas kernels, local(): pl.pallas_call(functools.partial(far_kernel, n), out_shape=jax.ShapeDtype...  2.97 us
    pallas_call x1, Pallas kernels, local(): pl.pallas_call(functools.partial(near_kernel, n), out_shape=jax.ShapeDtyp...  2.21 us
  transfers between devices with their start and end apart: 9, of which 2 were waited for; matrix products, arithmetic and copies ran while one was open for 0% of the time, Pallas kernels for 42%

profile of v2, /device:TPU:0, one launch (start us, length us, event | category | flops | bytes accessed | tf_op | source)
XLA Modules:
  0.0 32.7 jit_solution(9506818782279245345)
XLA Ops:
  0.0 0.0 copy-start
  0.0 0.0 copy-start.1
  0.0 0.0 copy-start.2
  0.0 3.0 %collective-permute-start.3 = (bf16[512,768]{1,0:T(8,128)(2,1)}, bf16[512,768]{1,0:T(8,128)(2,1)S(1)}, u32[]{:S(2)}, u32[]{:S(2)}) collective-permute-start(bf16[512,768]{1,0:T(8,128)(2,1)} %refs_2_.2), channel_id=1, source_target_pairs={{2,0},{17,1},{0,2},{19,3},{18,16},{1,17},{16,18},{3,19},{6,4},{21,... | collective-permute-start | bytes 2359304 | tf_op jit(solution)/shard_map/ppermute | solution.py:416
  3.0 3.5 %log_mel.1 = (bf16[16,2304]{1,0:T(8,128)(2,1)S(1)}, bf16[16,2304]{1,0:T(8,128)(2,1)S(1)}, bf16[16,2304]{1,0:T(8,128)(2,1)S(1)}, bf16[16,2304]{1,0:T(8,128)(2,1)S(1)}) custom-call(f32[64,3072]{1,0:T(8,128)} %bitcast.9, s32[1,64]{1,0:T(1,128)} %bitcast.10, f32[2,256]{1,0:T(2,128)} %constant.24.clone.refs_2_, bf16[2,2,256,256]{3,2,1,0:T(8,128)(2,1)} %constant.25.clone.refs_3_, ...), custom_call_target="tpu_custom_call" | custom-call | tf_op jit(solution)/shard_map/log_mel/pallas_call | solution.py:417
  6.5 3.7 %collective-permute-start = (bf16[16,2304]{1,0:T(8,128)(2,1)S(1)}, bf16[16,2304]{1,0:T(8,128)(2,1)S(1)}, u32[]{:S(2)}, u32[]{:S(2)}) collective-permute-start(bf16[16,2304]{1,0:T(8,128)(2,1)S(1)} %get-tuple-element.32), channel_id=1, source_target_pairs={{0,12},{4,8},{8,4},{12,0},{1,13},{5,9},{9,5},{13,1},{2,14},{6,10},... | collective-permute-start | bytes 221192 | tf_op jit(solution)/shard_map/ppermute | solution.py:441
  10.2 0.0 collective-permute-start.1
  10.2 0.8 %collective-permute-start.2 = (bf16[16,2304]{1,0:T(8,128)(2,1)S(1)}, bf16[16,2304]{1,0:T(8,128)(2,1)S(1)}, u32[]{:S(2)}, u32[]{:S(2)}) collective-permute-start(bf16[16,2304]{1,0:T(8,128)(2,1)S(1)} %get-tuple-element.34), channel_id=1, source_target_pairs={{0,4},{4,0},{8,12},{12,8},{1,5},{5,1},{9,13},{13,9},{2,6},{6,2},{1... | collective-permute-start | bytes 221192 | tf_op jit(solution)/shard_map/ppermute | solution.py:441
  10.9 3.1 %prepare.1 = (f32[6,2,288,432]{3,2,1,0:T(8,128)S(1)}, bf16[3,1536,768]{2,1,0:T(8,128)(2,1)S(1)}) custom-call(s32[4]{0:T(128)} %lengths_hbm.1, f32[12,543]{1,0:T(8,128)} %table_hbm, bf16[3,1536,768]{2,1,0:T(8,128)(2,1)} %bitcast.11), custom_call_target="tpu_custom_call" | custom-call | flops 2147483648 | bytes 8388608 | tf_op jit(solution)/shard_map/prepare/pallas_call | solution.py:461
  14.0 0.0 collective-permute-done.refs_0_
  14.1 2.1 %collective-permute-done.1.refs_1_ = bf16[16,2304]{1,0:T(8,128)(2,1)S(1)} collective-permute-done((bf16[16,2304]{1,0:T(8,128)(2,1)S(1)}, bf16[16,2304]{1,0:T(8,128)(2,1)S(1)}, u32[]{:S(2)}, u32[]{:S(2)}) %collective-permute-start.1) | collective-permute-done | bytes 73760 | tf_op jit(solution)/shard_map/ppermute | solution.py:441
  16.1 0.0 collective-permute-done.2.refs_2_
  16.1 0.0 collective-permute-done.3.refs_3_
  16.1 0.3 place.1.refs_0_
  16.4 1.5 %collective-permute-start.4 = (bf16[32,2176]{1,0:T(8,128)(2,1)S(1)}, bf16[32,2176]{1,0:T(8,128)(2,1)S(1)}, u32[]{:S(2)}, u32[]{:S(2)}) collective-permute-start(bf16[32,2176]{1,0:T(8,128)(2,1)S(1)} %place.1.refs_0_), channel_id=1, source_target_pairs={{2,0},{0,2},{3,1},{1,3},{6,4},{4,6},{7,5},{5,7},{10,8},{8,10},{11,... | collective-permute-start | bytes 417800 | tf_op jit(solution)/shard_map/ppermute | solution.py:392
  17.9 0.0 collective-permute-start.5
  17.9 0.0 copy-done.2
  17.9 0.6 %collective-permute-start.6 = (bf16[768]{0:T(1024)(128)(2,1)S(1)}, bf16[768]{0:T(1024)(128)(2,1)S(1)}, u32[]{:S(2)}, u32[]{:S(2)}) collective-permute-start(bf16[768]{0:T(1024)(128)(2,1)S(1)} %copy-done.2), channel_id=1, source_target_pairs={{2,0},{0,2},{3,1},{1,3},{6,4},{4,6},{7,5},{5,7},{10,8},{8,10},{11,... | collective-permute-start | bytes 4616 | tf_op jit(solution)/shard_map/ppermute | solution.py:392
  18.5 3.5 %collective-permute-done.4.refs_1_ = bf16[32,2176]{1,0:T(8,128)(2,1)S(1)} collective-permute-done((bf16[32,2176]{1,0:T(8,128)(2,1)S(1)}, bf16[32,2176]{1,0:T(8,128)(2,1)S(1)}, u32[]{:S(2)}, u32[]{:S(2)}) %collective-permute-start.4) | collective-permute-done | bytes 139296 | tf_op jit(solution)/shard_map/ppermute | solution.py:392
  22.0 1.3 %collective-permute-start.8 = (bf16[32,2176]{1,0:T(8,128)(2,1)S(1)}, bf16[32,2176]{1,0:T(8,128)(2,1)S(1)}, u32[]{:S(2)}, u32[]{:S(2)}) collective-permute-start(bf16[32,2176]{1,0:T(8,128)(2,1)S(1)} %broadcast_select_fusion), channel_id=1, source_target_pairs={{4,1},{1,4},{8,5},{5,8},{12,9},{9,12},{0,2},{13,15},{6,3},{3,6},{1... | collective-permute-start | bytes 417800 | tf_op jit(solution)/shard_map/ppermute | solution.py:512
  23.3 0.0 collective-permute-done.6
  23.3 0.0 collective-permute-done.5.refs_4_
  23.3 0.0 copy-done
  23.3 0.0 copy-done.1
  23.4 4.1 %half.1 = (bf16[2,144,768]{2,1,0:T(8,128)(2,1)S(1)}, bf16[2,144,768]{2,1,0:T(8,128)(2,1)S(1)}, bf16[2,144,768]{2,1,0:T(8,128)(2,1)S(1)}, bf16[2,144,768]{2,1,0:T...) custom-call(bf16[32,2176]{1,0:T(8,128)(2,1)S(1)} %place.1.refs_0_, ...), custom_call_target="tpu_custom_call" | custom-call | flops 4294967296 | bytes 9437184 | tf_op jit(solution)/shard_map/half/pallas_call | solution.py:513
  27.4 0.1 collective-permute-start.7
  27.5 0.0 collective-permute-done.8.refs_3_
  27.5 3.0 %far.1.refs_4_ = bf16[144,768]{1,0:T(8,128)(2,1)S(1)} custom-call(bf16[2,144,768]{2,1,0:T(8,128)(2,1)S(1)} %get-tuple-element.50.refs_0_, bf16[2,144,768]{2,1,0:T(8,128)(2,1)S(1)} %get-tuple-element.51.refs_1_, bf16[2,144,768]{2,1,0:T(8,128)(2,1)S(1)} %get-tuple-element.52.refs_2_, bf16[32,2176]{1,0:T(8,128)(2,1)S(1)} %collective-permute-done.8.refs_3_, ...), custom_call_target="tpu_custom_call" | custom-call | flops 17179869184 | bytes 9437184 | tf_op jit(solution)/shard_map/far/pallas_call | solution.py:531
  30.5 0.0 collective-permute-done.7.refs_3_
  30.5 2.2 %near.1 = bf16[272,768]{1,0:T(8,128)(2,1)} custom-call(bf16[2,144,768]{2,1,0:T(8,128)(2,1)S(1)} %get-tuple-element.50.refs_0_, bf16[2,144,768]{2,1,0:T(8,128)(2,1)S(1)} %get-tuple-element.51.refs_1_, bf16[2,144,768]{2,1,0:T(8,128)(2,1)S(1)} %get-tuple-element.52.refs_2_, bf16[2,144,768]{2,1,0:T(8,128)(2,1)S(1)} %collective-permute-done.7.refs_3_, ...), custom_call_target="tpu_custom_call" | custom-call | tf_op jit(solution)/shard_map/near/pallas_call | solution.py:545
  (1 shorter events, 0.0 us)
Async XLA Ops:
  0.0 23.3 %copy-start = (bf16[512,768]{1,0:T(8,128)(2,1)S(1)}, bf16[512,768]{1,0:T(8,128)(2,1)}, u32[]{:S(2)}) copy-start(bf16[512,768]{1,0:T(8,128)(2,1)} %refs_2_.2) | copy-start | bytes 2359300
  0.0 23.3 %copy-start.1 = (f32[1536]{0:T(1024)S(1)}, f32[1536]{0:T(1024)}, u32[]{:S(2)}) copy-start(f32[1536]{0:T(1024)} %param.16) | copy-start | bytes 18436
  0.0 17.9 %copy-start.2 = (bf16[768]{0:T(1024)(128)(2,1)S(1)}, bf16[768]{0:T(1024)(128)(2,1)}, u32[]{:S(2)}) copy-start(bf16[768]{0:T(1024)(128)(2,1)} %param.15) | copy-start | bytes 4612
  0.0 16.1 %collective-permute-start.3 = (bf16[512,768]{1,0:T(8,128)(2,1)}, bf16[512,768]{1,0:T(8,128)(2,1)S(1)}, u32[]{:S(2)}, u32[]{:S(2)}) collective-permute-start(bf16[512,768]{1,0:T(8,128)(2,1)} %refs_2_.2), channel_id=1, source_target_pairs={{2,0},{17,1},{0,2},{19,3},{18,16},{1,17},{16,18},{3,19},{6,4},{21,... | collective-permute-start | bytes 2359304 | tf_op jit(solution)/shard_map/ppermute | solution.py:416
  6.5 7.6 %collective-permute-start = (bf16[16,2304]{1,0:T(8,128)(2,1)S(1)}, bf16[16,2304]{1,0:T(8,128)(2,1)S(1)}, u32[]{:S(2)}, u32[]{:S(2)}) collective-permute-start(bf16[16,2304]{1,0:T(8,128)(2,1)S(1)} %get-tuple-element.32), channel_id=1, source_target_pairs={{0,12},{4,8},{8,4},{12,0},{1,13},{5,9},{9,5},{13,1},{2,14},{6,10},... | collective-permute-start | bytes 221192 | tf_op jit(solution)/shard_map/ppermute | solution.py:441
  10.2 6.0 %collective-permute-start.1 = (bf16[16,2304]{1,0:T(8,128)(2,1)S(1)}, bf16[16,2304]{1,0:T(8,128)(2,1)S(1)}, u32[]{:S(2)}, u32[]{:S(2)}) collective-permute-start(bf16[16,2304]{1,0:T(8,128)(2,1)S(1)} %get-tuple-element.33), channel_id=1, source_target_pairs={{0,8},{4,12},{8,0},{12,4},{1,9},{5,13},{9,1},{13,5},{2,10},{6,14},... | collective-permute-start | bytes 221192 | tf_op jit(solution)/shard_map/ppermute | solution.py:441
  10.2 6.0 %collective-permute-start.2 = (bf16[16,2304]{1,0:T(8,128)(2,1)S(1)}, bf16[16,2304]{1,0:T(8,128)(2,1)S(1)}, u32[]{:S(2)}, u32[]{:S(2)}) collective-permute-start(bf16[16,2304]{1,0:T(8,128)(2,1)S(1)} %get-tuple-element.34), channel_id=1, source_target_pairs={{0,4},{4,0},{8,12},{12,8},{1,5},{5,1},{9,13},{13,9},{2,6},{6,2},{1... | collective-permute-start | bytes 221192 | tf_op jit(solution)/shard_map/ppermute | solution.py:441
  16.4 5.6 %collective-permute-start.4 = (bf16[32,2176]{1,0:T(8,128)(2,1)S(1)}, bf16[32,2176]{1,0:T(8,128)(2,1)S(1)}, u32[]{:S(2)}, u32[]{:S(2)}) collective-permute-start(bf16[32,2176]{1,0:T(8,128)(2,1)S(1)} %place.1.refs_0_), channel_id=1, source_target_pairs={{2,0},{0,2},{3,1},{1,3},{6,4},{4,6},{7,5},{5,7},{10,8},{8,10},{11,... | collective-permute-start | bytes 417800 | tf_op jit(solution)/shard_map/ppermute | solution.py:392
  17.9 5.5 %collective-permute-start.5 = (bf16[512,768]{1,0:T(8,128)(2,1)S(1)}, bf16[512,768]{1,0:T(8,128)(2,1)S(1)}, u32[]{:S(2)}, u32[]{:S(2)}) collective-permute-start(bf16[512,768]{1,0:T(8,128)(2,1)S(1)} %collective-permute-done.3.refs_3_), channel_id=1, source_target_pairs={{0,1},{1,0},{2,3},{3,2},{4,5},{5,4},{6,7},{7,6},{8,9},{9,8},{10,11... | collective-permute-start | bytes 2359304 | tf_op jit(solution)/shard_map/ppermute | solution.py:495
  17.9 5.5 %collective-permute-start.6 = (bf16[768]{0:T(1024)(128)(2,1)S(1)}, bf16[768]{0:T(1024)(128)(2,1)S(1)}, u32[]{:S(2)}, u32[]{:S(2)}) collective-permute-start(bf16[768]{0:T(1024)(128)(2,1)S(1)} %copy-done.2), channel_id=1, source_target_pairs={{2,0},{0,2},{3,1},{1,3},{6,4},{4,6},{7,5},{5,7},{10,8},{8,10},{11,... | collective-permute-start | bytes 4616 | tf_op jit(solution)/shard_map/ppermute | solution.py:392
  22.0 5.5 %collective-permute-start.8 = (bf16[32,2176]{1,0:T(8,128)(2,1)S(1)}, bf16[32,2176]{1,0:T(8,128)(2,1)S(1)}, u32[]{:S(2)}, u32[]{:S(2)}) collective-permute-start(bf16[32,2176]{1,0:T(8,128)(2,1)S(1)} %broadcast_select_fusion), channel_id=1, source_target_pairs={{4,1},{1,4},{8,5},{5,8},{12,9},{9,12},{0,2},{13,15},{6,3},{3,6},{1... | collective-permute-start | bytes 417800 | tf_op jit(solution)/shard_map/ppermute | solution.py:512
  27.4 3.1 %collective-permute-start.7 = (bf16[2,144,768]{2,1,0:T(8,128)(2,1)S(1)}, bf16[2,144,768]{2,1,0:T(8,128)(2,1)S(1)}, u32[]{:S(2)}, u32[]{:S(2)}) collective-permute-start(bf16[2,144,768]{2,1,0:T(8,128)(2,1)S(1)} %get-tuple-element.53), channel_id=1, source_target_pairs={{0,1},{1,0},{2,3},{3,2},{4,5},{5,4},{6,7},{7,6},{8,9},{9,8},{10,11... | collective-permute-start | bytes 1327112 | tf_op jit(solution)/shard_map/ppermute | solution.py:530

commit v3 on v2

--- a/solution.py
+++ b/solution.py
@@ -1,4 +1,5 @@
 import functools
+import itertools
 import math
 
 import jax
@@ -162,23 +163,8 @@
         out[...] = packed[d * count : (d + 1) * count]
 
 
-def place_kernel(*refs):
-    parts, out = refs[:-1], refs[-1]
-    rows = jnp.concatenate([part[...] for part in parts], axis=0)
-    slots = rows.shape[0]
-    mark = rows[:, MEL_WIDTH : MEL_WIDTH + LANES].astype(F32)[:, :1]
-    row, col = iota((slots, slots), 0), iota((slots, slots), 1)
-    mark = jnp.sum(jnp.where(row == col, mark, 0.0), axis=0, keepdims=True)
-    at = iota((PE, slots), 0)
-    groups = PE // GROUP
-    wanted = (at % groups) * GROUP + at // groups + 1
-    pick = (wanted.astype(F32) == mark).astype(F32).astype(BF16)
-    out[...] = dot(pick, rows[:, :MEL_WIDTH]).astype(BF16)
-
-
 def token_rows(pieces):
     groups = PE // GROUP
-    pieces = pieces.astype(F32)
     rows = []
     for i in range(FP):
         cells = []
@@ -192,6 +178,20 @@
     token = (col % groups) * FP + col // groups
     order = ((row == token) & (col < CH)).astype(F32).astype(BF16)
     return dot(order, mixed).astype(BF16)
+
+
+def place_kernel(*refs):
+    parts, out = refs[:-1], refs[-1]
+    rows = jnp.concatenate([part[...] for part in parts], axis=0)
+    slots = rows.shape[0]
+    mark = rows[:, MEL_WIDTH : MEL_WIDTH + LANES].astype(F32)[:, :1]
+    row, col = iota((slots, slots), 0), iota((slots, slots), 1)
+    mark = jnp.sum(jnp.where(row == col, mark, 0.0), axis=0, keepdims=True)
+    at = iota((PE, slots), 0)
+    groups = PE // GROUP
+    wanted = (at % groups) * GROUP + at // groups + 1
+    pick = (wanted.astype(F32) == mark).astype(F32).astype(BF16)
+    out[...] = token_rows(dot(pick, rows[:, :MEL_WIDTH]))
 
 
 def prepare_kernel(
@@ -267,16 +267,18 @@
 
 def normalize(tokens, conv, conv_bias, gain, out):
     summed = dot(tokens, conv[...]) + conv_bias[...]
-    features = (summed / (1.0 + jnp.exp(-summed))).astype(BF16).astype(F32)
+    half = 0.5 * summed
+    features = (half + half * jnp.tanh(half)).astype(BF16).astype(F32)
     scale = 1.0 / features.shape[1]
     centred = features - jnp.sum(features, axis=1, keepdims=True) * scale
     variance = jnp.sum(centred * centred, axis=1, keepdims=True) * scale
     out[...] = (centred * lax.rsqrt(variance + EPSILON) * gain[...]).astype(BF16)
 
 
-def half_kernel(n, *refs):
-    pieces, parts, bias_parts = refs[:n], refs[n : 3 * n - 1], refs[3 * n - 1 : 4 * n - 1]
-    gain_rows, qkv, *outs, sent, conv, conv_bias, gain, normed = refs[4 * n - 1 :]
+def own_kernel(n, *refs):
+    pieces, parts, refs = refs[0], refs[1 : 2 * n], refs[2 * n :]
+    bias_parts, gain_rows, refs = refs[:n], refs[n], refs[n + 1 :]
+    qkv, q_out, k_out, v_out, conv, conv_bias, gain, normed = refs
     me, core = lax.axis_index("head"), lax.axis_index("sub")
     depth = parts[0].shape[1]
     for d in range(n):
@@ -288,25 +290,35 @@
         if d == 0:
             conv[:, at] = parts[0][...]
         else:
-            got, passed = parts[2 * d - 1 : 2 * d + 1]
+            got, swapped = parts[2 * d - 1 : 2 * d + 1]
 
             @pl.when(core == 0)
             def _(got=got, at=at):
                 conv[:, at] = got[...]
 
             @pl.when(core == 1)
-            def _(passed=passed, at=at):
-                conv[:, at] = passed[...]
+            def _(swapped=swapped, at=at):
+                conv[:, at] = swapped[...]
 
     for k in range(gain_rows.shape[0]):
         gain[:, k * LANES : (k + 1) * LANES] = gain_rows[k : k + 1, :]
-    tokens = jnp.concatenate([token_rows(piece[...]) for piece in pieces], axis=0)
+    normalize(pieces[...], conv, conv_bias, gain, normed)
+    for p, out in enumerate((q_out, k_out, v_out)):
+        out[0] = dot(normed[...], qkv[p]).astype(BF16)
+
+
+def others_kernel(n, *refs):
+    own, pieces = refs[:3], refs[3 : n + 2]
+    conv, conv_bias, gain, qkv, *outs, sent, normed = refs[n + 2 :]
+    me, core = lax.axis_index("head"), lax.axis_index("sub")
+    tokens = jnp.concatenate([piece[...] for piece in pieces], axis=0)
     normalize(tokens, conv, conv_bias, gain, normed)
     wanted = jnp.where(core == 0, n - 1, 0)
-    for p, out in enumerate(outs):
+    for p, (source, out) in enumerate(zip(own, outs)):
+        out[me] = source[0]
         got = dot(normed[...], qkv[p]).astype(BF16)
-        for d in range(n):
-            out[lax.rem(me + d, n)] = got[d * ROWS : (d + 1) * ROWS]
+        for d in range(1, n):
+            out[lax.rem(me + d, n)] = got[(d - 1) * ROWS : d * ROWS]
         if p > 0:
             sent[p - 1] = out[wanted]
 
@@ -336,10 +348,13 @@
 
 
 def far_kernel(n, *refs):
-    queries, keys, values, far, conv, conv_bias, gain, qkv, bias, out = refs[:10]
-    normed, far_keys, far_values = refs[10:]
-    core = lax.axis_index("sub")
-    normalize(token_rows(far[...]), conv, conv_bias, gain, normed)
+    (queries, keys, values), rounds, refs = refs[:3], refs[3 : n + 3], refs[n + 3 :]
+    conv, conv_bias, gain, qkv, bias, out, normed, far_keys, far_values = refs
+    me, core = lax.axis_index("head"), lax.axis_index("sub")
+    far, turn = rounds[0][...], jnp.where(core == 0, n - 1 - me, me)
+    for r in range(1, n):
+        far = jnp.where(turn == r, rounds[r][...], far)
+    normalize(far, conv, conv_bias, gain, normed)
     far_keys[...] = dot(normed[...], qkv[1]).astype(BF16)
     far_values[...] = dot(normed[...], qkv[2]).astype(BF16)
     block, first = jnp.where(core == 0, 0, n - 1), jnp.where(core == 0, 0, n - 2)
@@ -351,8 +366,9 @@
 
 
 def near_kernel(n, *refs):
-    queries, keys, values, near, far_context, bias, out = refs
+    queries, keys, values, near, far_context, bias, out_hbm, out, sems = refs
     core = lax.axis_index("sub")
+    copies = []
     block, first = jnp.where(core == 0, n - 1, 0), jnp.where(core == 0, n - 2, 0)
     for pair in range(queries.shape[2] // LANES):
         at = slice(pair * LANES, (pair + 1) * LANES)
@@ -374,6 +390,10 @@
             jnp.concatenate([other] + middle + [context], axis=0),
             jnp.concatenate([context] + middle + [other], axis=0),
         ).astype(BF16)
+        copies.append(pltpu.make_async_copy(out.at[:, at], out_hbm.at[:, at], sems.at[pair]))
+        copies[-1].start()
+    for copy in copies:
+        copy.wait()
 
 
 def vmem(count):
@@ -405,7 +425,7 @@
     fourier, filters, window = fourier_tables(), mel_tables(), window_halves()
     in_hbm = pl.BlockSpec(memory_space=pltpu.HBM)
     groups = lax.axis_size("groups")
-    weight_got = []
+    weight_got, bias_got = [], from_heads(sub_bias, n)
     for d in range(1, n):
         links = []
         for g in range(groups):
@@ -449,13 +469,7 @@
     local_width = qkv_weight.shape[2]
     pairs = local_width // LANES
     gain = norm_gain.reshape(-1, LANES)
-    me, core = lax.axis_index("head"), lax.axis_index("sub")
-    last, first = lax.rem(n - 1 - me + n, n), lax.rem(n - me, n)
-    far_at = jnp.where(core == 0, first, last)
-    far_is = [far_at == d for d in range(n)]
-    rel_bias, gain, far_is, _ = lax.optimization_barrier(
-        (rel_bias, gain, far_is, packed[0])
-    )
+    rel_bias, gain, _ = lax.optimization_barrier((rel_bias, gain, packed[0]))
     entries = rel_bias.shape[1]
     qkv = jnp.transpose(qkv_weight, (1, 0, 2))
     bias, qkv = pl.pallas_call(
@@ -476,62 +490,83 @@
         cost_estimate=pl.CostEstimate(flops=1 << 31, bytes_accessed=8 << 20, transcendentals=0),
         name="prepare",
     )(from_hbm(utt_lengths), from_hbm(rel_bias), from_hbm(qkv))
-    received, weight_got, bias, qkv, gain, far_is = lax.optimization_barrier(
-        (received, weight_got, bias, qkv, gain, far_is)
+    received, weight_got, bias_got, bias, qkv, gain = lax.optimization_barrier(
+        (received, weight_got, bias_got, bias, qkv, gain)
     )
     own = pl.pallas_call(
         place_kernel,
-        out_shape=jax.ShapeDtypeStruct((PE, MEL_WIDTH), BF16),
+        out_shape=jax.ShapeDtypeStruct((ROWS, STACK * MEL), BF16),
         in_specs=vmem(len(received)),
         out_specs=vmem(1)[0],
         compiler_params=pltpu.CompilerParams(vmem_limit_bytes=8 << 20),
         name="place",
     )(*received)
-    bias_sent, _ = lax.optimization_barrier((sub_bias, own))
-    bias_lines = [part.reshape(-1, LANES) for part in [sub_bias] + from_heads(bias_sent, n)]
     conv = [sub_weight]
     for got in weight_got:
         got, _ = lax.optimization_barrier((got, own))
         conv += [got, lax.ppermute(got, "sub", [(0, 1), (1, 0)])]
+    conv_bias = [line.reshape(-1, LANES) for line in [sub_bias] + bias_got]
 
     others = from_heads(own, n)
     width = qkv_weight.shape[0]
     qkv = in_vmem(qkv)
     limit = pltpu.CompilerParams(vmem_limit_bytes=16 << 20)
-    far_sent = own
-    for d in range(1, n):
-        far_sent = jnp.where(far_is[d], others[d - 1], far_sent)
-    links = []
-    for h in range(n):
-        for k in range(shards - 1):
-            above, below = ((k + 1) * n + h) * cores, (k * n + h) * cores + 1
-            links += [(above, below), (below, above)]
-        links.append((h * cores, (h + 1) % n * cores))
-        ends = (shards - 1) * n
-        links.append(((ends + h) * cores + 1, (ends + (h + 1) % n) * cores + 1))
-    far = lax.ppermute(far_sent, ("seq", "head", "sub"), links)
-    *half_qkv, near_sent, whole, whole_bias, whole_gain = pl.pallas_call(
-        functools.partial(half_kernel, n),
-        out_shape=[jax.ShapeDtypeStruct((n, ROWS, local_width), BF16)] * 3
+    rounds = [None] * n
+    for r in reversed(range(n)):
+        links = {}
+        for g in range(groups):
+            for k in range(shards - 1):
+                for source, target in (
+                    ((g, k, n - 1, 1), (g, k + 1, r, 0)),
+                    ((g, k + 1, 0, 0), (g, k, n - 1 - r, 1)),
+                ):
+                    links[source] = target
+        for source, target in list(links.items()):
+            links.setdefault(target, source)
+        for g in range(groups):
+            for end in ((g, 0, 0, 0), (g, shards - 1, n - 1, 1)):
+                beside = (*end[:2], n - 1 - end[2], end[3])
+                if end not in links and beside not in links:
+                    links.update({end: beside, beside: end} if r == 0 else {})
+        for place in itertools.product(range(groups), range(shards), range(n), range(cores)):
+            links.setdefault(place, ((place[0] + 1) % groups, *place[1:]))
+        assert len(set(links.values())) == len(links)
+        sizes = (groups, shards, n, cores)
+        flat = [tuple(int(np.ravel_multi_index(p, sizes)) for p in link) for link in links.items()]
+        rounds[r] = lax.ppermute(own, ("groups", "seq", "head", "sub"), flat)
+    limit = pltpu.CompilerParams(vmem_limit_bytes=16 << 20)
+    *own_qkv, whole, whole_bias, whole_gain = pl.pallas_call(
+        functools.partial(own_kernel, n),
+        out_shape=[jax.ShapeDtypeStruct((1, ROWS, local_width), BF16)] * 3
         + [
-            jax.ShapeDtypeStruct((2, ROWS, local_width), BF16),
             jax.ShapeDtypeStruct((sub_weight.shape[0], width), BF16),
             jax.ShapeDtypeStruct((1, width), F32),
             jax.ShapeDtypeStruct((1, width), F32),
         ],
-        in_specs=vmem(n + len(conv) + n + 2),
-        out_specs=vmem(7),
-        scratch_shapes=[pltpu.VMEM((n * ROWS, width), BF16)],
+        in_specs=vmem(1 + len(conv) + len(conv_bias) + 2),
+        out_specs=vmem(6),
+        scratch_shapes=[pltpu.VMEM((ROWS, width), BF16)],
+        compiler_params=limit,
+        cost_estimate=pl.CostEstimate(flops=1 << 20, bytes_accessed=1 << 20, transcendentals=0),
+        name="own",
+    )(own, *conv, *conv_bias, gain, qkv)
+    weights = (whole, whole_bias, whole_gain, qkv)
+    *half_qkv, near_sent = pl.pallas_call(
+        functools.partial(others_kernel, n),
+        out_shape=[jax.ShapeDtypeStruct((n, ROWS, local_width), BF16)] * 3
+        + [jax.ShapeDtypeStruct((2, ROWS, local_width), BF16)],
+        in_specs=vmem(n + 2 + len(weights)),
+        out_specs=vmem(4),
+        scratch_shapes=[pltpu.VMEM(((n - 1) * ROWS, width), BF16)],
         compiler_params=limit,
         cost_estimate=pl.CostEstimate(flops=4 << 30, bytes_accessed=9 << 20, transcendentals=0),
-        name="half",
-    )(own, *others, *conv, *bias_lines, gain, qkv)
-    weights = (whole, whole_bias, whole_gain, qkv)
+        name="others",
+    )(*own_qkv, *others, *weights)
     near = lax.ppermute(near_sent, "sub", [(0, 1), (1, 0)])
     far_context = pl.pallas_call(
         functools.partial(far_kernel, n),
         out_shape=jax.ShapeDtypeStruct((ROWS, local_width), BF16),
-        in_specs=vmem(4 + len(weights) + 1),
+        in_specs=vmem(3 + n + len(weights) + 1),
         out_specs=vmem(1)[0],
         scratch_shapes=[
             pltpu.VMEM((ROWS, width), BF16),
@@ -541,12 +576,16 @@
         compiler_params=limit,
         cost_estimate=pl.CostEstimate(flops=16 << 30, bytes_accessed=9 << 20, transcendentals=0),
         name="far",
-    )(*half_qkv, far, *weights, in_vmem(bias))
+    )(*half_qkv, *rounds[::-1], *weights, in_vmem(bias))
     return pl.pallas_call(
         functools.partial(near_kernel, n),
         out_shape=jax.ShapeDtypeStruct((n * CH, local_width), BF16),
         in_specs=vmem(6),
-        out_specs=vmem(1)[0],
+        out_specs=in_hbm,
+        scratch_shapes=[
+            pltpu.VMEM((n * CH, local_width), BF16),
+            pltpu.SemaphoreType.DMA((pairs,)),
+        ],
         compiler_params=limit,
         name="near",
     )(*half_qkv, near, far_context, in_vmem(bias))

time: 32.9 us -> 31 us (0.942)
  waiting for transfers between devices: 5.62 us -> 2.58 us
  Pallas kernels: 16.1 us -> 16.7 us
    ppermute x2, waiting for transfers between devices: 3.55 us -> 1.19 us  [from_heads(): lax.ppermute(block, 'head', [((i + d) % n, i) for i in range(n)])]
    ppermute x3, waiting for transfers between devices: 2.06 us -> 1.38 us  [local(): lax.ppermute(packed[d], 'seq', [(i, i ^ d) for i in range(shards)])]
    pallas_call x2 -> x3, Pallas kernels: 4.33 us -> 4.88 us  [the longest x1 2.24 us: local(): pl.pallas_call(functools.partial(others_kernel, n), out_shape=[jax.ShapeD...]
    ppermute x1 -> x2, starting transfers between devices: 1.29 us -> 1.65 us  [local(): rounds[r] = lax.ppermute(own, ('groups', 'seq', 'head', 'sub'), flat)]
  transfers between devices with their start and end apart: 9 -> 10, of which waited for: 2 -> 3; matrix products, arithmetic and copies ran while one was open for 0% -> 0% of each run, Pallas kernels for 42% -> 46%
where the time goes in v3:
time: 31 us; the launch traced here: 30.5 us
  Pallas kernels  16.7 us (54%)
  starting transfers between devices  11.1 us (36%)
  waiting for transfers between devices  2.58 us (8%)
    ppermute x3, starting transfers between devices, local(): lax.ppermute(packed[d], 'seq', [(i, i ^ d) for i in range(shards)])  4.45 us
    pallas_call x1, Pallas kernels, local(): pl.pallas_call(functools.partial(mel_kernel, shards, capacity, relative),...  3.46 us
    pallas_call x1, Pallas kernels, local(): pl.pallas_call(prepare_kernel, out_shape=[pltpu.VMEM((pairs, n, 2 * ROWS,...  3.1 us
    ppermute x1, starting transfers between devices, local(): lax.ppermute(sub_weight, ('groups', 'head', 'sub'), links)  3.01 us
    pallas_call x1, Pallas kernels, local(): pl.pallas_call(functools.partial(far_kernel, n), out_shape=jax.ShapeDtype...  3 us
    pallas_call x1, Pallas kernels, local(): pl.pallas_call(functools.partial(near_kernel, n), out_shape=jax.ShapeDtyp...  2.27 us
    pallas_call x1, Pallas kernels, local(): pl.pallas_call(functools.partial(others_kernel, n), out_shape=[jax.ShapeD...  2.24 us
    pallas_call x1, Pallas kernels, local(): pl.pallas_call(functools.partial(own_kernel, n), out_shape=[jax.ShapeDtyp...  2.19 us
  transfers between devices with their start and end apart: 10, of which 3 were waited for; matrix products, arithmetic and copies ran while one was open for 0% of the time, Pallas kernels for 46%

profile of v3, /device:TPU:0, one launch (start us, length us, event | category | flops | bytes accessed | tf_op | source)
XLA Modules:
  0.0 30.5 jit_solution(12708609792999052934)
XLA Ops:
  0.0 0.0 copy-start
  0.0 0.0 copy-start.2
  0.0 3.0 %collective-permute-start.3 = (bf16[512,768]{1,0:T(8,128)(2,1)}, bf16[512,768]{1,0:T(8,128)(2,1)S(1)}, u32[]{:S(2)}, u32[]{:S(2)}) collective-permute-start(bf16[512,768]{1,0:T(8,128)(2,1)} %refs_1_.1), channel_id=1, source_target_pairs={{2,0},{17,1},{0,2},{19,3},{18,16},{1,17},{16,18},{3,19},{6,4},{21,... | collective-permute-start | bytes 2359304 | tf_op jit(solution)/shard_map/ppermute | solution.py:436
  3.0 3.5 %log_mel.1 = (bf16[16,2304]{1,0:T(8,128)(2,1)S(1)}, bf16[16,2304]{1,0:T(8,128)(2,1)S(1)}, bf16[16,2304]{1,0:T(8,128)(2,1)S(1)}, bf16[16,2304]{1,0:T(8,128)(2,1)S(1)}) custom-call(f32[64,3072]{1,0:T(8,128)} %bitcast.9, s32[1,64]{1,0:T(1,128)} %bitcast.10, f32[2,256]{1,0:T(2,128)} %constant.6.clone.refs_2_, bf16[2,2,256,256]{3,2,1,0:T(8,128)(2,1)} %constant.7.clone.refs_3_, ...), custom_call_target="tpu_custom_call" | custom-call | tf_op jit(solution)/shard_map/log_mel/pallas_call | solution.py:437
  6.5 3.7 %collective-permute-start = (bf16[16,2304]{1,0:T(8,128)(2,1)S(1)}, bf16[16,2304]{1,0:T(8,128)(2,1)S(1)}, u32[]{:S(2)}, u32[]{:S(2)}) collective-permute-start(bf16[16,2304]{1,0:T(8,128)(2,1)S(1)} %get-tuple-element.33), channel_id=1, source_target_pairs={{0,12},{4,8},{8,4},{12,0},{1,13},{5,9},{9,5},{13,1},{2,14},{6,10},... | collective-permute-start | bytes 221192 | tf_op jit(solution)/shard_map/ppermute | solution.py:461
  10.2 0.0 collective-permute-start.1
  10.2 0.8 %collective-permute-start.2 = (bf16[16,2304]{1,0:T(8,128)(2,1)S(1)}, bf16[16,2304]{1,0:T(8,128)(2,1)S(1)}, u32[]{:S(2)}, u32[]{:S(2)}) collective-permute-start(bf16[16,2304]{1,0:T(8,128)(2,1)S(1)} %get-tuple-element.35), channel_id=1, source_target_pairs={{0,4},{4,0},{8,12},{12,8},{1,5},{5,1},{9,13},{13,9},{2,6},{6,2},{1... | collective-permute-start | bytes 221192 | tf_op jit(solution)/shard_map/ppermute | solution.py:461
  10.9 0.4 %collective-permute-start.4 = (bf16[768]{0:T(1024)(128)(2,1)}, bf16[768]{0:T(1024)(128)(2,1)S(1)}, u32[]{:S(2)}, u32[]{:S(2)}) collective-permute-start(bf16[768]{0:T(1024)(128)(2,1)} %param.15), channel_id=1, source_target_pairs={{2,0},{0,2},{3,1},{1,3},{6,4},{4,6},{7,5},{5,7},{10,8},{8,10},{11,... | collective-permute-start | bytes 4616 | tf_op jit(solution)/shard_map/ppermute | solution.py:412
  11.3 3.1 %prepare.1 = (f32[6,2,288,432]{3,2,1,0:T(8,128)S(1)}, bf16[3,1536,768]{2,1,0:T(8,128)(2,1)S(1)}) custom-call(s32[4]{0:T(128)} %lengths_hbm.1, f32[12,543]{1,0:T(8,128)} %table_hbm, bf16[3,1536,768]{2,1,0:T(8,128)(2,1)} %bitcast.11), custom_call_target="tpu_custom_call" | custom-call | flops 2147483648 | bytes 8388608 | tf_op jit(solution)/shard_map/prepare/pallas_call | solution.py:475
  14.4 0.3 collective-permute-done.4
  14.7 0.0 collective-permute-done.refs_0_
  14.7 1.4 %collective-permute-done.1.refs_1_ = bf16[16,2304]{1,0:T(8,128)(2,1)S(1)} collective-permute-done((bf16[16,2304]{1,0:T(8,128)(2,1)S(1)}, bf16[16,2304]{1,0:T(8,128)(2,1)S(1)}, u32[]{:S(2)}, u32[]{:S(2)}) %collective-permute-start.1) | collective-permute-done | bytes 73760 | tf_op jit(solution)/shard_map/ppermute | solution.py:461
  16.1 0.0 collective-permute-done.2.refs_2_
  16.1 0.0 collective-permute-done.3.refs_2_
  16.1 0.4 %place.1.refs_0_ = bf16[144,512]{1,0:T(8,128)(2,1)S(1)} custom-call(bf16[16,2304]{1,0:T(8,128)(2,1)S(1)} %collective-permute-done.refs_0_, bf16[16,2304]{1,0:T(8,128)(2,1)S(1)} %collective-permute-done.1.refs_1_, bf16[16,2304]{1,0:T(8,128)(2,1)S(1)} %collective-permute-done.2.refs_2_, bf16[16,2304]{1,0:T(8,128)(2,1)S(1)} %get-tuple-element.44.refs_3_), custom_call_target="tpu_custom_call" | custom-call | tf_op jit(solution)/shard_map/place/pallas_call | solution.py:496
  16.6 0.1 collective-permute-start.5
  16.6 1.5 %collective-permute-start.6 = (bf16[144,512]{1,0:T(8,128)(2,1)S(1)}, bf16[144,512]{1,0:T(8,128)(2,1)S(1)}, u32[]{:S(2)}, u32[]{:S(2)}) collective-permute-start(bf16[144,512]{1,0:T(8,128)(2,1)S(1)} %place.1.refs_0_), channel_id=1, source_target_pairs={{2,0},{0,2},{3,1},{1,3},{6,4},{4,6},{7,5},{5,7},{10,8},{8,10},{11,... | collective-permute-start | bytes 442376 | tf_op jit(solution)/shard_map/ppermute | solution.py:412
  18.1 0.6 %collective-permute-start.8 = (bf16[144,512]{1,0:T(8,128)(2,1)S(1)}, bf16[144,512]{1,0:T(8,128)(2,1)S(1)}, u32[]{:S(2)}, u32[]{:S(2)}) collective-permute-start(bf16[144,512]{1,0:T(8,128)(2,1)S(1)} %place.1.refs_0_), channel_id=1, source_target_pairs={{3,6},{4,1},{7,10},{8,5},{11,14},{12,9},{19,22},{20,17},{23,26},{2... | collective-permute-start | bytes 442376 | tf_op jit(solution)/shard_map/ppermute | solution.py:536
  18.7 1.1 %collective-permute-start.9 = (bf16[144,512]{1,0:T(8,128)(2,1)S(1)}, bf16[144,512]{1,0:T(8,128)(2,1)S(1)}, u32[]{:S(2)}, u32[]{:S(2)}) collective-permute-start(bf16[144,512]{1,0:T(8,128)(2,1)S(1)} %place.1.refs_0_), channel_id=1, source_target_pairs={{3,4},{4,3},{7,8},{8,7},{11,12},{12,11},{19,20},{20,19},{23,24},{2... | collective-permute-start | bytes 442376 | tf_op jit(solution)/shard_map/ppermute | solution.py:536
  19.8 0.0 collective-permute-done.5.refs_3_
  19.8 0.0 copy-done
  19.8 0.0 copy-done.2
  19.8 0.0 copy-done.1
  19.8 2.2 %own.1 = (bf16[1,144,768]{2,1,0:T(8,128)(2,1)S(1)}, bf16[1,144,768]{2,1,0:T(8,128)(2,1)S(1)}, bf16[1,144,768]{2,1,0:T(8,128)(2,1)S(1)}, bf16[512,1536]{1,0:T(8,1...) custom-call(bf16[144,512]{1,0:T(8,128)(2,1)S(1)} %place.1.refs_0_, bf16[512,768]{1,0:T(8,128)(2,1)S(1)} %copy-done, ...), custom_call_target="tpu_custom_call" | custom-call | flops 1048576 | bytes 1048576 | tf_op jit(solution)/shard_map/own/pallas_call | solution.py:538
  22.0 0.9 %collective-permute-done.6.refs_3_ = bf16[144,512]{1,0:T(8,128)(2,1)S(1)} collective-permute-done((bf16[144,512]{1,0:T(8,128)(2,1)S(1)}, bf16[144,512]{1,0:T(8,128)(2,1)S(1)}, u32[]{:S(2)}, u32[]{:S(2)}) %collective-permute-start.6) | collective-permute-done | bytes 147488 | tf_op jit(solution)/shard_map/ppermute | solution.py:412
  22.9 2.2 %others.1 = (bf16[2,144,768]{2,1,0:T(8,128)(2,1)S(1)}, bf16[2,144,768]{2,1,0:T(8,128)(2,1)S(1)}, bf16[2,144,768]{2,1,0:T(8,128)(2,1)S(1)}, bf16[2,144,768]{2,1,0:T(8,128)(2,1)S(1)}) custom-call(bf16[1,144,768]{2,1,0:T(8,128)(2,1)S(1)} %get-tuple-element.50.refs_0_, bf16[1,144,768]{2,1,0:T(8,128)(2,1)S(1)} %get-tuple-element.51.refs_1_, ...), custom_call_target="tpu_custom_call" | custom-call | flops 4294967296 | bytes 9437184 | tf_op jit(solution)/shard_map/others/pallas_call | solution.py:554
  25.2 0.1 collective-permute-start.7
  25.2 0.0 collective-permute-done.8.refs_3_
  25.2 0.0 collective-permute-done.9.refs_4_
  25.2 3.0 %far.1.refs_4_ = bf16[144,768]{1,0:T(8,128)(2,1)S(1)} custom-call(bf16[2,144,768]{2,1,0:T(8,128)(2,1)S(1)} %get-tuple-element.56.refs_0_, bf16[2,144,768]{2,1,0:T(8,128)(2,1)S(1)} %get-tuple-element.57.refs_1_, bf16[2,144,768]{2,1,0:T(8,128)(2,1)S(1)} %get-tuple-element.58.refs_2_, bf16[144,512]{1,0:T(8,128)(2,1)S(1)} %collective-permute-done.8.refs_3_, ...), custom_call_target="tpu_custom_call" | custom-call | flops 17179869184 | bytes 9437184 | tf_op jit(solution)/shard_map/far/pallas_call | solution.py:566
  28.2 0.0 collective-permute-done.7.refs_3_
  28.3 2.3 %near.1 = bf16[272,768]{1,0:T(8,128)(2,1)} custom-call(bf16[2,144,768]{2,1,0:T(8,128)(2,1)S(1)} %get-tuple-element.56.refs_0_, bf16[2,144,768]{2,1,0:T(8,128)(2,1)S(1)} %get-tuple-element.57.refs_1_, bf16[2,144,768]{2,1,0:T(8,128)(2,1)S(1)} %get-tuple-element.58.refs_2_, bf16[2,144,768]{2,1,0:T(8,128)(2,1)S(1)} %collective-permute-done.7.refs_3_, ...), custom_call_target="tpu_custom_call" | custom-call | tf_op jit(solution)/shard_map/near/pallas_call | solution.py:580
  (1 shorter events, 0.0 us)
Async XLA Ops:
  0.0 19.8 %copy-start = (bf16[512,768]{1,0:T(8,128)(2,1)S(1)}, bf16[512,768]{1,0:T(8,128)(2,1)}, u32[]{:S(2)}) copy-start(bf16[512,768]{1,0:T(8,128)(2,1)} %refs_1_.1) | copy-start | bytes 2359300
  0.0 19.8 %copy-start.2 = (bf16[768]{0:T(1024)(128)(2,1)S(1)}, bf16[768]{0:T(1024)(128)(2,1)}, u32[]{:S(2)}) copy-start(bf16[768]{0:T(1024)(128)(2,1)} %param.15) | copy-start | bytes 4612
  0.0 19.8 %copy-start.1 = (f32[1536]{0:T(1024)S(1)}, f32[1536]{0:T(1024)}, u32[]{:S(2)}) copy-start(f32[1536]{0:T(1024)} %param.16) | copy-start | bytes 18436
  0.0 16.1 %collective-permute-start.3 = (bf16[512,768]{1,0:T(8,128)(2,1)}, bf16[512,768]{1,0:T(8,128)(2,1)S(1)}, u32[]{:S(2)}, u32[]{:S(2)}) collective-permute-start(bf16[512,768]{1,0:T(8,128)(2,1)} %refs_1_.1), channel_id=1, source_target_pairs={{2,0},{17,1},{0,2},{19,3},{18,16},{1,17},{16,18},{3,19},{6,4},{21,... | collective-permute-start | bytes 2359304 | tf_op jit(solution)/shard_map/ppermute | solution.py:436
  6.5 8.3 %collective-permute-start = (bf16[16,2304]{1,0:T(8,128)(2,1)S(1)}, bf16[16,2304]{1,0:T(8,128)(2,1)S(1)}, u32[]{:S(2)}, u32[]{:S(2)}) collective-permute-start(bf16[16,2304]{1,0:T(8,128)(2,1)S(1)} %get-tuple-element.33), channel_id=1, source_target_pairs={{0,12},{4,8},{8,4},{12,0},{1,13},{5,9},{9,5},{13,1},{2,14},{6,10},... | collective-permute-start | bytes 221192 | tf_op jit(solution)/shard_map/ppermute | solution.py:461
  10.2 6.0 %collective-permute-start.1 = (bf16[16,2304]{1,0:T(8,128)(2,1)S(1)}, bf16[16,2304]{1,0:T(8,128)(2,1)S(1)}, u32[]{:S(2)}, u32[]{:S(2)}) collective-permute-start(bf16[16,2304]{1,0:T(8,128)(2,1)S(1)} %get-tuple-element.34), channel_id=1, source_target_pairs={{0,8},{4,12},{8,0},{12,4},{1,9},{5,13},{9,1},{13,5},{2,10},{6,14},... | collective-permute-start | bytes 221192 | tf_op jit(solution)/shard_map/ppermute | solution.py:461
  10.2 6.0 %collective-permute-start.2 = (bf16[16,2304]{1,0:T(8,128)(2,1)S(1)}, bf16[16,2304]{1,0:T(8,128)(2,1)S(1)}, u32[]{:S(2)}, u32[]{:S(2)}) collective-permute-start(bf16[16,2304]{1,0:T(8,128)(2,1)S(1)} %get-tuple-element.35), channel_id=1, source_target_pairs={{0,4},{4,0},{8,12},{12,8},{1,5},{5,1},{9,13},{13,9},{2,6},{6,2},{1... | collective-permute-start | bytes 221192 | tf_op jit(solution)/shard_map/ppermute | solution.py:461
  10.9 3.8 %collective-permute-start.4 = (bf16[768]{0:T(1024)(128)(2,1)}, bf16[768]{0:T(1024)(128)(2,1)S(1)}, u32[]{:S(2)}, u32[]{:S(2)}) collective-permute-start(bf16[768]{0:T(1024)(128)(2,1)} %param.15), channel_id=1, source_target_pairs={{2,0},{0,2},{3,1},{1,3},{6,4},{4,6},{7,5},{5,7},{10,8},{8,10},{11,... | collective-permute-start | bytes 4616 | tf_op jit(solution)/shard_map/ppermute | solution.py:412
  16.6 3.2 %collective-permute-start.5 = (bf16[512,768]{1,0:T(8,128)(2,1)S(1)}, bf16[512,768]{1,0:T(8,128)(2,1)S(1)}, u32[]{:S(2)}, u32[]{:S(2)}) collective-permute-start(bf16[512,768]{1,0:T(8,128)(2,1)S(1)} %collective-permute-done.3.refs_2_), channel_id=1, source_target_pairs={{0,1},{1,0},{2,3},{3,2},{4,5},{5,4},{6,7},{7,6},{8,9},{9,8},{10,11... | collective-permute-start | bytes 2359304 | tf_op jit(solution)/shard_map/ppermute | solution.py:507
  16.6 6.3 %collective-permute-start.6 = (bf16[144,512]{1,0:T(8,128)(2,1)S(1)}, bf16[144,512]{1,0:T(8,128)(2,1)S(1)}, u32[]{:S(2)}, u32[]{:S(2)}) collective-permute-start(bf16[144,512]{1,0:T(8,128)(2,1)S(1)} %place.1.refs_0_), channel_id=1, source_target_pairs={{2,0},{0,2},{3,1},{1,3},{6,4},{4,6},{7,5},{5,7},{10,8},{8,10},{11,... | collective-permute-start | bytes 442376 | tf_op jit(solution)/shard_map/ppermute | solution.py:412
  18.1 7.1 %collective-permute-start.8 = (bf16[144,512]{1,0:T(8,128)(2,1)S(1)}, bf16[144,512]{1,0:T(8,128)(2,1)S(1)}, u32[]{:S(2)}, u32[]{:S(2)}) collective-permute-start(bf16[144,512]{1,0:T(8,128)(2,1)S(1)} %place.1.refs_0_), channel_id=1, source_target_pairs={{3,6},{4,1},{7,10},{8,5},{11,14},{12,9},{19,22},{20,17},{23,26},{2... | collective-permute-start | bytes 442376 | tf_op jit(solution)/shard_map/ppermute | solution.py:536
  18.7 6.5 %collective-permute-start.9 = (bf16[144,512]{1,0:T(8,128)(2,1)S(1)}, bf16[144,512]{1,0:T(8,128)(2,1)S(1)}, u32[]{:S(2)}, u32[]{:S(2)}) collective-permute-start(bf16[144,512]{1,0:T(8,128)(2,1)S(1)} %place.1.refs_0_), channel_id=1, source_target_pairs={{3,4},{4,3},{7,8},{8,7},{11,12},{12,11},{19,20},{20,19},{23,24},{2... | collective-permute-start | bytes 442376 | tf_op jit(solution)/shard_map/ppermute | solution.py:536
  25.2 3.1 %collective-permute-start.7 = (bf16[2,144,768]{2,1,0:T(8,128)(2,1)S(1)}, bf16[2,144,768]{2,1,0:T(8,128)(2,1)S(1)}, u32[]{:S(2)}, u32[]{:S(2)}) collective-permute-start(bf16[2,144,768]{2,1,0:T(8,128)(2,1)S(1)} %get-tuple-element.59), channel_id=1, source_target_pairs={{0,1},{1,0},{2,3},{3,2},{4,5},{5,4},{6,7},{7,6},{8,9},{9,8},{10,11... | collective-permute-start | bytes 1327112 | tf_op jit(solution)/shard_map/ppermute | solution.py:565

commit v4 on v3

--- a/solution.py
+++ b/solution.py
@@ -511,29 +511,6 @@
     width = qkv_weight.shape[0]
     qkv = in_vmem(qkv)
     limit = pltpu.CompilerParams(vmem_limit_bytes=16 << 20)
-    rounds = [None] * n
-    for r in reversed(range(n)):
-        links = {}
-        for g in range(groups):
-            for k in range(shards - 1):
-                for source, target in (
-                    ((g, k, n - 1, 1), (g, k + 1, r, 0)),
-                    ((g, k + 1, 0, 0), (g, k, n - 1 - r, 1)),
-                ):
-                    links[source] = target
-        for source, target in list(links.items()):
-            links.setdefault(target, source)
-        for g in range(groups):
-            for end in ((g, 0, 0, 0), (g, shards - 1, n - 1, 1)):
-                beside = (*end[:2], n - 1 - end[2], end[3])
-                if end not in links and beside not in links:
-                    links.update({end: beside, beside: end} if r == 0 else {})
-        for place in itertools.product(range(groups), range(shards), range(n), range(cores)):
-            links.setdefault(place, ((place[0] + 1) % groups, *place[1:]))
-        assert len(set(links.values())) == len(links)
-        sizes = (groups, shards, n, cores)
-        flat = [tuple(int(np.ravel_multi_index(p, sizes)) for p in link) for link in links.items()]
-        rounds[r] = lax.ppermute(own, ("groups", "seq", "head", "sub"), flat)
     limit = pltpu.CompilerParams(vmem_limit_bytes=16 << 20)
     *own_qkv, whole, whole_bias, whole_gain = pl.pallas_call(
         functools.partial(own_kernel, n),
@@ -551,6 +528,30 @@
         name="own",
     )(own, *conv, *conv_bias, gain, qkv)
     weights = (whole, whole_bias, whole_gain, qkv)
+    late, _ = lax.optimization_barrier((own, own_qkv[0]))
+    rounds = [None] * n
+    for r in reversed(range(n)):
+        links = {}
+        for g in range(groups):
+            for k in range(shards - 1):
+                for source, target in (
+                    ((g, k, n - 1, 1), (g, k + 1, r, 0)),
+                    ((g, k + 1, 0, 0), (g, k, n - 1 - r, 1)),
+                ):
+                    links[source] = target
+        for source, target in list(links.items()):
+            links.setdefault(target, source)
+        for g in range(groups):
+            for end in ((g, 0, 0, 0), (g, shards - 1, n - 1, 1)):
+                beside = (*end[:3], 1 - end[3])
+                if end not in links and beside not in links:
+                    links.update({end: beside, beside: end})
+        for place in itertools.product(range(groups), range(shards), range(n), range(cores)):
+            links.setdefault(place, ((place[0] + 1) % groups, *place[1:]))
+        assert len(set(links.values())) == len(links)
+        sizes = (groups, shards, n, cores)
+        flat = [tuple(int(np.ravel_multi_index(p, sizes)) for p in link) for link in links.items()]
+        rounds[r] = lax.ppermute(late if r == 0 else own, ("groups", "seq", "head", "sub"), flat)
     *half_qkv, near_sent = pl.pallas_call(
         functools.partial(others_kernel, n),
         out_shape=[jax.ShapeDtypeStruct((n, ROWS, local_width), BF16)] * 3

time: 31 us -> 30.9 us (level)
  waiting for transfers between devices: 2.58 us -> 3.17 us
  starting transfers between devices: 11.1 us -> 10.6 us
    ppermute x2, starting transfers between devices: 1.65 us -> 1.08 us  [local(): lax.ppermute(late if r == 0 else own, ('groups', 'seq', 'head', 'sub'), f...]
    ppermute x2, waiting for transfers between devices: 1.19 us -> 1.6 us  [from_heads(): lax.ppermute(block, 'head', [((i + d) % n, i) for i in range(n)])]
  transfers between devices with their start and end apart: 10 -> 10, of which waited for: 3 -> 4; matrix products, arithmetic and copies ran while one was open for 0% -> 0% of each run, Pallas kernels for 46% -> 46%
where the time goes in v4:
time: 30.9 us; the launch traced here: 30.5 us
  Pallas kernels  16.7 us (54%)
  starting transfers between devices  10.6 us (34%)
  waiting for transfers between devices  3.17 us (10%)
    ppermute x3, starting transfers between devices, local(): lax.ppermute(packed[d], 'seq', [(i, i ^ d) for i in range(shards)])  4.45 us
    pallas_call x1, Pallas kernels, local(): pl.pallas_call(functools.partial(mel_kernel, shards, capacity, relative),...  3.46 us
    pallas_call x1, Pallas kernels, local(): pl.pallas_call(prepare_kernel, out_shape=[pltpu.VMEM((pairs, n, 2 * ROWS,...  3.1 us
    ppermute x1, starting transfers between devices, local(): lax.ppermute(sub_weight, ('groups', 'head', 'sub'), links)  3.01 us
    pallas_call x1, Pallas kernels, local(): pl.pallas_call(functools.partial(far_kernel, n), out_shape=jax.ShapeDtype...  2.99 us
    pallas_call x1, Pallas kernels, local(): pl.pallas_call(functools.partial(near_kernel, n), out_shape=jax.ShapeDtyp...  2.27 us
    pallas_call x1, Pallas kernels, local(): pl.pallas_call(functools.partial(others_kernel, n), out_shape=[jax.ShapeD...  2.24 us
    pallas_call x1, Pallas kernels, local(): pl.pallas_call(functools.partial(own_kernel, n), out_shape=[jax.ShapeDtyp...  2.18 us
  transfers between devices with their start and end apart: 10, of which 4 were waited for; matrix products, arithmetic and copies ran while one was open for 0% of the time, Pallas kernels for 46%

profile of v4, /device:TPU:0, one launch (start us, length us, event | category | flops | bytes accessed | tf_op | source)
XLA Modules:
  0.0 30.5 jit_solution(15358423249602429894)
XLA Ops:
  0.0 0.0 copy-start
  0.0 0.0 copy-start.2
  0.0 3.0 %collective-permute-start.3 = (bf16[512,768]{1,0:T(8,128)(2,1)}, bf16[512,768]{1,0:T(8,128)(2,1)S(1)}, u32[]{:S(2)}, u32[]{:S(2)}) collective-permute-start(bf16[512,768]{1,0:T(8,128)(2,1)} %refs_1_.1), channel_id=1, source_target_pairs={{2,0},{17,1},{0,2},{19,3},{18,16},{1,17},{16,18},{3,19},{6,4},{21,... | collective-permute-start | bytes 2359304 | tf_op jit(solution)/shard_map/ppermute | solution.py:436
  3.0 3.5 %log_mel.1 = (bf16[16,2304]{1,0:T(8,128)(2,1)S(1)}, bf16[16,2304]{1,0:T(8,128)(2,1)S(1)}, bf16[16,2304]{1,0:T(8,128)(2,1)S(1)}, bf16[16,2304]{1,0:T(8,128)(2,1)S(1)}) custom-call(f32[64,3072]{1,0:T(8,128)} %bitcast.9, s32[1,64]{1,0:T(1,128)} %bitcast.10, f32[2,256]{1,0:T(2,128)} %constant.6.clone.refs_2_, bf16[2,2,256,256]{3,2,1,0:T(8,128)(2,1)} %constant.7.clone.refs_3_, ...), custom_call_target="tpu_custom_call" | custom-call | tf_op jit(solution)/shard_map/log_mel/pallas_call | solution.py:437
  6.5 3.7 %collective-permute-start = (bf16[16,2304]{1,0:T(8,128)(2,1)S(1)}, bf16[16,2304]{1,0:T(8,128)(2,1)S(1)}, u32[]{:S(2)}, u32[]{:S(2)}) collective-permute-start(bf16[16,2304]{1,0:T(8,128)(2,1)S(1)} %get-tuple-element.34), channel_id=1, source_target_pairs={{0,12},{4,8},{8,4},{12,0},{1,13},{5,9},{9,5},{13,1},{2,14},{6,10},... | collective-permute-start | bytes 221192 | tf_op jit(solution)/shard_map/ppermute | solution.py:461
  10.2 0.0 collective-permute-start.1
  10.2 0.8 %collective-permute-start.2 = (bf16[16,2304]{1,0:T(8,128)(2,1)S(1)}, bf16[16,2304]{1,0:T(8,128)(2,1)S(1)}, u32[]{:S(2)}, u32[]{:S(2)}) collective-permute-start(bf16[16,2304]{1,0:T(8,128)(2,1)S(1)} %get-tuple-element.36), channel_id=1, source_target_pairs={{0,4},{4,0},{8,12},{12,8},{1,5},{5,1},{9,13},{13,9},{2,6},{6,2},{1... | collective-permute-start | bytes 221192 | tf_op jit(solution)/shard_map/ppermute | solution.py:461
  10.9 0.4 %collective-permute-start.4 = (bf16[768]{0:T(1024)(128)(2,1)}, bf16[768]{0:T(1024)(128)(2,1)S(1)}, u32[]{:S(2)}, u32[]{:S(2)}) collective-permute-start(bf16[768]{0:T(1024)(128)(2,1)} %param.15), channel_id=1, source_target_pairs={{2,0},{0,2},{3,1},{1,3},{6,4},{4,6},{7,5},{5,7},{10,8},{8,10},{11,... | collective-permute-start | bytes 4616 | tf_op jit(solution)/shard_map/ppermute | solution.py:412
  11.3 3.1 %prepare.1 = (f32[6,2,288,432]{3,2,1,0:T(8,128)S(1)}, bf16[3,1536,768]{2,1,0:T(8,128)(2,1)S(1)}) custom-call(s32[4]{0:T(128)} %lengths_hbm.1, f32[12,543]{1,0:T(8,128)} %table_hbm, bf16[3,1536,768]{2,1,0:T(8,128)(2,1)} %bitcast.11), custom_call_target="tpu_custom_call" | custom-call | flops 2147483648 | bytes 8388608 | tf_op jit(solution)/shard_map/prepare/pallas_call | solution.py:475
  14.4 0.3 collective-permute-done.4
  14.7 0.0 collective-permute-done.refs_0_
  14.7 1.4 %collective-permute-done.1.refs_1_ = bf16[16,2304]{1,0:T(8,128)(2,1)S(1)} collective-permute-done((bf16[16,2304]{1,0:T(8,128)(2,1)S(1)}, bf16[16,2304]{1,0:T(8,128)(2,1)S(1)}, u32[]{:S(2)}, u32[]{:S(2)}) %collective-permute-start.1) | collective-permute-done | bytes 73760 | tf_op jit(solution)/shard_map/ppermute | solution.py:461
  16.1 0.0 collective-permute-done.2.refs_2_
  16.1 0.0 collective-permute-done.3.refs_2_
  16.1 0.4 %place.1.refs_0_ = bf16[144,512]{1,0:T(8,128)(2,1)S(1)} custom-call(bf16[16,2304]{1,0:T(8,128)(2,1)S(1)} %collective-permute-done.refs_0_, bf16[16,2304]{1,0:T(8,128)(2,1)S(1)} %collective-permute-done.1.refs_1_, bf16[16,2304]{1,0:T(8,128)(2,1)S(1)} %collective-permute-done.2.refs_2_, bf16[16,2304]{1,0:T(8,128)(2,1)S(1)} %get-tuple-element.45.refs_3_), custom_call_target="tpu_custom_call" | custom-call | tf_op jit(solution)/shard_map/place/pallas_call | solution.py:496
  16.6 0.1 collective-permute-start.5
  16.6 1.5 %collective-permute-start.6 = (bf16[144,512]{1,0:T(8,128)(2,1)S(1)}, bf16[144,512]{1,0:T(8,128)(2,1)S(1)}, u32[]{:S(2)}, u32[]{:S(2)}) collective-permute-start(bf16[144,512]{1,0:T(8,128)(2,1)S(1)} %place.1.refs_0_), channel_id=1, source_target_pairs={{2,0},{0,2},{3,1},{1,3},{6,4},{4,6},{7,5},{5,7},{10,8},{8,10},{11,... | collective-permute-start | bytes 442376 | tf_op jit(solution)/shard_map/ppermute | solution.py:412
  18.1 0.6 %collective-permute-start.8 = (bf16[144,512]{1,0:T(8,128)(2,1)S(1)}, bf16[144,512]{1,0:T(8,128)(2,1)S(1)}, u32[]{:S(2)}, u32[]{:S(2)}) collective-permute-start(bf16[144,512]{1,0:T(8,128)(2,1)S(1)} %place.1.refs_0_), channel_id=1, source_target_pairs={{3,6},{4,1},{7,10},{8,5},{11,14},{12,9},{19,22},{20,17},{23,26},{2... | collective-permute-start | bytes 442376 | tf_op jit(solution)/shard_map/ppermute | solution.py:554
  18.7 0.2 collective-permute-done.5.refs_3_
  18.9 0.0 copy-done
  18.9 0.0 copy-done.2
  18.9 0.0 copy-done.1
  18.9 2.2 %own.1 = (bf16[1,144,768]{2,1,0:T(8,128)(2,1)S(1)}, bf16[1,144,768]{2,1,0:T(8,128)(2,1)S(1)}, bf16[1,144,768]{2,1,0:T(8,128)(2,1)S(1)}, bf16[512,1536]{1,0:T(8,1...) custom-call(bf16[144,512]{1,0:T(8,128)(2,1)S(1)} %place.1.refs_0_, bf16[512,768]{1,0:T(8,128)(2,1)S(1)} %copy-done, ...), custom_call_target="tpu_custom_call" | custom-call | flops 1048576 | bytes 1048576 | tf_op jit(solution)/shard_map/own/pallas_call | solution.py:515
  21.1 0.5 %collective-permute-start.9 = (bf16[144,512]{1,0:T(8,128)(2,1)S(1)}, bf16[144,512]{1,0:T(8,128)(2,1)S(1)}, u32[]{:S(2)}, u32[]{:S(2)}) collective-permute-start(bf16[144,512]{1,0:T(8,128)(2,1)S(1)} %place.1.refs_0_), channel_id=1, source_target_pairs={{3,4},{4,3},{7,8},{8,7},{11,12},{12,11},{19,20},{20,19},{23,24},{2... | collective-permute-start | bytes 442376 | tf_op jit(solution)/shard_map/ppermute | solution.py:554
  21.6 1.3 %collective-permute-done.6.refs_3_ = bf16[144,512]{1,0:T(8,128)(2,1)S(1)} collective-permute-done((bf16[144,512]{1,0:T(8,128)(2,1)S(1)}, bf16[144,512]{1,0:T(8,128)(2,1)S(1)}, u32[]{:S(2)}, u32[]{:S(2)}) %collective-permute-start.6) | collective-permute-done | bytes 147488 | tf_op jit(solution)/shard_map/ppermute | solution.py:412
  22.9 2.2 %others.1 = (bf16[2,144,768]{2,1,0:T(8,128)(2,1)S(1)}, bf16[2,144,768]{2,1,0:T(8,128)(2,1)S(1)}, bf16[2,144,768]{2,1,0:T(8,128)(2,1)S(1)}, bf16[2,144,768]{2,1,0:T(8,128)(2,1)S(1)}) custom-call(bf16[1,144,768]{2,1,0:T(8,128)(2,1)S(1)} %get-tuple-element.51.refs_0_, bf16[1,144,768]{2,1,0:T(8,128)(2,1)S(1)} %get-tuple-element.52.refs_1_, ...), custom_call_target="tpu_custom_call" | custom-call | flops 4294967296 | bytes 9437184 | tf_op jit(solution)/shard_map/others/pallas_call | solution.py:555
  25.1 0.1 collective-permute-start.7
  25.2 0.0 collective-permute-done.8.refs_3_
  25.2 0.0 collective-permute-done.9.refs_4_
  25.2 3.0 %far.1.refs_4_ = bf16[144,768]{1,0:T(8,128)(2,1)S(1)} custom-call(bf16[2,144,768]{2,1,0:T(8,128)(2,1)S(1)} %get-tuple-element.57.refs_0_, bf16[2,144,768]{2,1,0:T(8,128)(2,1)S(1)} %get-tuple-element.58.refs_1_, bf16[2,144,768]{2,1,0:T(8,128)(2,1)S(1)} %get-tuple-element.59.refs_2_, bf16[144,512]{1,0:T(8,128)(2,1)S(1)} %collective-permute-done.8.refs_3_, ...), custom_call_target="tpu_custom_call" | custom-call | flops 17179869184 | bytes 9437184 | tf_op jit(solution)/shard_map/far/pallas_call | solution.py:567
  28.2 0.0 collective-permute-done.7.refs_3_
  28.2 2.3 %near.1 = bf16[272,768]{1,0:T(8,128)(2,1)} custom-call(bf16[2,144,768]{2,1,0:T(8,128)(2,1)S(1)} %get-tuple-element.57.refs_0_, bf16[2,144,768]{2,1,0:T(8,128)(2,1)S(1)} %get-tuple-element.58.refs_1_, bf16[2,144,768]{2,1,0:T(8,128)(2,1)S(1)} %get-tuple-element.59.refs_2_, bf16[2,144,768]{2,1,0:T(8,128)(2,1)S(1)} %collective-permute-done.7.refs_3_, ...), custom_call_target="tpu_custom_call" | custom-call | tf_op jit(solution)/shard_map/near/pallas_call | solution.py:581
  (1 shorter events, 0.0 us)
Async XLA Ops:
  0.0 18.9 %copy-start = (bf16[512,768]{1,0:T(8,128)(2,1)S(1)}, bf16[512,768]{1,0:T(8,128)(2,1)}, u32[]{:S(2)}) copy-start(bf16[512,768]{1,0:T(8,128)(2,1)} %refs_1_.1) | copy-start | bytes 2359300
  0.0 18.9 %copy-start.2 = (bf16[768]{0:T(1024)(128)(2,1)S(1)}, bf16[768]{0:T(1024)(128)(2,1)}, u32[]{:S(2)}) copy-start(bf16[768]{0:T(1024)(128)(2,1)} %param.15) | copy-start | bytes 4612
  0.0 18.9 %copy-start.1 = (f32[1536]{0:T(1024)S(1)}, f32[1536]{0:T(1024)}, u32[]{:S(2)}) copy-start(f32[1536]{0:T(1024)} %param.16) | copy-start | bytes 18436
  0.0 16.1 %collective-permute-start.3 = (bf16[512,768]{1,0:T(8,128)(2,1)}, bf16[512,768]{1,0:T(8,128)(2,1)S(1)}, u32[]{:S(2)}, u32[]{:S(2)}) collective-permute-start(bf16[512,768]{1,0:T(8,128)(2,1)} %refs_1_.1), channel_id=1, source_target_pairs={{2,0},{17,1},{0,2},{19,3},{18,16},{1,17},{16,18},{3,19},{6,4},{21,... | collective-permute-start | bytes 2359304 | tf_op jit(solution)/shard_map/ppermute | solution.py:436
  6.5 8.3 %collective-permute-start = (bf16[16,2304]{1,0:T(8,128)(2,1)S(1)}, bf16[16,2304]{1,0:T(8,128)(2,1)S(1)}, u32[]{:S(2)}, u32[]{:S(2)}) collective-permute-start(bf16[16,2304]{1,0:T(8,128)(2,1)S(1)} %get-tuple-element.34), channel_id=1, source_target_pairs={{0,12},{4,8},{8,4},{12,0},{1,13},{5,9},{9,5},{13,1},{2,14},{6,10},... | collective-permute-start | bytes 221192 | tf_op jit(solution)/shard_map/ppermute | solution.py:461
  10.2 6.0 %collective-permute-start.1 = (bf16[16,2304]{1,0:T(8,128)(2,1)S(1)}, bf16[16,2304]{1,0:T(8,128)(2,1)S(1)}, u32[]{:S(2)}, u32[]{:S(2)}) collective-permute-start(bf16[16,2304]{1,0:T(8,128)(2,1)S(1)} %get-tuple-element.35), channel_id=1, source_target_pairs={{0,8},{4,12},{8,0},{12,4},{1,9},{5,13},{9,1},{13,5},{2,10},{6,14},... | collective-permute-start | bytes 221192 | tf_op jit(solution)/shard_map/ppermute | solution.py:461
  10.2 6.0 %collective-permute-start.2 = (bf16[16,2304]{1,0:T(8,128)(2,1)S(1)}, bf16[16,2304]{1,0:T(8,128)(2,1)S(1)}, u32[]{:S(2)}, u32[]{:S(2)}) collective-permute-start(bf16[16,2304]{1,0:T(8,128)(2,1)S(1)} %get-tuple-element.36), channel_id=1, source_target_pairs={{0,4},{4,0},{8,12},{12,8},{1,5},{5,1},{9,13},{13,9},{2,6},{6,2},{1... | collective-permute-start | bytes 221192 | tf_op jit(solution)/shard_map/ppermute | solution.py:461
  10.9 3.8 %collective-permute-start.4 = (bf16[768]{0:T(1024)(128)(2,1)}, bf16[768]{0:T(1024)(128)(2,1)S(1)}, u32[]{:S(2)}, u32[]{:S(2)}) collective-permute-start(bf16[768]{0:T(1024)(128)(2,1)} %param.15), channel_id=1, source_target_pairs={{2,0},{0,2},{3,1},{1,3},{6,4},{4,6},{7,5},{5,7},{10,8},{8,10},{11,... | collective-permute-start | bytes 4616 | tf_op jit(solution)/shard_map/ppermute | solution.py:412
  16.6 2.4 %collective-permute-start.5 = (bf16[512,768]{1,0:T(8,128)(2,1)S(1)}, bf16[512,768]{1,0:T(8,128)(2,1)S(1)}, u32[]{:S(2)}, u32[]{:S(2)}) collective-permute-start(bf16[512,768]{1,0:T(8,128)(2,1)S(1)} %collective-permute-done.3.refs_2_), channel_id=1, source_target_pairs={{0,1},{1,0},{2,3},{3,2},{4,5},{5,4},{6,7},{7,6},{8,9},{9,8},{10,11... | collective-permute-start | bytes 2359304 | tf_op jit(solution)/shard_map/ppermute | solution.py:507
  16.6 6.3 %collective-permute-start.6 = (bf16[144,512]{1,0:T(8,128)(2,1)S(1)}, bf16[144,512]{1,0:T(8,128)(2,1)S(1)}, u32[]{:S(2)}, u32[]{:S(2)}) collective-permute-start(bf16[144,512]{1,0:T(8,128)(2,1)S(1)} %place.1.refs_0_), channel_id=1, source_target_pairs={{2,0},{0,2},{3,1},{1,3},{6,4},{4,6},{7,5},{5,7},{10,8},{8,10},{11,... | collective-permute-start | bytes 442376 | tf_op jit(solution)/shard_map/ppermute | solution.py:412
  18.1 7.1 %collective-permute-start.8 = (bf16[144,512]{1,0:T(8,128)(2,1)S(1)}, bf16[144,512]{1,0:T(8,128)(2,1)S(1)}, u32[]{:S(2)}, u32[]{:S(2)}) collective-permute-start(bf16[144,512]{1,0:T(8,128)(2,1)S(1)} %place.1.refs_0_), channel_id=1, source_target_pairs={{3,6},{4,1},{7,10},{8,5},{11,14},{12,9},{19,22},{20,17},{23,26},{2... | collective-permute-start | bytes 442376 | tf_op jit(solution)/shard_map/ppermute | solution.py:554
  21.1 4.1 %collective-permute-start.9 = (bf16[144,512]{1,0:T(8,128)(2,1)S(1)}, bf16[144,512]{1,0:T(8,128)(2,1)S(1)}, u32[]{:S(2)}, u32[]{:S(2)}) collective-permute-start(bf16[144,512]{1,0:T(8,128)(2,1)S(1)} %place.1.refs_0_), channel_id=1, source_target_pairs={{3,4},{4,3},{7,8},{8,7},{11,12},{12,11},{19,20},{20,19},{23,24},{2... | collective-permute-start | bytes 442376 | tf_op jit(solution)/shard_map/ppermute | solution.py:554
  25.1 3.1 %collective-permute-start.7 = (bf16[2,144,768]{2,1,0:T(8,128)(2,1)S(1)}, bf16[2,144,768]{2,1,0:T(8,128)(2,1)S(1)}, u32[]{:S(2)}, u32[]{:S(2)}) collective-permute-start(bf16[2,144,768]{2,1,0:T(8,128)(2,1)S(1)} %get-tuple-element.60), channel_id=1, source_target_pairs={{0,1},{1,0},{2,3},{3,2},{4,5},{5,4},{6,7},{7,6},{8,9},{9,8},{10,11... | collective-permute-start | bytes 1327112 | tf_op jit(solution)/shard_map/ppermute | solution.py:566

commit v5 on v4

--- a/solution.py
+++ b/solution.py
@@ -503,7 +503,6 @@
     )(*received)
     conv = [sub_weight]
     for got in weight_got:
-        got, _ = lax.optimization_barrier((got, own))
         conv += [got, lax.ppermute(got, "sub", [(0, 1), (1, 0)])]
     conv_bias = [line.reshape(-1, LANES) for line in [sub_bias] + bias_got]
 

time: 30.9 us -> 30.7 us (level)
  transfers between devices with their start and end apart: 10 -> 10, of which waited for: 4 -> 3; matrix products, arithmetic and copies ran while one was open for 0% -> 0% of each run, Pallas kernels for 46% -> 47%
where the time goes in v5:
time: 30.7 us; the launch traced here: 30.5 us
  Pallas kernels  16.7 us (54%)
  starting transfers between devices  10.6 us (35%)
  waiting for transfers between devices  3.07 us (10%)
    ppermute x3, starting transfers between devices, local(): lax.ppermute(packed[d], 'seq', [(i, i ^ d) for i in range(shards)])  4.45 us
    pallas_call x1, Pallas kernels, local(): pl.pallas_call(functools.partial(mel_kernel, shards, capacity, relative),...  3.46 us
    pallas_call x1, Pallas kernels, local(): pl.pallas_call(prepare_kernel, out_shape=[pltpu.VMEM((pairs, n, 2 * ROWS,...  3.1 us
    ppermute x1, starting transfers between devices, local(): lax.ppermute(sub_weight, ('groups', 'head', 'sub'), links)  3.01 us
    pallas_call x1, Pallas kernels, local(): pl.pallas_call(functools.partial(far_kernel, n), out_shape=jax.ShapeDtype...  2.99 us
    pallas_call x1, Pallas kernels, local(): pl.pallas_call(functools.partial(near_kernel, n), out_shape=jax.ShapeDtyp...  2.27 us
    pallas_call x1, Pallas kernels, local(): pl.pallas_call(functools.partial(others_kernel, n), out_shape=[jax.ShapeD...  2.25 us
    pallas_call x1, Pallas kernels, local(): pl.pallas_call(functools.partial(own_kernel, n), out_shape=[jax.ShapeDtyp...  2.2 us
  transfers between devices with their start and end apart: 10, of which 3 were waited for; matrix products, arithmetic and copies ran while one was open for 0% of the time, Pallas kernels for 47%

profile of v5, /device:TPU:0, one launch (start us, length us, event | category | flops | bytes accessed | tf_op | source)
XLA Modules:
  0.0 30.5 jit_solution(11286682293134001868)
XLA Ops:
  0.0 0.0 copy-start
  0.0 0.0 copy-start.2
  0.0 3.0 %collective-permute-start.3 = (bf16[512,768]{1,0:T(8,128)(2,1)}, bf16[512,768]{1,0:T(8,128)(2,1)S(1)}, u32[]{:S(2)}, u32[]{:S(2)}) collective-permute-start(bf16[512,768]{1,0:T(8,128)(2,1)} %refs_1_.1), channel_id=1, source_target_pairs={{2,0},{17,1},{0,2},{19,3},{18,16},{1,17},{16,18},{3,19},{6,4},{21,... | collective-permute-start | bytes 2359304 | tf_op jit(solution)/shard_map/ppermute | solution.py:436
  3.0 3.5 %log_mel.1 = (bf16[16,2304]{1,0:T(8,128)(2,1)S(1)}, bf16[16,2304]{1,0:T(8,128)(2,1)S(1)}, bf16[16,2304]{1,0:T(8,128)(2,1)S(1)}, bf16[16,2304]{1,0:T(8,128)(2,1)S(1)}) custom-call(f32[64,3072]{1,0:T(8,128)} %bitcast.9, s32[1,64]{1,0:T(1,128)} %bitcast.10, f32[2,256]{1,0:T(2,128)} %constant.6.clone.refs_2_, bf16[2,2,256,256]{3,2,1,0:T(8,128)(2,1)} %constant.7.clone.refs_3_, ...), custom_call_target="tpu_custom_call" | custom-call | tf_op jit(solution)/shard_map/log_mel/pallas_call | solution.py:437
  6.5 3.7 %collective-permute-start = (bf16[16,2304]{1,0:T(8,128)(2,1)S(1)}, bf16[16,2304]{1,0:T(8,128)(2,1)S(1)}, u32[]{:S(2)}, u32[]{:S(2)}) collective-permute-start(bf16[16,2304]{1,0:T(8,128)(2,1)S(1)} %get-tuple-element.33), channel_id=1, source_target_pairs={{0,12},{4,8},{8,4},{12,0},{1,13},{5,9},{9,5},{13,1},{2,14},{6,10},... | collective-permute-start | bytes 221192 | tf_op jit(solution)/shard_map/ppermute | solution.py:461
  10.2 0.0 collective-permute-start.1
  10.2 0.8 %collective-permute-start.2 = (bf16[16,2304]{1,0:T(8,128)(2,1)S(1)}, bf16[16,2304]{1,0:T(8,128)(2,1)S(1)}, u32[]{:S(2)}, u32[]{:S(2)}) collective-permute-start(bf16[16,2304]{1,0:T(8,128)(2,1)S(1)} %get-tuple-element.35), channel_id=1, source_target_pairs={{0,4},{4,0},{8,12},{12,8},{1,5},{5,1},{9,13},{13,9},{2,6},{6,2},{1... | collective-permute-start | bytes 221192 | tf_op jit(solution)/shard_map/ppermute | solution.py:461
  10.9 0.4 %collective-permute-start.4 = (bf16[768]{0:T(1024)(128)(2,1)}, bf16[768]{0:T(1024)(128)(2,1)S(1)}, u32[]{:S(2)}, u32[]{:S(2)}) collective-permute-start(bf16[768]{0:T(1024)(128)(2,1)} %param.15), channel_id=1, source_target_pairs={{2,0},{0,2},{3,1},{1,3},{6,4},{4,6},{7,5},{5,7},{10,8},{8,10},{11,... | collective-permute-start | bytes 4616 | tf_op jit(solution)/shard_map/ppermute | solution.py:412
  11.3 3.1 %prepare.1 = (f32[6,2,288,432]{3,2,1,0:T(8,128)S(1)}, bf16[3,1536,768]{2,1,0:T(8,128)(2,1)S(1)}) custom-call(s32[4]{0:T(128)} %lengths_hbm.1, f32[12,543]{1,0:T(8,128)} %table_hbm, bf16[3,1536,768]{2,1,0:T(8,128)(2,1)} %bitcast.11), custom_call_target="tpu_custom_call" | custom-call | flops 2147483648 | bytes 8388608 | tf_op jit(solution)/shard_map/prepare/pallas_call | solution.py:475
  14.4 0.3 collective-permute-done.4
  14.7 0.0 collective-permute-done.refs_0_
  14.7 1.4 %collective-permute-done.1.refs_1_ = bf16[16,2304]{1,0:T(8,128)(2,1)S(1)} collective-permute-done((bf16[16,2304]{1,0:T(8,128)(2,1)S(1)}, bf16[16,2304]{1,0:T(8,128)(2,1)S(1)}, u32[]{:S(2)}, u32[]{:S(2)}) %collective-permute-start.1) | collective-permute-done | bytes 73760 | tf_op jit(solution)/shard_map/ppermute | solution.py:461
  16.1 0.0 collective-permute-done.2.refs_2_
  16.1 0.0 collective-permute-done.3.refs_2_
  16.1 0.0 collective-permute-start.5
  16.1 0.4 %place.1.refs_0_ = bf16[144,512]{1,0:T(8,128)(2,1)S(1)} custom-call(bf16[16,2304]{1,0:T(8,128)(2,1)S(1)} %collective-permute-done.refs_0_, bf16[16,2304]{1,0:T(8,128)(2,1)S(1)} %collective-permute-done.1.refs_1_, bf16[16,2304]{1,0:T(8,128)(2,1)S(1)} %collective-permute-done.2.refs_2_, bf16[16,2304]{1,0:T(8,128)(2,1)S(1)} %get-tuple-element.44.refs_3_), custom_call_target="tpu_custom_call" | custom-call | tf_op jit(solution)/shard_map/place/pallas_call | solution.py:496
  16.6 1.5 %collective-permute-start.6 = (bf16[144,512]{1,0:T(8,128)(2,1)S(1)}, bf16[144,512]{1,0:T(8,128)(2,1)S(1)}, u32[]{:S(2)}, u32[]{:S(2)}) collective-permute-start(bf16[144,512]{1,0:T(8,128)(2,1)S(1)} %place.1.refs_0_), channel_id=1, source_target_pairs={{2,0},{0,2},{3,1},{1,3},{6,4},{4,6},{7,5},{5,7},{10,8},{8,10},{11,... | collective-permute-start | bytes 442376 | tf_op jit(solution)/shard_map/ppermute | solution.py:412
  18.1 0.6 %collective-permute-start.8 = (bf16[144,512]{1,0:T(8,128)(2,1)S(1)}, bf16[144,512]{1,0:T(8,128)(2,1)S(1)}, u32[]{:S(2)}, u32[]{:S(2)}) collective-permute-start(bf16[144,512]{1,0:T(8,128)(2,1)S(1)} %place.1.refs_0_), channel_id=1, source_target_pairs={{3,6},{4,1},{7,10},{8,5},{11,14},{12,9},{19,22},{20,17},{23,26},{2... | collective-permute-start | bytes 442376 | tf_op jit(solution)/shard_map/ppermute | solution.py:553
  18.7 0.0 collective-permute-done.5.refs_3_
  18.7 0.0 copy-done
  18.7 0.0 copy-done.2
  18.7 0.0 copy-done.1
  18.7 2.2 %own.1 = (bf16[1,144,768]{2,1,0:T(8,128)(2,1)S(1)}, bf16[1,144,768]{2,1,0:T(8,128)(2,1)S(1)}, bf16[1,144,768]{2,1,0:T(8,128)(2,1)S(1)}, bf16[512,1536]{1,0:T(8,1...) custom-call(bf16[144,512]{1,0:T(8,128)(2,1)S(1)} %place.1.refs_0_, bf16[512,768]{1,0:T(8,128)(2,1)S(1)} %copy-done, ...), custom_call_target="tpu_custom_call" | custom-call | flops 1048576 | bytes 1048576 | tf_op jit(solution)/shard_map/own/pallas_call | solution.py:514
  20.9 0.6 %collective-permute-start.9 = (bf16[144,512]{1,0:T(8,128)(2,1)S(1)}, bf16[144,512]{1,0:T(8,128)(2,1)S(1)}, u32[]{:S(2)}, u32[]{:S(2)}) collective-permute-start(bf16[144,512]{1,0:T(8,128)(2,1)S(1)} %place.1.refs_0_), channel_id=1, source_target_pairs={{3,4},{4,3},{7,8},{8,7},{11,12},{12,11},{19,20},{20,19},{23,24},{2... | collective-permute-start | bytes 442376 | tf_op jit(solution)/shard_map/ppermute | solution.py:553
  21.5 1.4 %collective-permute-done.6.refs_3_ = bf16[144,512]{1,0:T(8,128)(2,1)S(1)} collective-permute-done((bf16[144,512]{1,0:T(8,128)(2,1)S(1)}, bf16[144,512]{1,0:T(8,128)(2,1)S(1)}, u32[]{:S(2)}, u32[]{:S(2)}) %collective-permute-start.6) | collective-permute-done | bytes 147488 | tf_op jit(solution)/shard_map/ppermute | solution.py:412
  22.9 2.2 %others.1 = (bf16[2,144,768]{2,1,0:T(8,128)(2,1)S(1)}, bf16[2,144,768]{2,1,0:T(8,128)(2,1)S(1)}, bf16[2,144,768]{2,1,0:T(8,128)(2,1)S(1)}, bf16[2,144,768]{2,1,0:T(8,128)(2,1)S(1)}) custom-call(bf16[1,144,768]{2,1,0:T(8,128)(2,1)S(1)} %get-tuple-element.49.refs_0_, bf16[1,144,768]{2,1,0:T(8,128)(2,1)S(1)} %get-tuple-element.50.refs_1_, ...), custom_call_target="tpu_custom_call" | custom-call | flops 4294967296 | bytes 9437184 | tf_op jit(solution)/shard_map/others/pallas_call | solution.py:554
  25.1 0.1 collective-permute-start.7
  25.2 0.0 collective-permute-done.8.refs_3_
  25.2 0.0 collective-permute-done.9.refs_4_
  25.2 3.0 %far.1.refs_4_ = bf16[144,768]{1,0:T(8,128)(2,1)S(1)} custom-call(bf16[2,144,768]{2,1,0:T(8,128)(2,1)S(1)} %get-tuple-element.55.refs_0_, bf16[2,144,768]{2,1,0:T(8,128)(2,1)S(1)} %get-tuple-element.56.refs_1_, bf16[2,144,768]{2,1,0:T(8,128)(2,1)S(1)} %get-tuple-element.57.refs_2_, bf16[144,512]{1,0:T(8,128)(2,1)S(1)} %collective-permute-done.8.refs_3_, ...), custom_call_target="tpu_custom_call" | custom-call | flops 17179869184 | bytes 9437184 | tf_op jit(solution)/shard_map/far/pallas_call | solution.py:566
  28.2 0.0 collective-permute-done.7.refs_3_
  28.2 2.3 %near.1 = bf16[272,768]{1,0:T(8,128)(2,1)} custom-call(bf16[2,144,768]{2,1,0:T(8,128)(2,1)S(1)} %get-tuple-element.55.refs_0_, bf16[2,144,768]{2,1,0:T(8,128)(2,1)S(1)} %get-tuple-element.56.refs_1_, bf16[2,144,768]{2,1,0:T(8,128)(2,1)S(1)} %get-tuple-element.57.refs_2_, bf16[2,144,768]{2,1,0:T(8,128)(2,1)S(1)} %collective-permute-done.7.refs_3_, ...), custom_call_target="tpu_custom_call" | custom-call | tf_op jit(solution)/shard_map/near/pallas_call | solution.py:580
  (1 shorter events, 0.0 us)
Async XLA Ops:
  0.0 18.7 %copy-start = (bf16[512,768]{1,0:T(8,128)(2,1)S(1)}, bf16[512,768]{1,0:T(8,128)(2,1)}, u32[]{:S(2)}) copy-start(bf16[512,768]{1,0:T(8,128)(2,1)} %refs_1_.1) | copy-start | bytes 2359300
  0.0 18.7 %copy-start.2 = (bf16[768]{0:T(1024)(128)(2,1)S(1)}, bf16[768]{0:T(1024)(128)(2,1)}, u32[]{:S(2)}) copy-start(bf16[768]{0:T(1024)(128)(2,1)} %param.15) | copy-start | bytes 4612
  0.0 18.7 %copy-start.1 = (f32[1536]{0:T(1024)S(1)}, f32[1536]{0:T(1024)}, u32[]{:S(2)}) copy-start(f32[1536]{0:T(1024)} %param.16) | copy-start | bytes 18436
  0.0 16.1 %collective-permute-start.3 = (bf16[512,768]{1,0:T(8,128)(2,1)}, bf16[512,768]{1,0:T(8,128)(2,1)S(1)}, u32[]{:S(2)}, u32[]{:S(2)}) collective-permute-start(bf16[512,768]{1,0:T(8,128)(2,1)} %refs_1_.1), channel_id=1, source_target_pairs={{2,0},{17,1},{0,2},{19,3},{18,16},{1,17},{16,18},{3,19},{6,4},{21,... | collective-permute-start | bytes 2359304 | tf_op jit(solution)/shard_map/ppermute | solution.py:436
  6.5 8.3 %collective-permute-start = (bf16[16,2304]{1,0:T(8,128)(2,1)S(1)}, bf16[16,2304]{1,0:T(8,128)(2,1)S(1)}, u32[]{:S(2)}, u32[]{:S(2)}) collective-permute-start(bf16[16,2304]{1,0:T(8,128)(2,1)S(1)} %get-tuple-element.33), channel_id=1, source_target_pairs={{0,12},{4,8},{8,4},{12,0},{1,13},{5,9},{9,5},{13,1},{2,14},{6,10},... | collective-permute-start | bytes 221192 | tf_op jit(solution)/shard_map/ppermute | solution.py:461
  10.2 6.0 %collective-permute-start.1 = (bf16[16,2304]{1,0:T(8,128)(2,1)S(1)}, bf16[16,2304]{1,0:T(8,128)(2,1)S(1)}, u32[]{:S(2)}, u32[]{:S(2)}) collective-permute-start(bf16[16,2304]{1,0:T(8,128)(2,1)S(1)} %get-tuple-element.34), channel_id=1, source_target_pairs={{0,8},{4,12},{8,0},{12,4},{1,9},{5,13},{9,1},{13,5},{2,10},{6,14},... | collective-permute-start | bytes 221192 | tf_op jit(solution)/shard_map/ppermute | solution.py:461
  10.2 6.0 %collective-permute-start.2 = (bf16[16,2304]{1,0:T(8,128)(2,1)S(1)}, bf16[16,2304]{1,0:T(8,128)(2,1)S(1)}, u32[]{:S(2)}, u32[]{:S(2)}) collective-permute-start(bf16[16,2304]{1,0:T(8,128)(2,1)S(1)} %get-tuple-element.35), channel_id=1, source_target_pairs={{0,4},{4,0},{8,12},{12,8},{1,5},{5,1},{9,13},{13,9},{2,6},{6,2},{1... | collective-permute-start | bytes 221192 | tf_op jit(solution)/shard_map/ppermute | solution.py:461
  10.9 3.8 %collective-permute-start.4 = (bf16[768]{0:T(1024)(128)(2,1)}, bf16[768]{0:T(1024)(128)(2,1)S(1)}, u32[]{:S(2)}, u32[]{:S(2)}) collective-permute-start(bf16[768]{0:T(1024)(128)(2,1)} %param.15), channel_id=1, source_target_pairs={{2,0},{0,2},{3,1},{1,3},{6,4},{4,6},{7,5},{5,7},{10,8},{8,10},{11,... | collective-permute-start | bytes 4616 | tf_op jit(solution)/shard_map/ppermute | solution.py:412
  16.1 2.5 %collective-permute-start.5 = (bf16[512,768]{1,0:T(8,128)(2,1)S(1)}, bf16[512,768]{1,0:T(8,128)(2,1)S(1)}, u32[]{:S(2)}, u32[]{:S(2)}) collective-permute-start(bf16[512,768]{1,0:T(8,128)(2,1)S(1)} %collective-permute-done.3.refs_2_), channel_id=1, source_target_pairs={{0,1},{1,0},{2,3},{3,2},{4,5},{5,4},{6,7},{7,6},{8,9},{9,8},{10,11... | collective-permute-start | bytes 2359304 | tf_op jit(solution)/shard_map/ppermute | solution.py:506
  16.6 6.3 %collective-permute-start.6 = (bf16[144,512]{1,0:T(8,128)(2,1)S(1)}, bf16[144,512]{1,0:T(8,128)(2,1)S(1)}, u32[]{:S(2)}, u32[]{:S(2)}) collective-permute-start(bf16[144,512]{1,0:T(8,128)(2,1)S(1)} %place.1.refs_0_), channel_id=1, source_target_pairs={{2,0},{0,2},{3,1},{1,3},{6,4},{4,6},{7,5},{5,7},{10,8},{8,10},{11,... | collective-permute-start | bytes 442376 | tf_op jit(solution)/shard_map/ppermute | solution.py:412
  18.1 7.1 %collective-permute-start.8 = (bf16[144,512]{1,0:T(8,128)(2,1)S(1)}, bf16[144,512]{1,0:T(8,128)(2,1)S(1)}, u32[]{:S(2)}, u32[]{:S(2)}) collective-permute-start(bf16[144,512]{1,0:T(8,128)(2,1)S(1)} %place.1.refs_0_), channel_id=1, source_target_pairs={{3,6},{4,1},{7,10},{8,5},{11,14},{12,9},{19,22},{20,17},{23,26},{2... | collective-permute-start | bytes 442376 | tf_op jit(solution)/shard_map/ppermute | solution.py:553
  20.9 4.3 %collective-permute-start.9 = (bf16[144,512]{1,0:T(8,128)(2,1)S(1)}, bf16[144,512]{1,0:T(8,128)(2,1)S(1)}, u32[]{:S(2)}, u32[]{:S(2)}) collective-permute-start(bf16[144,512]{1,0:T(8,128)(2,1)S(1)} %place.1.refs_0_), channel_id=1, source_target_pairs={{3,4},{4,3},{7,8},{8,7},{11,12},{12,11},{19,20},{20,19},{23,24},{2... | collective-permute-start | bytes 442376 | tf_op jit(solution)/shard_map/ppermute | solution.py:553
  25.1 3.1 %collective-permute-start.7 = (bf16[2,144,768]{2,1,0:T(8,128)(2,1)S(1)}, bf16[2,144,768]{2,1,0:T(8,128)(2,1)S(1)}, u32[]{:S(2)}, u32[]{:S(2)}) collective-permute-start(bf16[2,144,768]{2,1,0:T(8,128)(2,1)S(1)} %get-tuple-element.58), channel_id=1, source_target_pairs={{0,1},{1,0},{2,3},{3,2},{4,5},{5,4},{6,7},{7,6},{8,9},{9,8},{10,11... | collective-permute-start | bytes 1327112 | tf_op jit(solution)/shard_map/ppermute | solution.py:565
